TPU v7x, 256 devices: a whole 4x4x8 slice. The times are simulated.
256 devices in a mesh: tm: 8 (over z), gx: 16 (over x, y_hi, core), gy: 2 (over y_lo).
Axes of the slice: x: 4, y: 4 (y_hi: 2, y_lo: 2; y = y_hi * 2 + y_lo), z: 8, core: 2. Of those that a mesh axis runs over, the one named last changes fastest.
Arguments:
- lagrange: float32 [16, 8, 1024, 256], P('tm', None, 'gx', 'gy'), may hold values from -6 to 6
- obs_lagrange: float32 [16, 16, 2, 1024], P('tm', 'gx', 'gy'), may hold values from -6 to 6
- increment: float32 [16, 8, 1024, 256], P('tm', None, 'gx', 'gy'), may hold values from -6 to 6
- forcing: float32 [16, 8, 1024, 256], P('tm', None, 'gx', 'gy'), may hold values from -6 to 6
- departures: float32 [16, 16, 2, 1024], P('tm', 'gx', 'gy'), may hold values from -6 to 6
- model_var: float32 [16, 8, 1024, 256], P('tm', None, 'gx', 'gy'), may hold values from 0.3 to 3
- obs_var: float32 [16, 16, 2, 1024], P('tm', 'gx', 'gy'), may hold values from 0.5 to 2
- wind_east: float32 [16, 8, 1024, 256], P('tm', None, 'gx', 'gy'), may hold values from -0.3 to 0.3
- wind_north: float32 [16, 8, 1024, 256], P('tm', None, 'gx', 'gy'), may hold values from -0.3 to 0.3
- obs_cells: int32 [16, 16, 2, 1024], P('tm', 'gx', 'gy'), may hold values from 0 to 65535
- step_count: int32 [16], P('tm'), may hold values from 1 to 4, as said below
Outputs:
- lagrange_next: float32 [16, 8, 1024, 256], P('tm', None, 'gx', 'gy')
- obs_lagrange_next: float32 [16, 16, 2, 1024], P('tm', 'gx', 'gy')
- increment_next: float32 [16, 8, 1024, 256], P('tm', None, 'gx', 'gy')
- residual_model: float32 [16, 8, 1024, 256], P('tm', None, 'gx', 'gy')
- residual_obs: float32 [16, 16, 2, 1024], P('tm', 'gx', 'gy')
- residual_increment: float32 [16, 8, 1024, 256], P('tm', None, 'gx', 'gy')
Inputs may be any that keep to these rules, and one draw needn't show every extreme that they name: `step_count`: each sub-window's number of model steps; at least one sub-window takes 4.
All inputs are finite; a program needn't handle non-finite values.
Results may differ from a plain program's by a relative error of at most 0.0003.
Values sent between devices are 32-bit elements; how exact they have to be, the bound alone decides.
No kernel may reach another device: no remote copies, remote signals or barrier semaphores. Data moves between devices by JAX's collectives and lax.ppermute only.
A program may use at most 64 MiB of HBM per device.

v0:
```python
import functools

import jax
import jax.numpy as jnp
from jax import lax
from jax.experimental import pallas as pl
from jax.experimental.pallas import tpu as pltpu
from jax.sharding import PartitionSpec as P

DIFFUSION = 0.18
VERTICAL = 0.1
CENTRE = 1.0 - 4.0 * DIFFUSION - 2.0 * VERTICAL

LEV, CX, CY = 8, 64, 128
HALO = 8
EXT = CX + 2 * HALO
TOP = 8
BUF = EXT + 2 * TOP
VMEM_LIMIT = 16 * 1024 * 1024
PACK_LIMIT = 60 * 1024 * 1024
NBLOCKS = 10 * LEV + 6
F32 = jnp.float32

VM = pl.BlockSpec(memory_space=pltpu.VMEM)
SM = pl.BlockSpec(memory_space=pltpu.SMEM)
FAR = pl.BlockSpec(memory_space=pltpu.HBM)


def call(body, outs, ins, scratch=(), micros=1.0, fetched=(), limit=VMEM_LIMIT):
    shapes = [jax.ShapeDtypeStruct(s, F32) for s in outs]
    nbytes = 4 * sum(int(a.size) for a in ins) + 4 * sum(
        functools.reduce(lambda a, b: a * b, s, 1) for s in outs
    )
    in_specs = [SM if (a.dtype == jnp.int32 and a.size < 64) else VM for a in ins]
    for i in fetched:
        in_specs[i] = FAR
    return pl.pallas_call(
        body,
        out_shape=shapes,
        in_specs=in_specs,
        out_specs=[VM] * len(shapes),
        scratch_shapes=list(scratch),
        compiler_params=pltpu.CompilerParams(vmem_limit_bytes=limit),
        cost_estimate=pl.CostEstimate(
            flops=int(1.1e9 * micros), bytes_accessed=nbytes, transcendentals=0
        ),
    )(*ins)


def iota(shape, dim):
    return lax.broadcasted_iota(jnp.int32, shape, dim)


def split(x):
    high = x.astype(jnp.bfloat16)
    low = (x - high.astype(F32)).astype(jnp.bfloat16)
    return high, low


def one_hots(cells):
    n = cells.shape[1]
    rows = (iota((LEV * CX, n), 0) == (cells >> 7)).astype(jnp.bfloat16)
    lanes = iota((CY, n), 0) == (cells & 127)
    return rows, lanes


def scatter(rows, lanes, values):
    high, low = split(values)
    zero = jnp.zeros((), jnp.bfloat16)
    parts = jnp.concatenate(
        [jnp.where(lanes, high.astype(F32), 0.0), jnp.where(lanes, low.astype(F32), 0.0)], 0
    ).astype(jnp.bfloat16)
    both = lax.dot_general(
        rows, parts, (((1,), (1,)), ((), ())), preferred_element_type=F32
    )
    return both[:, :CY] + both[:, CY:]


def gather(rows, lanes, field):
    high, low = split(field)
    both = lax.dot_general(
        jnp.concatenate([high, low], 1), rows, (((0,), (0,)), ((), ())),
        preferred_element_type=F32,
    )
    picked = both[:CY] + both[CY:]
    return jnp.sum(jnp.where(lanes, picked, 0.0), 0, keepdims=True)


def swap_halves(x):
    inner = (iota(x.shape, x.ndim - 1) & 15) < 8
    axis = x.ndim - 1
    return jnp.where(inner, pltpu.roll(x, CY - 8, axis), pltpu.roll(x, 8, axis))


def own_half(shape, gy):
    lane = iota(shape, len(shape) - 1) & 15
    return jnp.where(gy == 0, lane, lane ^ 8) < 8


def pack_kernel(
    cells_h, m_h, l_h, f_h, mv_h, v_h, we_h, wn_h,
    b_out, a_out, by_out, strip_out, z_out, lh_out, g1_out,
    g_s, cells, m, l, f, mv, v, we, wn, sems,
):
    far = (cells_h, m_h, l_h, f_h, mv_h, v_h, we_h, wn_h)
    near = (cells, m, l, f, mv, v, we, wn)
    copies = [pltpu.make_async_copy(a, b, sems.at[i]) for i, (a, b) in enumerate(zip(far, near))]
    for copy in copies:
        copy.start()
    copies[0].wait()
    copies[1].wait()
    core = lax.axis_index("gx") % 2
    gy = lax.axis_index("gy")
    lane = iota((CX, CY), 1)
    for s in range(2):
        rows, lanes = one_hots(cells[s, 0])
        h = scatter(rows, lanes, m[s, 0])
        if s == 0:
            for copy in copies[2:]:
                copy.wait()
        lh_out[s] = l[s] + h.reshape(LEV, CX, CY)
        g_s[s] = f[s] - mv[s] * l[s] - v[s]
    g1_out[...] = g_s[1]
    for z in range(LEV):
        for i in range(CX // 8):
            z_out[z * 8 + i] = l[0, z, 8 * i : 8 * i + 8]
            z_out[64 + z * 8 + i] = g_s[0, z, 8 * i : 8 * i + 8]

    def own(get):
        packed = jnp.zeros((CX, CY), F32)
        for z in range(LEV):
            rolled = pltpu.roll(get(z), (16 * z + 8) % CY, 1)
            packed = jnp.where((lane >> 4) == z, rolled, packed)
        return packed

    half = own_half((CX, CY), gy)
    pairs = (
        ((v, 0), (v, 1)), ((l, 0), (g_s, 0)), ((l, 1), (g_s, 1)),
        ((lh_out, 0), (lh_out, 1)), ((we, 0), (wn, 0)), ((we, 1), (wn, 1)),
    )
    for p, (one, two) in enumerate(pairs):
        first = own(lambda z, one=one: one[0][one[1], z])
        second = own(lambda z, two=two: two[0][two[1], z])
        strip_out[p] = jnp.where(half, first, swap_halves(second))
    for i in range(CX // 8):
        z_out[128 + i] = strip_out[1, 8 * i : 8 * i + 8]

    sub = iota((8, CY), 0)
    for out, top in ((b_out, core == 0), (a_out, core != 0)):
        row = jnp.where(top, 0, CX - 8)
        row = pl.multiple_of(row, 8)
        edge = pl.ds(row, 8)
        for k, field in enumerate((v, l, we, wn)):
            for s in range(2):
                out[pl.ds((2 * k + s) * LEV, LEV)] = field[s, :, edge, :]
        keep = jnp.where(top, sub, 7 - sub) < 4
        for s in range(2):
            for z in range(LEV):
                lh_edge = lh_out[s, z, edge, :]
                g_edge = pltpu.roll(g_s[s, z, edge, :], 4, 0)
                out[(8 + s) * LEV + z] = jnp.where(keep, lh_edge, g_edge)
        out[pl.ds(10 * LEV, 6)] = strip_out[:, edge, :]
    by_out[...] = b_out[10 * LEV :]


def obs_kernel(cells, m, v, dep, ov, rm_out, h2_out):
    for s in range(2):
        rows, lanes = one_hots(cells[s, 0])
        seen = gather(rows, lanes, v[s].reshape(LEV * CX, CY))
        rm = dep[s, 0] - (ov[s, 0] * m[s, 0] + seen)
        rm_out[s, 0] = rm
        h2_out[s] = scatter(rows, lanes, rm).reshape(LEV, CX, CY)


class Place:
    def __init__(self):
        gx = lax.axis_index("gx")
        self.gy = lax.axis_index("gy")
        core = gx % 2
        self.b_row = pl.multiple_of(jnp.where(core == 0, TOP, TOP + HALO + CX), 8)
        self.a_row = pl.multiple_of(jnp.where(core == 0, TOP + HALO + CX, TOP), 8)
        self.core = core
        self.ay_rows = pl.ds(pl.multiple_of(core * 8, 8), 8)
        self.low = jnp.where(gx == 0, 0.0, 1.0)
        self.high = jnp.where(gx == lax.axis_size("gx") - 1, 0.0, 1.0)


def clear(ref, guard_levels):
    lead = ref.shape[:-2]
    zero = jnp.zeros(lead + (TOP, CY), F32)
    ref[..., 0:TOP, :] = zero
    ref[..., BUF - TOP : BUF, :] = zero
    if guard_levels:
        full = jnp.zeros((BUF, CY), F32)
        for i in range(lead[0]):
            ref[i, 0] = full
            ref[i, LEV + 1] = full


def fill(dst, base, place, tile, b_block, a_block):
    for z in range(LEV):
        dst[base + z, TOP + HALO : TOP + HALO + CX] = tile(z)
        dst[base + z, pl.ds(place.b_row, 8)] = b_block(z)
        dst[base + z, pl.ds(place.a_row, 8)] = a_block(z)


def unpack(place, own, received):
    half = own_half(own.shape, place.gy)
    return jnp.where(half, own, received), swap_halves(jnp.where(half, received, own))


def fill_strips(first, second, place, own, got, own_b, got_b, own_a, got_a):
    mid = pl.ds(TOP + HALO, CX)
    for where, a, b in (
        (mid, own, got),
        (pl.ds(place.b_row, 8), own_b, got_b),
        (pl.ds(place.a_row, 8), own_a, got_a),
    ):
        one, two = unpack(place, a, b)
        first[where] = one
        second[where] = two


ROWS = slice(TOP, TOP + EXT)
UP = slice(TOP + 1, TOP + EXT + 1)
DOWN = slice(TOP - 1, TOP + EXT - 1)


def injected(strip, gy):
    lane = iota((EXT, CY), 1) & 15
    moved = jnp.where(gy == 0, pltpu.roll(strip, 119, 1), pltpu.roll(strip, 121, 1))
    return jnp.where(lane == jnp.where(gy == 0, 15, 0), moved, 0.0)


def coefficients(place, wind, strip, coef, scoef, adjoint):
    lane = iota((EXT, CY), 1)
    if not adjoint:
        for z in range(LEV):
            east, north = 0.5 * wind[0, z, ROWS], 0.5 * wind[1, z, ROWS]
            coef[0, z] = DIFFUSION - east
            coef[1, z] = DIFFUSION + east
            coef[2, z] = DIFFUSION - north
            coef[3, z] = DIFFUSION + north
        east, north = 0.5 * strip[0, ROWS], 0.5 * strip[1, ROWS]
        scoef[0] = DIFFUSION - east
        scoef[1] = DIFFUSION + east
        scoef[2] = DIFFUSION - north
        scoef[3] = DIFFUSION + north
        return
    inj = injected(strip[1, ROWS], place.gy)
    for z in range(LEV):
        north = wind[1, z, ROWS]
        edge = pltpu.roll(inj, (CY - 16 * z) % CY, 1)
        after = jnp.where(lane == CY - 1, edge, pltpu.roll(north, CY - 1, 1))
        before = jnp.where(lane == 0, edge, pltpu.roll(north, 1, 1))
        coef[0, z] = DIFFUSION + 0.5 * wind[0, z, UP]
        coef[1, z] = DIFFUSION - 0.5 * wind[0, z, DOWN]
        coef[2, z] = DIFFUSION + 0.5 * after
        coef[3, z] = DIFFUSION - 0.5 * before
    scoef[0] = DIFFUSION + 0.5 * strip[0, UP]
    scoef[1] = DIFFUSION - 0.5 * strip[0, DOWN]
    scoef[2] = DIFFUSION + 0.5 * pltpu.roll(strip[1, ROWS], CY - 1, 1)
    scoef[3] = DIFFUSION - 0.5 * pltpu.roll(strip[1, ROWS], 1, 1)


def store(dst, z, out, place):
    dst[z, TOP : TOP + HALO] = out[:HALO] * place.low
    dst[z, TOP + HALO : TOP + HALO + CX] = out[HALO : HALO + CX]
    dst[z, TOP + HALO + CX : TOP + EXT] = out[HALO + CX :] * place.high


def first_slot(count):
    return count & 1


def one_step(place, src, dst, ssrc, sdst, coef, scoef):
    lane = iota((EXT, CY), 1)
    own = ssrc[ROWS]
    inj = injected(own, place.gy)
    for z in range(LEV):
        mid = src[z + 1, ROWS]
        edge = pltpu.roll(inj, (CY - 16 * z) % CY, 1)
        after = jnp.where(lane == CY - 1, edge, pltpu.roll(mid, CY - 1, 1))
        before = jnp.where(lane == 0, edge, pltpu.roll(mid, 1, 1))
        out = (
            CENTRE * mid
            + coef[0, z] * src[z + 1, UP]
            + coef[1, z] * src[z + 1, DOWN]
            + coef[2, z] * after
            + coef[3, z] * before
            + VERTICAL * (src[z + 2, ROWS] + src[z, ROWS])
        )
        store(dst, z + 1, out, place)
    above = jnp.where(lane < CY - 16, pltpu.roll(own, CY - 16, 1), 0.0)
    below = jnp.where(lane >= 16, pltpu.roll(own, 16, 1), 0.0)
    out = (
        CENTRE * own
        + scoef[0] * ssrc[UP]
        + scoef[1] * ssrc[DOWN]
        + scoef[2] * pltpu.roll(own, CY - 1, 1)
        + scoef[3] * pltpu.roll(own, 1, 1)
        + VERTICAL * (above + below)
    )
    sdst[TOP : TOP + HALO] = out[:HALO] * place.low
    sdst[TOP + HALO : TOP + HALO + CX] = out[HALO : HALO + CX]
    sdst[TOP + HALO + CX : TOP + EXT] = out[HALO + CX :] * place.high


def sweep(place, state, strip, coef, scoef, count):
    def two(i, _):
        for j in range(2):

            @pl.when(2 * i + j >= 4 - count)
            def _():
                one_step(
                    place, state.at[j], state.at[1 - j], strip.at[j, 0], strip.at[1 - j, 0],
                    coef, scoef,
                )

        return 0

    lax.fori_loop(0, 2, two, 0)


STATE = pltpu.VMEM((2, LEV + 2, BUF, CY), F32)
STRIP = pltpu.VMEM((2, 1, BUF, CY), F32)
COEF = pltpu.VMEM((4, LEV, EXT, CY), F32)
SCOEF = pltpu.VMEM((4, EXT, CY), F32)
WIND = pltpu.VMEM((2, LEV, BUF, CY), F32)
WSTRIP = pltpu.VMEM((2, BUF, CY), F32)


def fill_winds(place, s, we, wn, bg, ag, own, got, by, ay, wind, wstrip):
    for k, field in enumerate((we, wn)):
        fill(
            wind.at[k], 0, place, lambda z, field=field: field[s, z],
            lambda z, k=k: bg[(4 + 2 * k + s) * LEV + z],
            lambda z, k=k: ag[(4 + 2 * k + s) * LEV + z],
        )
    p = 4 + s
    fill_strips(
        wstrip.at[0], wstrip.at[1], place, own[p], got[p],
        bg[10 * LEV + p], by[p], ag[10 * LEV + p], ay[p, place.ay_rows],
    )


def first_kernel(
    counts, v, l, we, wn, mv, lh, g1, own, got, bg, ag, by, ay,
    ext_out, rv_out, even_out, odd_out,
    x_f, x_b, s_f, s_b, coef, scoef, wind, wstrip, extra, estrip,
):
    place = Place()
    clear(x_f, True)
    clear(x_b, True)
    for ref in (s_f, s_b, wind, wstrip, extra, estrip):
        clear(ref, False)

    def strips(p, first, second):
        fill_strips(
            first, second, place, own[p], got[p],
            bg[10 * LEV + p], by[p], ag[10 * LEV + p], ay[p, place.ay_rows],
        )

    fill_winds(place, 0, we, wn, bg, ag, own, got, by, ay, wind, wstrip)
    fill(
        x_b.at[first_slot(counts[0])], 1, place, lambda z: l[1, z],
        lambda z: bg[3 * LEV + z], lambda z: ag[3 * LEV + z],
    )
    strips(2, s_b.at[first_slot(counts[0]), 0], estrip.at[1])
    coefficients(place, wind, wstrip, coef, scoef, True)
    sweep(place, x_b, s_b, coef, scoef, counts[0])
    end = 0
    fill(
        extra.at[0], 0, place, lambda z: lh[0, z],
        lambda z: bg[8 * LEV + z], lambda z: ag[8 * LEV + z],
    )
    fill(
        extra.at[1], 0, place, lambda z: g1[z],
        lambda z: pltpu.roll(bg[9 * LEV + z], 4, 0),
        lambda z: pltpu.roll(ag[9 * LEV + z], 4, 0),
    )
    for z in range(LEV):
        rv = x_b[end, z + 1, ROWS] - extra[0, z, ROWS]
        ext_out[0, z] = rv
        rv_out[0, z] = rv[HALO : HALO + CX]
        rv_out[1, z] = mv[0, z]
    strips(3, estrip.at[0], s_f.at[0, 0])
    ext_out[0, LEV] = s_b[end, 0, ROWS] - estrip[0, ROWS]

    for s in range(2):
        if s == 1:
            fill_winds(place, 1, we, wn, bg, ag, own, got, by, ay, wind, wstrip)
        coefficients(place, wind, wstrip, coef, scoef, False)
        fill(
            x_f.at[first_slot(counts[s])], 1, place, lambda z, s=s: v[s, z],
            lambda z, s=s: bg[s * LEV + z], lambda z, s=s: ag[s * LEV + z],
        )
        if s == 0:
            strips(0, s_f.at[first_slot(counts[s]), 0], estrip.at[0])
        else:
            strips(0, estrip.at[0], s_f.at[first_slot(counts[s]), 0])
        sweep(place, x_f, s_f, coef, scoef, counts[s])
        for z in range(LEV):
            out = x_f[end, z + 1, ROWS]
            if s == 0:
                ext_out[1, z] = out + extra[1, z, ROWS]
            else:
                ext_out[2, z] = out
        out = s_f[end, 0, ROWS]
        ext_out[1 + s, LEV] = out + estrip[1, ROWS] if s == 0 else out

    tile = slice(HALO, HALO + CX)
    odd = lax.axis_index("tm") % 2

    @pl.when(odd == 0)
    def _():
        even_out[0] = ext_out[2, :LEV, tile]
        even_out[1] = rv_out[1]
        odd_out[...] = rv_out[...]

    @pl.when(odd == 1)
    def _():
        even_out[...] = rv_out[...]
        odd_out[0] = ext_out[2, :LEV, tile]
        odd_out[1] = rv_out[1]


def lane_sum(x):
    return functools.reduce(
        lambda a, b: a + b, [x[:, i : i + CY] for i in range(0, x.shape[1], CY)]
    )


def second_kernel(
    counts, cells, ext, we, wn, lh, own, got, bg, ag, by, ay, zt, zh,
    mv, h2, rm, ov,
    rv1_out, rl1_out, rl2_out, f21_out, b20_out, ql1_out, qv1_out, qm_out, dots_out,
    x_f, x_b, s_f, s_b, coef, scoef, wind, wstrip, extra, estrip,
):
    place = Place()
    clear(x_f, True)
    clear(x_b, True)
    for ref in (s_f, s_b, wind, wstrip, extra, estrip):
        clear(ref, False)
    tile = slice(HALO, HALO + CX)
    follows = jnp.where(lax.axis_index("tm") == lax.axis_size("tm") - 1, 0.0, 1.0)

    fill_winds(place, 1, we, wn, bg, ag, own, got, by, ay, wind, wstrip)
    coefficients(place, wind, wstrip, coef, scoef, True)

    def z_tile(base):
        return lambda z: zt[base + 8 * z : base + 8 * z + 8].reshape(CX, CY)

    fill(x_b.at[first_slot(counts[1])], 1, place, z_tile(0), lambda z: zh[z], lambda z: zh[16 + z])
    fill(
        extra.at[1], 0, place, z_tile(64),
        lambda z: pltpu.roll(zh[8 + z], 4, 0), lambda z: pltpu.roll(zh[24 + z], 4, 0),
    )
    fill_strips(
        s_b.at[first_slot(counts[1]), 0], estrip.at[1], place,
        zt[128:136].reshape(CX, CY), zh[37:45].reshape(CX, CY),
        zh[32], zh[33], zh[34], zh[35 + place.core],
    )
    sweep(place, x_b, s_b, coef, scoef, counts[1])
    end = 0
    slot = first_slot(counts[1])

    fill(
        extra.at[0], 0, place, lambda z: lh[1, z],
        lambda z: bg[9 * LEV + z], lambda z: ag[9 * LEV + z],
    )
    fill_strips(
        s_f.at[0, 0], estrip.at[0], place, own[3], got[3],
        bg[10 * LEV + 3], by[3], ag[10 * LEV + 3], ay[3, place.ay_rows],
    )
    for z in range(LEV):
        rv = x_b[end, z + 1, ROWS] - extra[0, z, ROWS]
        x_f[slot, z + 1, ROWS] = rv
        rv1_out[z] = rv[tile]
        rl = (extra[1, z, ROWS] + ext[2, z]) * follows
        x_b[slot, z + 1, ROWS] = rl
        rl2_out[z] = rl[tile]
    s_f[slot, 0, ROWS] = s_b[end, 0, ROWS] - estrip[0, ROWS]
    s_b[slot, 0, ROWS] = (estrip[1, ROWS] + ext[2, LEV]) * follows

    sweep(place, x_b, s_b, coef, scoef, counts[1])
    cross = jnp.zeros((8, CY), F32)
    square = jnp.zeros((8, CY), F32)

    def dots(r, q):
        return jnp.sum((r * q).reshape(-1, 8, CY), 0), jnp.sum((q * q).reshape(-1, 8, CY), 0)

    for z in range(LEV):
        rl1 = ext[1, z, tile]
        rl1_out[z] = rl1
        qv = rl1 - x_b[end, z + 1, TOP + HALO : TOP + HALO + CX] + h2[1, z]
        qv1_out[z] = qv
        c, q = dots(rv1_out[z], qv)
        cross, square = cross + c, square + q
    coefficients(place, wind, wstrip, coef, scoef, False)
    sweep(place, x_f, s_f, coef, scoef, counts[1])
    for z in range(LEV):
        f21_out[z] = x_f[end, z + 1, TOP + HALO : TOP + HALO + CX]

    slot = first_slot(counts[0])
    fill_winds(place, 0, we, wn, bg, ag, own, got, by, ay, wind, wstrip)
    coefficients(place, wind, wstrip, coef, scoef, False)
    for z in range(LEV):
        x_f[slot, z + 1, ROWS] = ext[0, z]
        x_b[slot, z + 1, ROWS] = ext[1, z]
    s_f[slot, 0, ROWS] = ext[0, LEV]
    s_b[slot, 0, ROWS] = ext[1, LEV]
    sweep(place, x_f, s_f, coef, scoef, counts[0])
    for z in range(LEV):
        rl1 = ext[1, z, tile]
        ql = mv[1, z] * rl1 + rv1_out[z] - x_f[end, z + 1, TOP + HALO : TOP + HALO + CX]
        ql1_out[z] = ql
        c, q = dots(rl1, ql)
        cross, square = cross + c, square + q
    coefficients(place, wind, wstrip, coef, scoef, True)
    sweep(place, x_b, s_b, coef, scoef, counts[0])
    for z in range(LEV):
        b20_out[z] = x_b[end, z + 1, TOP + HALO : TOP + HALO + CX]

    for s in range(2):
        rows, lanes = one_hots(cells[s, 0])
        if s == 0:
            field = ext[0, 0:LEV, tile].reshape(LEV * CX, CY)
        else:
            field = rv1_out[...].reshape(LEV * CX, CY)
        seen = gather(rows, lanes, field)
        r = rm[s, 0]
        q = ov[s, 0] * r + seen
        qm_out[s, 0] = q
        c, q = lane_sum(r * q), lane_sum(q * q)
        first = iota((8, CY), 0) == 0
        cross = cross + jnp.where(first, c, 0.0)
        square = square + jnp.where(first, q, 0.0)
    dots_out[0] = cross
    dots_out[1] = square


def dots_kernel(
    even, odd, rl2, f21, b20, z_own, h2, rv0, dots_in, rl0_out, qv0_out, send_out
):
    follows = jnp.where(lax.axis_index("tm") == lax.axis_size("tm") - 1, 0.0, 1.0)
    starts = jnp.where(lax.axis_index("tm") == 0, 1.0, 0.0)
    cross, square = dots_in[0], dots_in[1]
    is_odd = lax.axis_index("tm") % 2 == 1

    def total(x):
        return jnp.sum(x.reshape(-1, 8, CY), 0)

    for z in range(LEV):
        rl0 = z_own[64 + 8 * z : 72 + 8 * z].reshape(CX, CY) + jnp.where(is_odd, even[0, z], odd[0, z])
        rv = rv0[0, z]
        qv = rl0 - b20[z] + h2[0, z]
        rl0_out[z] = rl0
        qv0_out[z] = qv
        ql = (rv0[1, z] * rl0 + rv) * starts
        rl2z = rl2[z]
        next_mv = jnp.where(is_odd, odd[1, z], even[1, z])
        next_rv = jnp.where(is_odd, odd[0, z], even[0, z])
        q2 = (next_mv * rl2z + next_rv - f21[z]) * follows
        cross += total(rv * qv) + total(rl0 * ql) + total(rl2z * q2)
        square += total(qv * qv) + total(ql * ql) + total(q2 * q2)
    cross = jnp.sum(jnp.sum(cross, 0, keepdims=True), 1, keepdims=True)
    square = jnp.sum(jnp.sum(square, 0, keepdims=True), 1, keepdims=True)
    n = send_out.shape[0]
    lane = iota((n, CY), 1)
    send_out[...] = jnp.where(lane == 0, cross, jnp.where(lane == 1, square, 0.0))


def last_kernel(
    sums, l, m, v, rl0, rl1, rv0, rv1, rm, z_f2, ql1, qv0, qv1, qm,
    l_out, m_out, v_out, a_out, b_out, c_out,
):
    total = jnp.sum(sums[...], 0, keepdims=True)
    lane = iota((1, CY), 1)
    cross = jnp.sum(jnp.where(lane == 0, total, 0.0), 1, keepdims=True)
    square = jnp.sum(jnp.where(lane == 1, total, 0.0), 1, keepdims=True)
    alpha = cross / (square + 1e-06)
    m_out[...] = m[...] + alpha * rm[...]
    b_out[...] = rm[...] - alpha * qm[...]
    for z in range(LEV):
        ql0 = rv0[1, z] * rl0[z] + rv0[0, z] - z_f2[z]
        l_out[0, z] = l[0, z] + alpha * rl0[z]
        l_out[1, z] = l[1, z] + alpha * rl1[z]
        v_out[0, z] = v[0, z] + alpha * rv0[0, z]
        v_out[1, z] = v[1, z] + alpha * rv1[z]
        a_out[0, z] = rl0[z] - alpha * ql0
        a_out[1, z] = rl1[z] - alpha * ql1[z]
        c_out[0, z] = rv0[0, z] - alpha * qv0[z]
        c_out[1, z] = rv1[z] - alpha * qv1[z]


def shards(sizes, l4, m4, v4, f4, d4, mv4, ov4, we4, wn4, cells4, counts):
    ntm, ngx, ngy = sizes
    tile = (LEV, CX, CY)
    obs = m4.shape

    def pair_b(i):
        return i - 1 if i % 2 == 0 else i + 1

    def plane(move_x, move_y):
        pairs = []
        for x in range(ngx):
            for y in range(ngy):
                to = move_x(x)
                if 0 <= to < ngx:
                    pairs.append((x * ngy + y, to * ngy + (1 - y if move_y else y)))
        return pairs

    axes = ("gx", "gy")
    down = [(i + 1, i) for i in range(ntm - 1)]
    up = [(i, i + 1) for i in range(ntm - 1)]
    edge = 10 * LEV

    fields = pltpu.VMEM((2,) + tile, F32)
    b_send, a_send, by_send, own, z_send, lh, g1 = call(
        pack_kernel,
        [(NBLOCKS, 8, CY)] * 2 + [(6, 8, CY), (6, CX, CY), (136, 8, CY), (2,) + tile, tile],
        [cells4, m4, l4, f4, mv4, v4, we4, wn4],
        [fields, pltpu.VMEM(obs, jnp.int32), pltpu.VMEM(obs, F32)]
        + [fields] * 6
        + [pltpu.SemaphoreType.DMA((8,))],
        micros=2.5,
        fetched=range(8),
        limit=PACK_LIMIT,
    )
    got = lax.ppermute(own, axes, plane(lambda i: i, True))
    bg = lax.ppermute(b_send, axes, plane(pair_b, False))
    ag = lax.ppermute(a_send, axes, plane(lambda i: i ^ 1, False))
    by = lax.ppermute(by_send, axes, plane(pair_b, True))
    zt = lax.ppermute(z_send, "tm", down)
    ay_send = jnp.concatenate([got[:, :8], got[:, CX - 8 :]], 1)
    ay_send, late_cells = lax.optimization_barrier((ay_send, cells4))
    ay = lax.ppermute(ay_send, axes, plane(lambda i: i ^ 1, False))
    rm, h2 = call(obs_kernel, [obs, (2,) + tile], [late_cells, m4, v4, d4, ov4], micros=2.4)

    z_edges = jnp.concatenate(
        [
            bg[2 * LEV : 3 * LEV], bg[8 * LEV : 9 * LEV],
            ag[2 * LEV : 3 * LEV], ag[8 * LEV : 9 * LEV],
            bg[edge + 1 : edge + 2], by[1:2], ag[edge + 1 : edge + 2],
            ay[1].reshape(2, 8, CY), got[1].reshape(8, 8, CY),
        ],
        0,
    )
    zh = lax.ppermute(z_edges, "tm", down)
    scratch = [
        STATE, STATE, STRIP, STRIP, COEF, SCOEF, WIND, WSTRIP,
        pltpu.VMEM((2, LEV, BUF, CY), F32), pltpu.VMEM((2, BUF, CY), F32),
    ]
    ext, rv0, even_send, odd_send = call(
        first_kernel,
        [(3, LEV + 1, EXT, CY)] + [(2,) + tile] * 3,
        [counts, v4, l4, we4, wn4, mv4, lh, g1, own, got, bg, ag, by, ay],
        scratch,
        micros=5.0,
    )
    swap = lambda first: [(i, i + 1) for i in range(first, ntm - 1, 2)] + [
        (i + 1, i) for i in range(first, ntm - 1, 2)
    ]
    even = lax.ppermute(even_send, "tm", swap(0))
    odd = lax.ppermute(odd_send, "tm", swap(1))
    rv1, rl1, rl2, f21, b20, ql1, qv1, qm, dots = call(
        second_kernel,
        [tile] * 7 + [obs, (2, 8, CY)],
        [counts, cells4, ext, we4, wn4, lh, own, got, bg, ag, by, ay, zt, zh, mv4, h2, rm, ov4],
        scratch,
        micros=9.0,
    )
    z_f2 = lax.ppermute(f21, "tm", up)
    n = ntm * ngx * ngy
    rl0, qv0, send = call(
        dots_kernel,
        [tile, tile, (n, CY)],
        [even, odd, rl2, f21, b20, z_send, h2, rv0, dots],
        micros=0.4,
    )
    sums = lax.all_to_all(send, ("tm", "gx", "gy"), 0, 0, tiled=True)
    return call(
        last_kernel,
        [l4.shape, obs, l4.shape, l4.shape, obs, l4.shape],
        [sums, l4, m4, v4, rl0, rl1, rv0, rv1, rm, z_f2, ql1, qv0, qv1, qm],
        micros=1.5,
    )


def solution(mesh):
    field = P("tm", None, "gx", "gy")
    obs = P("tm", "gx", "gy", None)
    sizes = tuple(mesh.shape[a] for a in ("tm", "gx", "gy"))
    return jax.shard_map(
        functools.partial(shards, sizes),
        mesh=mesh,
        in_specs=(field, obs, field, field, obs, field, obs, field, field, obs, P("tm")),
        out_specs=(field, obs, field, field, obs, field),
        check_vma=False,
    )
```

profile of v0, /device:TPU:1, one launch (start us, length us, event | category | flops | bytes accessed | tf_op | source)
XLA Modules:
  0.0 80.4 jit_solution(37654506707044235)
XLA Ops:
  0.7 4.6 %shard_map.154 = (f32[86,8,128]{2,1,0:T(8,128)}, f32[86,8,128]{2,1,0:T(8,128)}, f32[6,8,128]{2,1,0:T(8,128)}, f32[6,64,128]{2,1,0:T(8,128)}, f32[136,8,128]{2,1,...) custom-call(s32[2,1,1,1024]{3,2,1,0:T(1,128)} %cells.2, f32[2,1,1,1024]{3,2,1,0:T(1,128)} %m.3, ...), custom_call_target="tpu_custom_call" | custom-call | flops 2750000128 | bytes 5431296 | tf_op jit(solution)/shard_map/pallas_call | solution.py:37
  5.2 2.2 %collective-permute-start = (f32[6,64,128]{2,1,0:T(8,128)}, f32[6,64,128]{2,1,0:T(8,128)S(1)}, u32[]{:S(2)}, u32[]{:S(2)}) collective-permute-start(f32[6,64,128]{2,1,0:T(8,128)} %get-tuple-element.35.own), channel_id=1, source_target_pairs={{0,1},{1,0},{2,3},{3,2},{4,5},{5,4},{6,7},{7,6},{8,9},{9,8},{10,11... | collective-permute-start | bytes 589832 | tf_op jit(solution)/shard_map/ppermute | solution.py:631
  7.5 4.6 %collective-permute-start.3 = (f32[6,8,128]{2,1,0:T(8,128)}, f32[6,8,128]{2,1,0:T(8,128)S(1)}, u32[]{:S(2)}, u32[]{:S(2)}) collective-permute-start(f32[6,8,128]{2,1,0:T(8,128)} %get-tuple-element.38), channel_id=1, source_target_pairs={{2,5},{3,4},{4,3},{5,2},{6,9},{7,8},{8,7},{9,6},{10,13},{11,12},{1... | collective-permute-start | bytes 73736 | tf_op jit(solution)/shard_map/ppermute | solution.py:634
  12.1 2.6 %collective-permute-start.1 = (f32[86,8,128]{2,1,0:T(8,128)}, f32[86,8,128]{2,1,0:T(8,128)S(1)}, u32[]{:S(2)}, u32[]{:S(2)}) collective-permute-start(f32[86,8,128]{2,1,0:T(8,128)} %get-tuple-element.36), channel_id=1, source_target_pairs={{2,4},{3,5},{4,2},{5,3},{6,8},{7,9},{8,6},{9,7},{10,12},{11,13},{1... | collective-permute-start | bytes 1056776 | tf_op jit(solution)/shard_map/ppermute | solution.py:632
  14.7 0.1 collective-permute-start.2
  14.8 1.3 %collective-permute-start.7 = (f32[136,8,128]{2,1,0:T(8,128)}, f32[136,8,128]{2,1,0:T(8,128)S(1)}, u32[]{:S(2)}, u32[]{:S(2)}) collective-permute-start(f32[136,8,128]{2,1,0:T(8,128)} %get-tuple-element.43.z_own), channel_id=1, source_target_pairs={{32,0},{64,32},{96,64},{128,96},{160,128},{192,160},{224,192},{33,... | collective-permute-start | bytes 1671176 | tf_op jit(solution)/shard_map/ppermute | solution.py:635
  16.2 0.0 copy-start.2
  16.2 0.0 copy-start.3
  16.3 0.6 collective-permute-start.4
  16.9 2.4 %shard_map.156 = (f32[2,1,1,1024]{3,2,1,0:T(1,128)S(1)}, f32[2,8,64,128]{3,2,1,0:T(8,128)S(1)}) custom-call(s32[2,1,1,1024]{3,2,1,0:T(1,128)S(1)} %copy-done.8, f32[2,1,1,1024]{3,2,1,0:T(1,128)S(1)} %copy-done.10, f32[2,8,64,128]{3,2,1,0:T(8,128)S(1)} %copy-done.4, f32[2,1,1,1024]{3,2,1,0:T(1,128)S(1)} %copy-done.7, f32[2,1,1,1024]{3,2,1,0:T(1,128)S(1)} %copy-done.9), custom_call_target="tpu_custom_call" | custom-call | flops 2640000000 | bytes 1089536 | tf_op jit(solution)/shard_map/pallas_call | solution.py:37
  19.3 3.8 %collective-permute-done.1.bg = f32[86,8,128]{2,1,0:T(8,128)S(1)} collective-permute-done((f32[86,8,128]{2,1,0:T(8,128)}, f32[86,8,128]{2,1,0:T(8,128)S(1)}, u32[]{:S(2)}, u32[]{:S(2)}) %collective-permute-start.1) | collective-permute-done | bytes 352288 | tf_op jit(solution)/shard_map/ppermute | solution.py:632
  23.2 1.3 %collective-permute-start.8 = (f32[45,8,128]{2,1,0:T(8,128)S(1)}, f32[45,8,128]{2,1,0:T(8,128)S(1)}, u32[]{:S(2)}, u32[]{:S(2)}) collective-permute-start(f32[45,8,128]{2,1,0:T(8,128)S(1)} %fusion), channel_id=1, source_target_pairs={{32,0},{64,32},{96,64},{128,96},{160,128},{192,160},{224,192},{33,... | collective-permute-start | bytes 552968 | tf_op jit(solution)/shard_map/ppermute | solution.py:650
  24.6 5.9 %shard_map.155 = (f32[3,9,80,128]{3,2,1,0:T(8,128)S(1)}, f32[2,8,64,128]{3,2,1,0:T(8,128)S(1)}, f32[2,8,64,128]{3,2,1,0:T(8,128)S(1)}, f32[2,8,64,128]{3,2,1,0:T(8,128)S(1)}) custom-call(s32[2]{0:T(128)S(1)} %copy-done.11, f32[2,8,64,128]{3,2,1,0:T(8,128)S(1)} %copy-done.4, f32[2,8,64,128]{3,2,1,0:T(8,128)S(1)} %copy-done.5, ...), custom_call_target="tpu_custom_call" | custom-call | flops 5500000256 | bytes 7258120 | tf_op jit(solution)/shard_map/pallas_call | solution.py:37
  30.5 2.3 %collective-permute-start.5 = (f32[2,8,64,128]{3,2,1,0:T(8,128)S(1)}, f32[2,8,64,128]{3,2,1,0:T(8,128)S(1)}, u32[]{:S(2)}, u32[]{:S(2)}) collective-permute-start(f32[2,8,64,128]{3,2,1,0:T(8,128)S(1)} %get-tuple-element.40), channel_id=1, source_target_pairs={{0,32},{64,96},{128,160},{192,224},{32,0},{96,64},{160,128},{224,1... | collective-permute-start | bytes 1572872 | tf_op jit(solution)/shard_map/ppermute | solution.py:665
  32.9 0.9 %collective-permute-start.6 = (f32[2,8,64,128]{3,2,1,0:T(8,128)S(1)}, f32[2,8,64,128]{3,2,1,0:T(8,128)S(1)}, u32[]{:S(2)}, u32[]{:S(2)}) collective-permute-start(f32[2,8,64,128]{3,2,1,0:T(8,128)S(1)} %get-tuple-element.41), channel_id=1, source_target_pairs={{32,64},{96,128},{160,192},{64,32},{128,96},{192,160},{33,65},{97,... | collective-permute-start | bytes 1572872 | tf_op jit(solution)/shard_map/ppermute | solution.py:666
  33.7 1.3 %collective-permute-done.8.zh = f32[45,8,128]{2,1,0:T(8,128)S(1)} collective-permute-done((f32[45,8,128]{2,1,0:T(8,128)S(1)}, f32[45,8,128]{2,1,0:T(8,128)S(1)}, u32[]{:S(2)}, u32[]{:S(2)}) %collective-permute-start.8) | collective-permute-done | bytes 184352 | tf_op jit(solution)/shard_map/ppermute | solution.py:650
  35.0 9.0 %shard_map.157 = (f32[8,64,128]{2,1,0:T(8,128)S(1)}, f32[8,64,128]{2,1,0:T(8,128)S(1)}, f32[8,64,128]{2,1,0:T(8,128)S(1)}, f32[8,64,128]{2,1,0:T(8,128)S(1)}, f3...) custom-call(s32[2]{0:T(128)S(1)} %copy-done.11, ...), custom_call_target="tpu_custom_call" | custom-call | flops 9900000256 | bytes 7516168 | tf_op jit(solution)/shard_map/pallas_call | solution.py:37
  44.1 5.6 %collective-permute-start.9 = (f32[8,64,128]{2,1,0:T(8,128)S(1)}, f32[8,64,128]{2,1,0:T(8,128)S(1)}, u32[]{:S(2)}, u32[]{:S(2)}) collective-permute-start(f32[8,64,128]{2,1,0:T(8,128)S(1)} %get-tuple-element.48.f21), channel_id=1, source_target_pairs={{0,32},{32,64},{64,96},{96,128},{128,160},{160,192},{192,224},{1,3... | collective-permute-start | bytes 786440 | tf_op jit(solution)/shard_map/ppermute | solution.py:674
  49.7 1.0 %shard_map.158 = (f32[8,64,128]{2,1,0:T(8,128)S(1)}, f32[8,64,128]{2,1,0:T(8,128)S(1)}, f32[256,128]{1,0:T(8,128)}) custom-call(f32[2,8,64,128]{3,2,1,0:T(8,128)S(1)} %collective-permute-done.5.even, f32[2,8,64,128]{3,2,1,0:T(8,128)S(1)} %collective-permute-done.6.odd, f32[8,64,128]{2,1,0:T(8,128)S(1)} %get-tuple-element.47.rl2, ...), custom_call_target="tpu_custom_call" | custom-call | flops 440000000 | bytes 4104192 | tf_op jit(solution)/shard_map/pallas_call | solution.py:37
  50.7 13.9 %all-to-all-start = ((f32[256,1,128]{2,1,0:T(1,128)}), f32[256,1,128]{2,1,0:T(1,128)S(1)}, u32[]{:S(2)}, u32[]{:S(2)}) async-start(f32[256,1,128]{2,1,0:T(1,128)} %bitcast.3), calls=%async_computation | async-start | bytes 262144 | tf_op jit(solution)/shard_map/all_to_all | solution.py:682
  64.6 12.7 %all-to-all-done = f32[256,1,128]{2,1,0:T(1,128)S(1)} async-done(((f32[256,1,128]{2,1,0:T(1,128)}), f32[256,1,128]{2,1,0:T(1,128)S(1)}, u32[]{:S(2)}, u32[]{:S(2)}) %all-to-all-start) | async-done | bytes 131104 | tf_op jit(solution)/shard_map/all_to_all | solution.py:682
  77.3 0.9 %copy-done.13 = f32[8,64,128]{2,1,0:T(8,128)S(1)} copy-done((f32[8,64,128]{2,1,0:T(8,128)S(1)}, f32[8,64,128]{2,1,0:T(8,128)}, u32[]{:S(2)}) %copy-start.13) | copy-done | bytes 262168
  78.2 0.7 copy-done.17
  78.9 1.5 %shard_map.159 = (f32[2,8,64,128]{3,2,1,0:T(8,128)}, f32[2,1,1,1024]{3,2,1,0:T(1,128)}, f32[2,8,64,128]{3,2,1,0:T(8,128)}, f32[2,8,64,128]{3,2,1,0:T(8,128)}, f3...) custom-call(f32[256,128]{1,0:T(8,128)S(1)} %bitcast.12, f32[2,8,64,128]{3,2,1,0:T(8,128)S(1)} %copy-done.5, ...), custom_call_target="tpu_custom_call" | custom-call | flops 1650000000 | bytes 5677056 | tf_op jit(solution)/shard_map/pallas_call | solution.py:37
  (51 shorter events, 0.1 us)
Async XLA Ops:
  0.6 16.2 %copy-start.4 = (f32[2,8,64,128]{3,2,1,0:T(8,128)S(1)}, f32[2,8,64,128]{3,2,1,0:T(8,128)}, u32[]{:S(2)}) copy-start(f32[2,8,64,128]{3,2,1,0:T(8,128)} %v.5) | copy-start | bytes 1572868
  0.6 16.2 %copy-start.8 = (s32[2,1,1,1024]{3,2,1,0:T(1,128)S(1)}, s32[2,1,1,1024]{3,2,1,0:T(1,128)}, u32[]{:S(2)}) copy-start(s32[2,1,1,1024]{3,2,1,0:T(1,128)} %cells.2) | copy-start | bytes 24580
  0.7 16.2 %copy-start.10 = (f32[2,1,1,1024]{3,2,1,0:T(1,128)S(1)}, f32[2,1,1,1024]{3,2,1,0:T(1,128)}, u32[]{:S(2)}) copy-start(f32[2,1,1,1024]{3,2,1,0:T(1,128)} %m.3) | copy-start | bytes 24580
  0.7 16.2 %copy-start.9 = (f32[2,1,1,1024]{3,2,1,0:T(1,128)S(1)}, f32[2,1,1,1024]{3,2,1,0:T(1,128)}, u32[]{:S(2)}) copy-start(f32[2,1,1,1024]{3,2,1,0:T(1,128)} %ov.3) | copy-start | bytes 24580
  0.7 16.2 %copy-start.7 = (f32[2,1,1,1024]{3,2,1,0:T(1,128)S(1)}, f32[2,1,1,1024]{3,2,1,0:T(1,128)}, u32[]{:S(2)}) copy-start(f32[2,1,1,1024]{3,2,1,0:T(1,128)} %dep.1) | copy-start | bytes 24580
  5.2 10.9 %collective-permute-start = (f32[6,64,128]{2,1,0:T(8,128)}, f32[6,64,128]{2,1,0:T(8,128)S(1)}, u32[]{:S(2)}, u32[]{:S(2)}) collective-permute-start(f32[6,64,128]{2,1,0:T(8,128)} %get-tuple-element.35.own), channel_id=1, source_target_pairs={{0,1},{1,0},{2,3},{3,2},{4,5},{5,4},{6,7},{7,6},{8,9},{9,8},{10,11... | collective-permute-start | bytes 589832 | tf_op jit(solution)/shard_map/ppermute | solution.py:631
  7.5 15.7 %collective-permute-start.3 = (f32[6,8,128]{2,1,0:T(8,128)}, f32[6,8,128]{2,1,0:T(8,128)S(1)}, u32[]{:S(2)}, u32[]{:S(2)}) collective-permute-start(f32[6,8,128]{2,1,0:T(8,128)} %get-tuple-element.38), channel_id=1, source_target_pairs={{2,5},{3,4},{4,3},{5,2},{6,9},{7,8},{8,7},{9,6},{10,13},{11,12},{1... | collective-permute-start | bytes 73736 | tf_op jit(solution)/shard_map/ppermute | solution.py:634
  12.1 11.0 %collective-permute-start.1 = (f32[86,8,128]{2,1,0:T(8,128)}, f32[86,8,128]{2,1,0:T(8,128)S(1)}, u32[]{:S(2)}, u32[]{:S(2)}) collective-permute-start(f32[86,8,128]{2,1,0:T(8,128)} %get-tuple-element.36), channel_id=1, source_target_pairs={{2,4},{3,5},{4,2},{5,3},{6,8},{7,9},{8,6},{9,7},{10,12},{11,13},{1... | collective-permute-start | bytes 1056776 | tf_op jit(solution)/shard_map/ppermute | solution.py:632
  14.7 8.4 %collective-permute-start.2 = (f32[86,8,128]{2,1,0:T(8,128)}, f32[86,8,128]{2,1,0:T(8,128)S(1)}, u32[]{:S(2)}, u32[]{:S(2)}) collective-permute-start(f32[86,8,128]{2,1,0:T(8,128)} %get-tuple-element.37), channel_id=1, source_target_pairs={{0,2},{1,3},{2,0},{3,1},{4,6},{5,7},{6,4},{7,5},{8,10},{9,11},{10,... | collective-permute-start | bytes 1056776 | tf_op jit(solution)/shard_map/ppermute | solution.py:633
  14.8 20.2 %collective-permute-start.7 = (f32[136,8,128]{2,1,0:T(8,128)}, f32[136,8,128]{2,1,0:T(8,128)S(1)}, u32[]{:S(2)}, u32[]{:S(2)}) collective-permute-start(f32[136,8,128]{2,1,0:T(8,128)} %get-tuple-element.43.z_own), channel_id=1, source_target_pairs={{32,0},{64,32},{96,64},{128,96},{160,128},{192,160},{224,192},{33,... | collective-permute-start | bytes 1671176 | tf_op jit(solution)/shard_map/ppermute | solution.py:635
  16.2 8.3 %copy-start.1 = (f32[2,8,64,128]{3,2,1,0:T(8,128)S(1)}, f32[2,8,64,128]{3,2,1,0:T(8,128)}, u32[]{:S(2)}) copy-start(f32[2,8,64,128]{3,2,1,0:T(8,128)} %we.3) | copy-start | bytes 1572868
  16.2 8.3 %copy-start.2 = (f32[2,8,64,128]{3,2,1,0:T(8,128)S(1)}, f32[2,8,64,128]{3,2,1,0:T(8,128)}, u32[]{:S(2)}) copy-start(f32[2,8,64,128]{3,2,1,0:T(8,128)} %wn.3) | copy-start | bytes 1572868
  16.2 8.3 %copy-start.3 = (f32[2,8,64,128]{3,2,1,0:T(8,128)S(1)}, f32[2,8,64,128]{3,2,1,0:T(8,128)}, u32[]{:S(2)}) copy-start(f32[2,8,64,128]{3,2,1,0:T(8,128)} %mv.3) | copy-start | bytes 1572868
  16.2 8.3 %copy-start.5 = (f32[2,8,64,128]{3,2,1,0:T(8,128)S(1)}, f32[2,8,64,128]{3,2,1,0:T(8,128)}, u32[]{:S(2)}) copy-start(f32[2,8,64,128]{3,2,1,0:T(8,128)} %l.3) | copy-start | bytes 1572868
  16.2 8.3 %copy-start.6 = (f32[6,64,128]{2,1,0:T(8,128)S(1)}, f32[6,64,128]{2,1,0:T(8,128)}, u32[]{:S(2)}) copy-start(f32[6,64,128]{2,1,0:T(8,128)} %get-tuple-element.35.own) | copy-start | bytes 589828
  16.2 8.3 %copy-start.11 = (s32[2]{0:T(128)S(1)}, s32[2]{0:T(128)}, u32[]{:S(2)}) copy-start(s32[2]{0:T(128)} %counts.3) | copy-start | bytes 28
  16.3 8.3 %copy-start.14 = (f32[2,8,64,128]{3,2,1,0:T(8,128)S(1)}, f32[2,8,64,128]{3,2,1,0:T(8,128)}, u32[]{:S(2)}) copy-start(f32[2,8,64,128]{3,2,1,0:T(8,128)} %get-tuple-element.33.lh) | copy-start | bytes 1572868
  16.3 6.9 %collective-permute-start.4 = (f32[6,16,128]{2,1,0:T(8,128)S(1)}, f32[6,16,128]{2,1,0:T(8,128)S(1)}, u32[]{:S(2)}, u32[]{:S(2)}) collective-permute-start(f32[6,16,128]{2,1,0:T(8,128)S(1)} %pad_maximum_fusion), channel_id=1, source_target_pairs={{0,2},{1,3},{2,0},{3,1},{4,6},{5,7},{6,4},{7,5},{8,10},{9,11},{10,... | collective-permute-start | bytes 147464 | tf_op jit(solution)/shard_map/ppermute | solution.py:638
  23.2 11.8 %collective-permute-start.8 = (f32[45,8,128]{2,1,0:T(8,128)S(1)}, f32[45,8,128]{2,1,0:T(8,128)S(1)}, u32[]{:S(2)}, u32[]{:S(2)}) collective-permute-start(f32[45,8,128]{2,1,0:T(8,128)S(1)} %fusion), channel_id=1, source_target_pairs={{32,0},{64,32},{96,64},{128,96},{160,128},{192,160},{224,192},{33,... | collective-permute-start | bytes 552968 | tf_op jit(solution)/shard_map/ppermute | solution.py:650
  30.5 19.1 %collective-permute-start.5 = (f32[2,8,64,128]{3,2,1,0:T(8,128)S(1)}, f32[2,8,64,128]{3,2,1,0:T(8,128)S(1)}, u32[]{:S(2)}, u32[]{:S(2)}) collective-permute-start(f32[2,8,64,128]{3,2,1,0:T(8,128)S(1)} %get-tuple-element.40), channel_id=1, source_target_pairs={{0,32},{64,96},{128,160},{192,224},{32,0},{96,64},{160,128},{224,1... | collective-permute-start | bytes 1572872 | tf_op jit(solution)/shard_map/ppermute | solution.py:665
  32.9 16.8 %collective-permute-start.6 = (f32[2,8,64,128]{3,2,1,0:T(8,128)S(1)}, f32[2,8,64,128]{3,2,1,0:T(8,128)S(1)}, u32[]{:S(2)}, u32[]{:S(2)}) collective-permute-start(f32[2,8,64,128]{3,2,1,0:T(8,128)S(1)} %get-tuple-element.41), channel_id=1, source_target_pairs={{32,64},{96,128},{160,192},{64,32},{128,96},{192,160},{33,65},{97,... | collective-permute-start | bytes 1572872 | tf_op jit(solution)/shard_map/ppermute | solution.py:666
  35.0 14.7 %copy-start = (f32[136,8,128]{2,1,0:T(8,128)S(1)}, f32[136,8,128]{2,1,0:T(8,128)}, u32[]{:S(2)}) copy-start(f32[136,8,128]{2,1,0:T(8,128)} %get-tuple-element.43.z_own) | copy-start | bytes 1671172
  44.1 20.5 %collective-permute-start.9 = (f32[8,64,128]{2,1,0:T(8,128)S(1)}, f32[8,64,128]{2,1,0:T(8,128)S(1)}, u32[]{:S(2)}, u32[]{:S(2)}) collective-permute-start(f32[8,64,128]{2,1,0:T(8,128)S(1)} %get-tuple-element.48.f21), channel_id=1, source_target_pairs={{0,32},{32,64},{64,96},{96,128},{128,160},{160,192},{192,224},{1,3... | collective-permute-start | bytes 786440 | tf_op jit(solution)/shard_map/ppermute | solution.py:674
  50.7 26.6 %all-to-all-start = ((f32[256,1,128]{2,1,0:T(1,128)}), f32[256,1,128]{2,1,0:T(1,128)S(1)}, u32[]{:S(2)}, u32[]{:S(2)}) async-start(f32[256,1,128]{2,1,0:T(1,128)} %bitcast.3), calls=%async_computation | async-start | bytes 262144 | tf_op jit(solution)/shard_map/all_to_all | solution.py:682
  (5 other events, 23.3 us)
where the time goes:
time: 80.2 us; the launch traced here: 80.4 us
  starting transfers between devices  35.4 us (44%)
  Pallas kernels  24.5 us (31%)
  waiting for transfers between devices  17.8 us (22%)
  local copies, waits for them, and re-layouts  1.77 us (2%)
  between operations  1.06 us (1%)
    pallas_call x6, Pallas kernels, call(): pl.pallas_call(body, out_shape=shapes, in_specs=in_specs, out_specs=[VM]...  24.5 us
    all_to_all x1, starting transfers between devices, shards(): sums = lax.all_to_all(send, ('tm', 'gx', 'gy'), 0, 0, tiled=True)  13.9 us
    all_to_all x1, waiting for transfers between devices, shards(): sums = lax.all_to_all(send, ('tm', 'gx', 'gy'), 0, 0, tiled=True)  12.7 us
    ppermute x1, starting transfers between devices, shards(): z_f2 = lax.ppermute(f21, 'tm', up)  5.58 us
    ppermute x1, starting transfers between devices, shards(): by = lax.ppermute(by_send, axes, plane(pair_b, True))  4.63 us
    ppermute x1, waiting for transfers between devices, shards(): bg = lax.ppermute(b_send, axes, plane(pair_b, False))  3.78 us
    ppermute x1, starting transfers between devices, shards(): bg = lax.ppermute(b_send, axes, plane(pair_b, False))  2.64 us
    ppermute x1, starting transfers between devices, shards(): even = lax.ppermute(even_send, 'tm', swap(0))  2.34 us
  transfers between devices with their start and end apart: 11, of which 3 were waited for; matrix products, arithmetic and copies ran while one was open for 0% of the time, Pallas kernels for 23%

commit v1 on v0

--- a/solution.py
+++ b/solution.py
@@ -26,7 +26,7 @@
 FAR = pl.BlockSpec(memory_space=pltpu.HBM)
 
 
-def call(body, outs, ins, scratch=(), micros=1.0, fetched=(), limit=VMEM_LIMIT):
+def call(body, outs, ins, scratch=(), micros=1.0, fetched=(), written=(), limit=VMEM_LIMIT):
     shapes = [jax.ShapeDtypeStruct(s, F32) for s in outs]
     nbytes = 4 * sum(int(a.size) for a in ins) + 4 * sum(
         functools.reduce(lambda a, b: a * b, s, 1) for s in outs
@@ -38,7 +38,7 @@
         body,
         out_shape=shapes,
         in_specs=in_specs,
-        out_specs=[VM] * len(shapes),
+        out_specs=[FAR if i in written else VM for i in range(len(shapes))],
         scratch_shapes=list(scratch),
         compiler_params=pltpu.CompilerParams(vmem_limit_bytes=limit),
         cost_estimate=pl.CostEstimate(
@@ -99,7 +99,7 @@
 
 def pack_kernel(
     cells_h, m_h, l_h, f_h, mv_h, v_h, we_h, wn_h,
-    b_out, a_out, by_out, strip_out, z_out, lh_out, g1_out,
+    b_out, a_out, strip_out, z_out, lh_out, g1_out,
     g_s, cells, m, l, f, mv, v, we, wn, sems,
 ):
     far = (cells_h, m_h, l_h, f_h, mv_h, v_h, we_h, wn_h)
@@ -160,7 +160,6 @@
                 g_edge = pltpu.roll(g_s[s, z, edge, :], 4, 0)
                 out[(8 + s) * LEV + z] = jnp.where(keep, lh_edge, g_edge)
         out[pl.ds(10 * LEV, 6)] = strip_out[:, edge, :]
-    by_out[...] = b_out[10 * LEV :]
 
 
 def obs_kernel(cells, m, v, dep, ov, rm_out, h2_out):
@@ -432,7 +431,7 @@
 
 
 def second_kernel(
-    counts, cells, ext, we, wn, lh, own, got, bg, ag, by, ay, zt, zh,
+    counts, cells, ext, we, wn, lh, own, got, bg, ag, by, ay, zt, zh_even, zh_odd,
     mv, h2, rm, ov,
     rv1_out, rl1_out, rl2_out, f21_out, b20_out, ql1_out, qv1_out, qm_out, dots_out,
     x_f, x_b, s_f, s_b, coef, scoef, wind, wstrip, extra, estrip,
@@ -445,21 +444,24 @@
     tile = slice(HALO, HALO + CX)
     follows = jnp.where(lax.axis_index("tm") == lax.axis_size("tm") - 1, 0.0, 1.0)
 
+    def zh(i):
+        return zh_even[i] + zh_odd[i]
+
     fill_winds(place, 1, we, wn, bg, ag, own, got, by, ay, wind, wstrip)
     coefficients(place, wind, wstrip, coef, scoef, True)
 
     def z_tile(base):
         return lambda z: zt[base + 8 * z : base + 8 * z + 8].reshape(CX, CY)
 
-    fill(x_b.at[first_slot(counts[1])], 1, place, z_tile(0), lambda z: zh[z], lambda z: zh[16 + z])
+    fill(x_b.at[first_slot(counts[1])], 1, place, z_tile(0), lambda z: zh(z), lambda z: zh(16 + z))
     fill(
         extra.at[1], 0, place, z_tile(64),
-        lambda z: pltpu.roll(zh[8 + z], 4, 0), lambda z: pltpu.roll(zh[24 + z], 4, 0),
+        lambda z: pltpu.roll(zh(8 + z), 4, 0), lambda z: pltpu.roll(zh(24 + z), 4, 0),
     )
     fill_strips(
         s_b.at[first_slot(counts[1]), 0], estrip.at[1], place,
-        zt[128:136].reshape(CX, CY), zh[37:45].reshape(CX, CY),
-        zh[32], zh[33], zh[34], zh[35 + place.core],
+        zt[128:136].reshape(CX, CY), zh(slice(37, 45)).reshape(CX, CY),
+        zh(32), zh(33), zh(34), zh(35 + place.core),
     )
     sweep(place, x_b, s_b, coef, scoef, counts[1])
     end = 0
@@ -572,26 +574,50 @@
 
 
 def last_kernel(
-    sums, l, m, v, rl0, rl1, rv0, rv1, rm, z_f2, ql1, qv0, qv1, qm,
-    l_out, m_out, v_out, a_out, b_out, c_out,
+    sums, l, m, v, rl0, rl1, rv0, rv1, rm, f2_even, f2_odd, ql1, qv0, qv1_far, qm_far,
+    l_far, m_out, v_far, a_far, b_out, c_far,
+    qv1, qm, l_out, v_out, a_out, c_out, sems,
 ):
+    fetches = [
+        pltpu.make_async_copy(qv1_far, qv1, sems.at[0]),
+        pltpu.make_async_copy(qm_far, qm, sems.at[1]),
+    ]
+    for copy in fetches:
+        copy.start()
+    writes = [
+        pltpu.make_async_copy(near, far, sems.at[2 + i])
+        for i, (near, far) in enumerate(
+            ((l_out, l_far), (v_out, v_far), (a_out, a_far), (c_out, c_far))
+        )
+    ]
     total = jnp.sum(sums[...], 0, keepdims=True)
     lane = iota((1, CY), 1)
     cross = jnp.sum(jnp.where(lane == 0, total, 0.0), 1, keepdims=True)
     square = jnp.sum(jnp.where(lane == 1, total, 0.0), 1, keepdims=True)
     alpha = cross / (square + 1e-06)
+    for z in range(LEV):
+        l_out[0, z] = l[0, z] + alpha * rl0[z]
+        l_out[1, z] = l[1, z] + alpha * rl1[z]
+    writes[0].start()
+    for z in range(LEV):
+        v_out[0, z] = v[0, z] + alpha * rv0[0, z]
+        v_out[1, z] = v[1, z] + alpha * rv1[z]
+    writes[1].start()
+    for z in range(LEV):
+        ql0 = rv0[1, z] * rl0[z] + rv0[0, z] - (f2_even[z] + f2_odd[z])
+        a_out[0, z] = rl0[z] - alpha * ql0
+        a_out[1, z] = rl1[z] - alpha * ql1[z]
+    writes[2].start()
+    for copy in fetches:
+        copy.wait()
+    for z in range(LEV):
+        c_out[0, z] = rv0[0, z] - alpha * qv0[z]
+        c_out[1, z] = rv1[z] - alpha * qv1[z]
+    writes[3].start()
     m_out[...] = m[...] + alpha * rm[...]
     b_out[...] = rm[...] - alpha * qm[...]
-    for z in range(LEV):
-        ql0 = rv0[1, z] * rl0[z] + rv0[0, z] - z_f2[z]
-        l_out[0, z] = l[0, z] + alpha * rl0[z]
-        l_out[1, z] = l[1, z] + alpha * rl1[z]
-        v_out[0, z] = v[0, z] + alpha * rv0[0, z]
-        v_out[1, z] = v[1, z] + alpha * rv1[z]
-        a_out[0, z] = rl0[z] - alpha * ql0
-        a_out[1, z] = rl1[z] - alpha * ql1[z]
-        c_out[0, z] = rv0[0, z] - alpha * qv0[z]
-        c_out[1, z] = rv1[z] - alpha * qv1[z]
+    for copy in writes:
+        copy.wait()
 
 
 def shards(sizes, l4, m4, v4, f4, d4, mv4, ov4, we4, wn4, cells4, counts):
@@ -617,9 +643,9 @@
     edge = 10 * LEV
 
     fields = pltpu.VMEM((2,) + tile, F32)
-    b_send, a_send, by_send, own, z_send, lh, g1 = call(
+    b_send, a_send, own, z_send, lh, g1 = call(
         pack_kernel,
-        [(NBLOCKS, 8, CY)] * 2 + [(6, 8, CY), (6, CX, CY), (136, 8, CY), (2,) + tile, tile],
+        [(NBLOCKS, 8, CY)] * 2 + [(6, CX, CY), (136, 8, CY), (2,) + tile, tile],
         [cells4, m4, l4, f4, mv4, v4, we4, wn4],
         [fields, pltpu.VMEM(obs, jnp.int32), pltpu.VMEM(obs, F32)]
         + [fields] * 6
@@ -631,7 +657,7 @@
     got = lax.ppermute(own, axes, plane(lambda i: i, True))
     bg = lax.ppermute(b_send, axes, plane(pair_b, False))
     ag = lax.ppermute(a_send, axes, plane(lambda i: i ^ 1, False))
-    by = lax.ppermute(by_send, axes, plane(pair_b, True))
+    by = lax.ppermute(b_send[edge:], axes, plane(pair_b, True))
     zt = lax.ppermute(z_send, "tm", down)
     ay_send = jnp.concatenate([got[:, :8], got[:, CX - 8 :]], 1)
     ay_send, late_cells = lax.optimization_barrier((ay_send, cells4))
@@ -647,7 +673,8 @@
         ],
         0,
     )
-    zh = lax.ppermute(z_edges, "tm", down)
+    zh_even = lax.ppermute(z_edges, "tm", down[0::2])
+    zh_odd = lax.ppermute(z_edges, "tm", down[1::2])
     scratch = [
         STATE, STATE, STRIP, STRIP, COEF, SCOEF, WIND, WSTRIP,
         pltpu.VMEM((2, LEV, BUF, CY), F32), pltpu.VMEM((2, BUF, CY), F32),
@@ -667,11 +694,12 @@
     rv1, rl1, rl2, f21, b20, ql1, qv1, qm, dots = call(
         second_kernel,
         [tile] * 7 + [obs, (2, 8, CY)],
-        [counts, cells4, ext, we4, wn4, lh, own, got, bg, ag, by, ay, zt, zh, mv4, h2, rm, ov4],
+        [counts, cells4, ext, we4, wn4, lh, own, got, bg, ag, by, ay, zt, zh_even, zh_odd, mv4, h2, rm, ov4],
         scratch,
         micros=9.0,
     )
-    z_f2 = lax.ppermute(f21, "tm", up)
+    f2_even = lax.ppermute(f21, "tm", up[0::2])
+    f2_odd = lax.ppermute(f21, "tm", up[1::2])
     n = ntm * ngx * ngy
     rl0, qv0, send = call(
         dots_kernel,
@@ -683,8 +711,13 @@
     return call(
         last_kernel,
         [l4.shape, obs, l4.shape, l4.shape, obs, l4.shape],
-        [sums, l4, m4, v4, rl0, rl1, rv0, rv1, rm, z_f2, ql1, qv0, qv1, qm],
+        [sums, l4, m4, v4, rl0, rl1, rv0, rv1, rm, f2_even, f2_odd, ql1, qv0, qv1, qm],
+        [pltpu.VMEM(tile, F32), pltpu.VMEM(obs, F32)]
+        + [fields] * 4
+        + [pltpu.SemaphoreType.DMA((6,))],
         micros=1.5,
+        fetched=(13, 14),
+        written=(0, 2, 3, 5),
     )
 
 

time: 80.2 us -> 87.8 us (1.095)
  starting transfers between devices: 35.4 us -> 42.7 us
  local copies, waits for them, and re-layouts: 1.77 us -> 3.48 us
  waiting for transfers between devices: 17.8 us -> 16.2 us
  Pallas kernels: 24.5 us -> 23.5 us
    ppermute x1, starting transfers between devices: 2.64 us -> 5.36 us  [shards(): bg = lax.ppermute(b_send, axes, plane(pair_b, False))]
    ppermute x1, waiting for transfers between devices: 3.78 us -> 1.43 us  [shards(): bg = lax.ppermute(b_send, axes, plane(pair_b, False))]
    all_to_all x1, starting transfers between devices: 13.9 us -> 15.7 us  [shards(): sums = lax.all_to_all(send, ('tm', 'gx', 'gy'), 0, 0, tiled=True)]
    ppermute x3 -> x5, starting transfers between devices: 11.5 us -> 13 us  [the longest x1 8.48 us: shards(): f2_even = lax.ppermute(f21, 'tm', up[0::2])]
    ppermute x1, starting transfers between devices: 2.34 us -> 3.57 us  [shards(): even = lax.ppermute(even_send, 'tm', swap(0))]
    unnamed x44 -> x48, local copies, waits for them, and re-layouts: 1.76 us -> 2.72 us
    pallas_call x6, Pallas kernels: 24.5 us -> 23.5 us  [call(): pl.pallas_call(body, out_shape=shapes, in_specs=in_specs, out_specs=[FAR...]
    ppermute x3 -> x5, waiting for transfers between devices: 1.28 us -> 2.13 us  [the longest x1 2.12 us: shards(): zh_even = lax.ppermute(z_edges, 'tm', down[0::2])]
  transfers between devices with their start and end apart: 11 -> 13, of which waited for: 3 -> 3; matrix products, arithmetic and copies ran while one was open for 0% -> 1% of each run, Pallas kernels for 23% -> 19%
where the time goes in v1:
time: 87.8 us; the launch traced here: 87.2 us
  starting transfers between devices  42.7 us (49%)
  Pallas kernels  23.5 us (27%)
  waiting for transfers between devices  16.2 us (18%)
  local copies, waits for them, and re-layouts  3.48 us (4%)
  between operations  1.26 us (1%)
    pallas_call x6, Pallas kernels, call(): pl.pallas_call(body, out_shape=shapes, in_specs=in_specs, out_specs=[FAR...  23.5 us
    all_to_all x1, starting transfers between devices, shards(): sums = lax.all_to_all(send, ('tm', 'gx', 'gy'), 0, 0, tiled=True)  15.7 us
    all_to_all x1, waiting for transfers between devices, shards(): sums = lax.all_to_all(send, ('tm', 'gx', 'gy'), 0, 0, tiled=True)  12.7 us
    ppermute x1, starting transfers between devices, shards(): f2_even = lax.ppermute(f21, 'tm', up[0::2])  8.48 us
    ppermute x1, starting transfers between devices, shards(): bg = lax.ppermute(b_send, axes, plane(pair_b, False))  5.36 us
    ppermute x1, starting transfers between devices, shards(): even = lax.ppermute(even_send, 'tm', swap(0))  3.57 us
    unnamed x48, local copies, waits for them, and re-layouts  2.72 us
    ppermute x1, starting transfers between devices, shards(): got = lax.ppermute(own, axes, plane(lambda i: i, True))  2.21 us
  transfers between devices with their start and end apart: 13, of which 3 were waited for; matrix products, arithmetic and copies ran while one was open for 1% of the time, Pallas kernels for 19%

profile of v1, /device:TPU:1, one launch (start us, length us, event | category | flops | bytes accessed | tf_op | source)
XLA Modules:
  0.0 87.2 jit_solution(15835934036149611574)
XLA Ops:
  0.7 4.6 %shard_map.154 = (f32[86,8,128]{2,1,0:T(8,128)}, f32[86,8,128]{2,1,0:T(8,128)}, f32[6,64,128]{2,1,0:T(8,128)}, f32[136,8,128]{2,1,0:T(8,128)}, f32[2,8,64,128]{3,2,1,0:T(8,128)}, /*index=5*/f32[8,64,128]{2,1,0:T(8,128)}) custom-call(s32[2,1,1,1024]{3,2,1,0:T(1,128)} %cells.2, f32[2,1,1,1024]{3,2,1,0:T(1,128)} %m.3, f32[2,8,64,128]{3,2,1,0:T(8,128)} %l.3, ...), custom_call_target="tpu_custom_call" | custom-call | flops 2750000128 | bytes 5406720 | tf_op jit(solution)/shard_map/pallas_call | solution.py:37
  5.3 2.2 %collective-permute-start = (f32[6,64,128]{2,1,0:T(8,128)}, f32[6,64,128]{2,1,0:T(8,128)S(1)}, u32[]{:S(2)}, u32[]{:S(2)}) collective-permute-start(f32[6,64,128]{2,1,0:T(8,128)} %get-tuple-element.34.own), channel_id=1, source_target_pairs={{0,1},{1,0},{2,3},{3,2},{4,5},{5,4},{6,7},{7,6},{8,9},{9,8},{10,11... | collective-permute-start | bytes 589832 | tf_op jit(solution)/shard_map/ppermute | solution.py:657
  7.5 5.4 %collective-permute-start.1 = (f32[86,8,128]{2,1,0:T(8,128)}, f32[86,8,128]{2,1,0:T(8,128)S(1)}, u32[]{:S(2)}, u32[]{:S(2)}) collective-permute-start(f32[86,8,128]{2,1,0:T(8,128)} %get-tuple-element.35), channel_id=1, source_target_pairs={{2,4},{3,5},{4,2},{5,3},{6,8},{7,9},{8,6},{9,7},{10,12},{11,13},{1... | collective-permute-start | bytes 1056776 | tf_op jit(solution)/shard_map/ppermute | solution.py:658
  12.8 0.8 slice.36
  13.6 1.9 %collective-permute-start.3 = (f32[6,8,128]{2,1,0:T(8,128)S(1)}, f32[6,8,128]{2,1,0:T(8,128)S(1)}, u32[]{:S(2)}, u32[]{:S(2)}) collective-permute-start(f32[6,8,128]{2,1,0:T(8,128)S(1)} %slice.36), channel_id=1, source_target_pairs={{2,5},{3,4},{4,3},{5,2},{6,9},{7,8},{8,7},{9,6},{10,13},{11,12},{1... | collective-permute-start | bytes 73736 | tf_op jit(solution)/shard_map/ppermute | solution.py:660
  15.6 1.3 %collective-permute-start.7 = (f32[136,8,128]{2,1,0:T(8,128)}, f32[136,8,128]{2,1,0:T(8,128)S(1)}, u32[]{:S(2)}, u32[]{:S(2)}) collective-permute-start(f32[136,8,128]{2,1,0:T(8,128)} %get-tuple-element.41.z_own), channel_id=1, source_target_pairs={{32,0},{64,32},{96,64},{128,96},{160,128},{192,160},{224,192},{33,... | collective-permute-start | bytes 1671176 | tf_op jit(solution)/shard_map/ppermute | solution.py:661
  17.6 2.4 %shard_map.156 = (f32[2,1,1,1024]{3,2,1,0:T(1,128)S(1)}, f32[2,8,64,128]{3,2,1,0:T(8,128)S(1)}) custom-call(s32[2,1,1,1024]{3,2,1,0:T(1,128)S(1)} %copy-done.8, f32[2,1,1,1024]{3,2,1,0:T(1,128)S(1)} %copy-done.10, f32[2,8,64,128]{3,2,1,0:T(8,128)S(1)} %copy-done.4, f32[2,1,1,1024]{3,2,1,0:T(1,128)S(1)} %copy-done.7, f32[2,1,1,1024]{3,2,1,0:T(1,128)S(1)} %copy-done.9), custom_call_target="tpu_custom_call" | custom-call | flops 2640000000 | bytes 1089536 | tf_op jit(solution)/shard_map/pallas_call | solution.py:37
  20.1 1.4 %collective-permute-done.1.bg = f32[86,8,128]{2,1,0:T(8,128)S(1)} collective-permute-done((f32[86,8,128]{2,1,0:T(8,128)}, f32[86,8,128]{2,1,0:T(8,128)S(1)}, u32[]{:S(2)}, u32[]{:S(2)}) %collective-permute-start.1) | collective-permute-done | bytes 352288 | tf_op jit(solution)/shard_map/ppermute | solution.py:658
  21.6 0.7 collective-permute-start.9
  22.3 1.3 %collective-permute-start.8 = (f32[45,8,128]{2,1,0:T(8,128)S(1)}, f32[45,8,128]{2,1,0:T(8,128)S(1)}, u32[]{:S(2)}, u32[]{:S(2)}) collective-permute-start(f32[45,8,128]{2,1,0:T(8,128)S(1)} %fusion), channel_id=1, source_target_pairs={{32,0},{96,64},{160,128},{224,192},{33,1},{97,65},{161,129},{225,1... | collective-permute-start | bytes 552968 | tf_op jit(solution)/shard_map/ppermute | solution.py:676
  23.7 5.5 %shard_map.155 = (f32[3,9,80,128]{3,2,1,0:T(8,128)S(1)}, f32[2,8,64,128]{3,2,1,0:T(8,128)S(1)}, f32[2,8,64,128]{3,2,1,0:T(8,128)S(1)}, f32[2,8,64,128]{3,2,1,0:T(8,128)S(1)}) custom-call(s32[2]{0:T(128)S(1)} %copy-done.11, f32[2,8,64,128]{3,2,1,0:T(8,128)S(1)} %copy-done.4, f32[2,8,64,128]{3,2,1,0:T(8,128)S(1)} %copy-done.5, ...), custom_call_target="tpu_custom_call" | custom-call | flops 5500000256 | bytes 7258120 | tf_op jit(solution)/shard_map/pallas_call | solution.py:37
  29.2 3.6 %collective-permute-start.5 = (f32[2,8,64,128]{3,2,1,0:T(8,128)S(1)}, f32[2,8,64,128]{3,2,1,0:T(8,128)S(1)}, u32[]{:S(2)}, u32[]{:S(2)}) collective-permute-start(f32[2,8,64,128]{3,2,1,0:T(8,128)S(1)} %get-tuple-element.38), channel_id=1, source_target_pairs={{0,32},{64,96},{128,160},{192,224},{32,0},{96,64},{160,128},{224,1... | collective-permute-start | bytes 1572872 | tf_op jit(solution)/shard_map/ppermute | solution.py:692
  32.8 0.9 collective-permute-start.6
  33.6 2.1 %collective-permute-done.8.zh_even = f32[45,8,128]{2,1,0:T(8,128)S(1)} collective-permute-done((f32[45,8,128]{2,1,0:T(8,128)S(1)}, f32[45,8,128]{2,1,0:T(8,128)S(1)}, u32[]{:S(2)}, u32[]{:S(2)}) %collective-permute-start.8) | collective-permute-done | bytes 184352 | tf_op jit(solution)/shard_map/ppermute | solution.py:676
  35.8 7.8 %shard_map.157 = (f32[8,64,128]{2,1,0:T(8,128)S(1)}, f32[8,64,128]{2,1,0:T(8,128)S(1)}, f32[8,64,128]{2,1,0:T(8,128)S(1)}, f32[8,64,128]{2,1,0:T(8,128)S(1)}, f3...) custom-call(s32[2]{0:T(128)S(1)} %copy-done.11, ...), custom_call_target="tpu_custom_call" | custom-call | flops 9900000256 | bytes 7700488 | tf_op jit(solution)/shard_map/pallas_call | solution.py:37
  43.6 0.7 collective-permute-start.11
  44.3 8.5 %collective-permute-start.10 = (f32[8,64,128]{2,1,0:T(8,128)S(1)}, f32[8,64,128]{2,1,0:T(8,128)S(1)}, u32[]{:S(2)}, u32[]{:S(2)}) collective-permute-start(f32[8,64,128]{2,1,0:T(8,128)S(1)} %get-tuple-element.46.f21), channel_id=1, source_target_pairs={{0,32},{64,96},{128,160},{192,224},{1,33},{65,97},{129,161},{193,2... | collective-permute-start | bytes 786440 | tf_op jit(solution)/shard_map/ppermute | solution.py:701
  52.8 1.0 %shard_map.158 = (f32[8,64,128]{2,1,0:T(8,128)S(1)}, f32[8,64,128]{2,1,0:T(8,128)S(1)}, f32[256,128]{1,0:T(8,128)}) custom-call(f32[2,8,64,128]{3,2,1,0:T(8,128)S(1)} %collective-permute-done.5.even, f32[2,8,64,128]{3,2,1,0:T(8,128)S(1)} %collective-permute-done.6.odd, f32[8,64,128]{2,1,0:T(8,128)S(1)} %get-tuple-element.45.rl2, ...), custom_call_target="tpu_custom_call" | custom-call | flops 440000000 | bytes 4104192 | tf_op jit(solution)/shard_map/pallas_call | solution.py:37
  53.9 15.7 %all-to-all-start = ((f32[256,1,128]{2,1,0:T(1,128)}), f32[256,1,128]{2,1,0:T(1,128)S(1)}, u32[]{:S(2)}, u32[]{:S(2)}) async-start(f32[256,1,128]{2,1,0:T(1,128)} %bitcast.3), calls=%async_computation | async-start | bytes 262144 | tf_op jit(solution)/shard_map/all_to_all | solution.py:710
  69.6 12.7 %all-to-all-done = f32[256,1,128]{2,1,0:T(1,128)S(1)} async-done(((f32[256,1,128]{2,1,0:T(1,128)}), f32[256,1,128]{2,1,0:T(1,128)S(1)}, u32[]{:S(2)}, u32[]{:S(2)}) %all-to-all-start) | async-done | bytes 131104 | tf_op jit(solution)/shard_map/all_to_all | solution.py:710
  82.3 0.9 %copy-done.13 = f32[8,64,128]{2,1,0:T(8,128)S(1)} copy-done((f32[8,64,128]{2,1,0:T(8,128)S(1)}, f32[8,64,128]{2,1,0:T(8,128)}, u32[]{:S(2)}) %copy-start.13) | copy-done | bytes 262168
  83.2 0.9 %copy-done.15 = f32[8,64,128]{2,1,0:T(8,128)S(1)} copy-done((f32[8,64,128]{2,1,0:T(8,128)S(1)}, f32[8,64,128]{2,1,0:T(8,128)}, u32[]{:S(2)}) %copy-start.15) | copy-done | bytes 262168
  84.2 0.7 copy-done.19
  84.9 2.2 %shard_map.159 = (f32[2,8,64,128]{3,2,1,0:T(8,128)}, f32[2,1,1,1024]{3,2,1,0:T(1,128)}, f32[2,8,64,128]{3,2,1,0:T(8,128)}, f32[2,8,64,128]{3,2,1,0:T(8,128)}, f3...) custom-call(f32[256,128]{1,0:T(8,128)S(1)} %bitcast.12, f32[2,8,64,128]{3,2,1,0:T(8,128)S(1)} %copy-done.5, ...), custom_call_target="tpu_custom_call" | custom-call | flops 1650000000 | bytes 5939200 | tf_op jit(solution)/shard_map/pallas_call | solution.py:37
  (60 shorter events, 0.8 us)
Async XLA Ops:
  0.6 17.0 %copy-start.4 = (f32[2,8,64,128]{3,2,1,0:T(8,128)S(1)}, f32[2,8,64,128]{3,2,1,0:T(8,128)}, u32[]{:S(2)}) copy-start(f32[2,8,64,128]{3,2,1,0:T(8,128)} %v.5) | copy-start | bytes 1572868
  0.6 17.0 %copy-start.8 = (s32[2,1,1,1024]{3,2,1,0:T(1,128)S(1)}, s32[2,1,1,1024]{3,2,1,0:T(1,128)}, u32[]{:S(2)}) copy-start(s32[2,1,1,1024]{3,2,1,0:T(1,128)} %cells.2) | copy-start | bytes 24580
  0.7 17.0 %copy-start.10 = (f32[2,1,1,1024]{3,2,1,0:T(1,128)S(1)}, f32[2,1,1,1024]{3,2,1,0:T(1,128)}, u32[]{:S(2)}) copy-start(f32[2,1,1,1024]{3,2,1,0:T(1,128)} %m.3) | copy-start | bytes 24580
  0.7 17.0 %copy-start.9 = (f32[2,1,1,1024]{3,2,1,0:T(1,128)S(1)}, f32[2,1,1,1024]{3,2,1,0:T(1,128)}, u32[]{:S(2)}) copy-start(f32[2,1,1,1024]{3,2,1,0:T(1,128)} %ov.3) | copy-start | bytes 24580
  0.7 17.0 %copy-start.7 = (f32[2,1,1,1024]{3,2,1,0:T(1,128)S(1)}, f32[2,1,1,1024]{3,2,1,0:T(1,128)}, u32[]{:S(2)}) copy-start(f32[2,1,1,1024]{3,2,1,0:T(1,128)} %dep.1) | copy-start | bytes 24580
  5.3 11.6 %collective-permute-start = (f32[6,64,128]{2,1,0:T(8,128)}, f32[6,64,128]{2,1,0:T(8,128)S(1)}, u32[]{:S(2)}, u32[]{:S(2)}) collective-permute-start(f32[6,64,128]{2,1,0:T(8,128)} %get-tuple-element.34.own), channel_id=1, source_target_pairs={{0,1},{1,0},{2,3},{3,2},{4,5},{5,4},{6,7},{7,6},{8,9},{9,8},{10,11... | collective-permute-start | bytes 589832 | tf_op jit(solution)/shard_map/ppermute | solution.py:657
  7.5 14.0 %collective-permute-start.1 = (f32[86,8,128]{2,1,0:T(8,128)}, f32[86,8,128]{2,1,0:T(8,128)S(1)}, u32[]{:S(2)}, u32[]{:S(2)}) collective-permute-start(f32[86,8,128]{2,1,0:T(8,128)} %get-tuple-element.35), channel_id=1, source_target_pairs={{2,4},{3,5},{4,2},{5,3},{6,8},{7,9},{8,6},{9,7},{10,12},{11,13},{1... | collective-permute-start | bytes 1056776 | tf_op jit(solution)/shard_map/ppermute | solution.py:658
  13.6 8.0 %collective-permute-start.3 = (f32[6,8,128]{2,1,0:T(8,128)S(1)}, f32[6,8,128]{2,1,0:T(8,128)S(1)}, u32[]{:S(2)}, u32[]{:S(2)}) collective-permute-start(f32[6,8,128]{2,1,0:T(8,128)S(1)} %slice.36), channel_id=1, source_target_pairs={{2,5},{3,4},{4,3},{5,2},{6,9},{7,8},{8,7},{9,6},{10,13},{11,12},{1... | collective-permute-start | bytes 73736 | tf_op jit(solution)/shard_map/ppermute | solution.py:660
  15.5 6.0 %collective-permute-start.2 = (f32[86,8,128]{2,1,0:T(8,128)}, f32[86,8,128]{2,1,0:T(8,128)S(1)}, u32[]{:S(2)}, u32[]{:S(2)}) collective-permute-start(f32[86,8,128]{2,1,0:T(8,128)} %get-tuple-element.36), channel_id=1, source_target_pairs={{0,2},{1,3},{2,0},{3,1},{4,6},{5,7},{6,4},{7,5},{8,10},{9,11},{10,... | collective-permute-start | bytes 1056776 | tf_op jit(solution)/shard_map/ppermute | solution.py:659
  15.6 20.2 %collective-permute-start.7 = (f32[136,8,128]{2,1,0:T(8,128)}, f32[136,8,128]{2,1,0:T(8,128)S(1)}, u32[]{:S(2)}, u32[]{:S(2)}) collective-permute-start(f32[136,8,128]{2,1,0:T(8,128)} %get-tuple-element.41.z_own), channel_id=1, source_target_pairs={{32,0},{64,32},{96,64},{128,96},{160,128},{192,160},{224,192},{33,... | collective-permute-start | bytes 1671176 | tf_op jit(solution)/shard_map/ppermute | solution.py:661
  16.9 6.7 %copy-start.1 = (f32[2,8,64,128]{3,2,1,0:T(8,128)S(1)}, f32[2,8,64,128]{3,2,1,0:T(8,128)}, u32[]{:S(2)}) copy-start(f32[2,8,64,128]{3,2,1,0:T(8,128)} %we.3) | copy-start | bytes 1572868
  17.0 6.7 %copy-start.2 = (f32[2,8,64,128]{3,2,1,0:T(8,128)S(1)}, f32[2,8,64,128]{3,2,1,0:T(8,128)}, u32[]{:S(2)}) copy-start(f32[2,8,64,128]{3,2,1,0:T(8,128)} %wn.3) | copy-start | bytes 1572868
  17.0 4.5 %collective-permute-start.4 = (f32[6,16,128]{2,1,0:T(8,128)S(1)}, f32[6,16,128]{2,1,0:T(8,128)S(1)}, u32[]{:S(2)}, u32[]{:S(2)}) collective-permute-start(f32[6,16,128]{2,1,0:T(8,128)S(1)} %pad_maximum_fusion), channel_id=1, source_target_pairs={{0,2},{1,3},{2,0},{3,1},{4,6},{5,7},{6,4},{7,5},{8,10},{9,11},{10,... | collective-permute-start | bytes 147464 | tf_op jit(solution)/shard_map/ppermute | solution.py:664
  21.6 12.0 %collective-permute-start.9 = (f32[45,8,128]{2,1,0:T(8,128)S(1)}, f32[45,8,128]{2,1,0:T(8,128)S(1)}, u32[]{:S(2)}, u32[]{:S(2)}) collective-permute-start(f32[45,8,128]{2,1,0:T(8,128)S(1)} %fusion), channel_id=1, source_target_pairs={{64,32},{128,96},{192,160},{65,33},{129,97},{193,161},{66,34},{130... | collective-permute-start | bytes 552968 | tf_op jit(solution)/shard_map/ppermute | solution.py:677
  22.3 13.5 %collective-permute-start.8 = (f32[45,8,128]{2,1,0:T(8,128)S(1)}, f32[45,8,128]{2,1,0:T(8,128)S(1)}, u32[]{:S(2)}, u32[]{:S(2)}) collective-permute-start(f32[45,8,128]{2,1,0:T(8,128)S(1)} %fusion), channel_id=1, source_target_pairs={{32,0},{96,64},{160,128},{224,192},{33,1},{97,65},{161,129},{225,1... | collective-permute-start | bytes 552968 | tf_op jit(solution)/shard_map/ppermute | solution.py:676
  29.2 23.6 %collective-permute-start.5 = (f32[2,8,64,128]{3,2,1,0:T(8,128)S(1)}, f32[2,8,64,128]{3,2,1,0:T(8,128)S(1)}, u32[]{:S(2)}, u32[]{:S(2)}) collective-permute-start(f32[2,8,64,128]{3,2,1,0:T(8,128)S(1)} %get-tuple-element.38), channel_id=1, source_target_pairs={{0,32},{64,96},{128,160},{192,224},{32,0},{96,64},{160,128},{224,1... | collective-permute-start | bytes 1572872 | tf_op jit(solution)/shard_map/ppermute | solution.py:692
  32.8 20.1 %collective-permute-start.6 = (f32[2,8,64,128]{3,2,1,0:T(8,128)S(1)}, f32[2,8,64,128]{3,2,1,0:T(8,128)S(1)}, u32[]{:S(2)}, u32[]{:S(2)}) collective-permute-start(f32[2,8,64,128]{3,2,1,0:T(8,128)S(1)} %get-tuple-element.39), channel_id=1, source_target_pairs={{32,64},{96,128},{160,192},{64,32},{128,96},{192,160},{33,65},{97,... | collective-permute-start | bytes 1572872 | tf_op jit(solution)/shard_map/ppermute | solution.py:693
  35.8 17.1 %copy-start = (f32[136,8,128]{2,1,0:T(8,128)S(1)}, f32[136,8,128]{2,1,0:T(8,128)}, u32[]{:S(2)}) copy-start(f32[136,8,128]{2,1,0:T(8,128)} %get-tuple-element.41.z_own) | copy-start | bytes 1671172
  43.6 10.3 %copy-start.12 = (f32[8,64,128]{2,1,0:T(8,128)}, f32[8,64,128]{2,1,0:T(8,128)S(1)}, u32[]{:S(2)}) copy-start(f32[8,64,128]{2,1,0:T(8,128)S(1)} %get-tuple-element.54.ql1) | copy-start | bytes 786436
  43.6 10.3 %copy-start.14 = (f32[8,64,128]{2,1,0:T(8,128)}, f32[8,64,128]{2,1,0:T(8,128)S(1)}, u32[]{:S(2)}) copy-start(f32[8,64,128]{2,1,0:T(8,128)S(1)} %get-tuple-element.56.qv1_far) | copy-start | bytes 786436
  43.6 10.3 %copy-start.18 = (f32[2,1,1,1024]{3,2,1,0:T(1,128)}, f32[2,1,1,1024]{3,2,1,0:T(1,128)S(1)}, u32[]{:S(2)}) copy-start(f32[2,1,1,1024]{3,2,1,0:T(1,128)S(1)} %get-tuple-element.57.qm_far) | copy-start | bytes 24580
  43.6 26.0 %collective-permute-start.11 = (f32[8,64,128]{2,1,0:T(8,128)S(1)}, f32[8,64,128]{2,1,0:T(8,128)S(1)}, u32[]{:S(2)}, u32[]{:S(2)}) collective-permute-start(f32[8,64,128]{2,1,0:T(8,128)S(1)} %get-tuple-element.46.f21), channel_id=1, source_target_pairs={{32,64},{96,128},{160,192},{33,65},{97,129},{161,193},{34,66},{98,... | collective-permute-start | bytes 786440 | tf_op jit(solution)/shard_map/ppermute | solution.py:702
  44.3 25.3 %collective-permute-start.10 = (f32[8,64,128]{2,1,0:T(8,128)S(1)}, f32[8,64,128]{2,1,0:T(8,128)S(1)}, u32[]{:S(2)}, u32[]{:S(2)}) collective-permute-start(f32[8,64,128]{2,1,0:T(8,128)S(1)} %get-tuple-element.46.f21), channel_id=1, source_target_pairs={{0,32},{64,96},{128,160},{192,224},{1,33},{65,97},{129,161},{193,2... | collective-permute-start | bytes 786440 | tf_op jit(solution)/shard_map/ppermute | solution.py:701
  53.9 28.4 %all-to-all-start = ((f32[256,1,128]{2,1,0:T(1,128)}), f32[256,1,128]{2,1,0:T(1,128)S(1)}, u32[]{:S(2)}, u32[]{:S(2)}) async-start(f32[256,1,128]{2,1,0:T(1,128)} %bitcast.3), calls=%async_computation | async-start | bytes 262144 | tf_op jit(solution)/shard_map/all_to_all | solution.py:710
  (9 other events, 42.5 us)

commit v2 on v0

--- a/solution.py
+++ b/solution.py
@@ -26,7 +26,7 @@
 FAR = pl.BlockSpec(memory_space=pltpu.HBM)
 
 
-def call(body, outs, ins, scratch=(), micros=1.0, fetched=(), limit=VMEM_LIMIT):
+def call(body, outs, ins, scratch=(), micros=1.0, fetched=(), written=(), limit=VMEM_LIMIT):
     shapes = [jax.ShapeDtypeStruct(s, F32) for s in outs]
     nbytes = 4 * sum(int(a.size) for a in ins) + 4 * sum(
         functools.reduce(lambda a, b: a * b, s, 1) for s in outs
@@ -38,7 +38,7 @@
         body,
         out_shape=shapes,
         in_specs=in_specs,
-        out_specs=[VM] * len(shapes),
+        out_specs=[FAR if i in written else VM for i in range(len(shapes))],
         scratch_shapes=list(scratch),
         compiler_params=pltpu.CompilerParams(vmem_limit_bytes=limit),
         cost_estimate=pl.CostEstimate(
@@ -99,7 +99,7 @@
 
 def pack_kernel(
     cells_h, m_h, l_h, f_h, mv_h, v_h, we_h, wn_h,
-    b_out, a_out, by_out, strip_out, z_out, lh_out, g1_out,
+    b_out, a_out, strip_out, z_out, lh_out, g1_out,
     g_s, cells, m, l, f, mv, v, we, wn, sems,
 ):
     far = (cells_h, m_h, l_h, f_h, mv_h, v_h, we_h, wn_h)
@@ -160,7 +160,6 @@
                 g_edge = pltpu.roll(g_s[s, z, edge, :], 4, 0)
                 out[(8 + s) * LEV + z] = jnp.where(keep, lh_edge, g_edge)
         out[pl.ds(10 * LEV, 6)] = strip_out[:, edge, :]
-    by_out[...] = b_out[10 * LEV :]
 
 
 def obs_kernel(cells, m, v, dep, ov, rm_out, h2_out):
@@ -541,10 +540,14 @@
 
 
 def dots_kernel(
-    even, odd, rl2, f21, b20, z_own, h2, rv0, dots_in, rl0_out, qv0_out, send_out
+    even, odd, rl2, f21, b20, z_own, h2, rv0, dots_in, rl1, rv1, qv1, ql1, qm, rm, m,
+    keep_out, obs_out, send_out,
 ):
     follows = jnp.where(lax.axis_index("tm") == lax.axis_size("tm") - 1, 0.0, 1.0)
     starts = jnp.where(lax.axis_index("tm") == 0, 1.0, 0.0)
+    obs_out[0:2] = rm[...]
+    obs_out[2:4] = qm[...]
+    obs_out[4:6] = m[...]
     cross, square = dots_in[0], dots_in[1]
     is_odd = lax.axis_index("tm") % 2 == 1
 
@@ -555,8 +558,8 @@
         rl0 = z_own[64 + 8 * z : 72 + 8 * z].reshape(CX, CY) + jnp.where(is_odd, even[0, z], odd[0, z])
         rv = rv0[0, z]
         qv = rl0 - b20[z] + h2[0, z]
-        rl0_out[z] = rl0
-        qv0_out[z] = qv
+        for i, kept in enumerate((rl0, rl1[z], rv1[z], qv, qv1[z], ql1[z])):
+            keep_out[i, z] = kept
         ql = (rv0[1, z] * rl0 + rv) * starts
         rl2z = rl2[z]
         next_mv = jnp.where(is_odd, odd[1, z], even[1, z])
@@ -572,7 +575,7 @@
 
 
 def last_kernel(
-    sums, l, m, v, rl0, rl1, rv0, rv1, rm, z_f2, ql1, qv0, qv1, qm,
+    sums, l, v, rv0, z_f2, keep, obs_pair,
     l_out, m_out, v_out, a_out, b_out, c_out,
 ):
     total = jnp.sum(sums[...], 0, keepdims=True)
@@ -580,18 +583,20 @@
     cross = jnp.sum(jnp.where(lane == 0, total, 0.0), 1, keepdims=True)
     square = jnp.sum(jnp.where(lane == 1, total, 0.0), 1, keepdims=True)
     alpha = cross / (square + 1e-06)
-    m_out[...] = m[...] + alpha * rm[...]
-    b_out[...] = rm[...] - alpha * qm[...]
-    for z in range(LEV):
-        ql0 = rv0[1, z] * rl0[z] + rv0[0, z] - z_f2[z]
-        l_out[0, z] = l[0, z] + alpha * rl0[z]
-        l_out[1, z] = l[1, z] + alpha * rl1[z]
+    rm, qm = obs_pair[0:2], obs_pair[2:4]
+    m_out[...] = obs_pair[4:6] + alpha * rm
+    b_out[...] = rm - alpha * qm
+    for z in range(LEV):
+        rl0, rl1, rv1, qv0, qv1, ql1 = (keep[i, z] for i in range(6))
+        ql0 = rv0[1, z] * rl0 + rv0[0, z] - z_f2[z]
+        l_out[0, z] = l[0, z] + alpha * rl0
+        l_out[1, z] = l[1, z] + alpha * rl1
         v_out[0, z] = v[0, z] + alpha * rv0[0, z]
-        v_out[1, z] = v[1, z] + alpha * rv1[z]
-        a_out[0, z] = rl0[z] - alpha * ql0
-        a_out[1, z] = rl1[z] - alpha * ql1[z]
-        c_out[0, z] = rv0[0, z] - alpha * qv0[z]
-        c_out[1, z] = rv1[z] - alpha * qv1[z]
+        v_out[1, z] = v[1, z] + alpha * rv1
+        a_out[0, z] = rl0 - alpha * ql0
+        a_out[1, z] = rl1 - alpha * ql1
+        c_out[0, z] = rv0[0, z] - alpha * qv0
+        c_out[1, z] = rv1 - alpha * qv1
 
 
 def shards(sizes, l4, m4, v4, f4, d4, mv4, ov4, we4, wn4, cells4, counts):
@@ -617,9 +622,9 @@
     edge = 10 * LEV
 
     fields = pltpu.VMEM((2,) + tile, F32)
-    b_send, a_send, by_send, own, z_send, lh, g1 = call(
+    b_send, a_send, own, z_send, lh, g1 = call(
         pack_kernel,
-        [(NBLOCKS, 8, CY)] * 2 + [(6, 8, CY), (6, CX, CY), (136, 8, CY), (2,) + tile, tile],
+        [(NBLOCKS, 8, CY)] * 2 + [(6, CX, CY), (136, 8, CY), (2,) + tile, tile],
         [cells4, m4, l4, f4, mv4, v4, we4, wn4],
         [fields, pltpu.VMEM(obs, jnp.int32), pltpu.VMEM(obs, F32)]
         + [fields] * 6
@@ -631,7 +636,7 @@
     got = lax.ppermute(own, axes, plane(lambda i: i, True))
     bg = lax.ppermute(b_send, axes, plane(pair_b, False))
     ag = lax.ppermute(a_send, axes, plane(lambda i: i ^ 1, False))
-    by = lax.ppermute(by_send, axes, plane(pair_b, True))
+    by = lax.ppermute(b_send[edge:], axes, plane(pair_b, True))
     zt = lax.ppermute(z_send, "tm", down)
     ay_send = jnp.concatenate([got[:, :8], got[:, CX - 8 :]], 1)
     ay_send, late_cells = lax.optimization_barrier((ay_send, cells4))
@@ -673,17 +678,17 @@
     )
     z_f2 = lax.ppermute(f21, "tm", up)
     n = ntm * ngx * ngy
-    rl0, qv0, send = call(
+    keep, obs_pair, send = call(
         dots_kernel,
-        [tile, tile, (n, CY)],
-        [even, odd, rl2, f21, b20, z_send, h2, rv0, dots],
+        [(6,) + tile, (6,) + obs[1:], (n, CY)],
+        [even, odd, rl2, f21, b20, z_send, h2, rv0, dots, rl1, rv1, qv1, ql1, qm, rm, m4],
         micros=0.4,
     )
     sums = lax.all_to_all(send, ("tm", "gx", "gy"), 0, 0, tiled=True)
     return call(
         last_kernel,
         [l4.shape, obs, l4.shape, l4.shape, obs, l4.shape],
-        [sums, l4, m4, v4, rl0, rl1, rv0, rv1, rm, z_f2, ql1, qv0, qv1, qm],
+        [sums, l4, v4, rv0, z_f2, keep, obs_pair],
         micros=1.5,
     )
 

time: 80.2 us -> 82.6 us (1.030)
  Pallas kernels: 24.5 us -> 20.5 us
  starting transfers between devices: 35.4 us -> 39 us
  waiting for transfers between devices: 17.8 us -> 19.4 us
    ppermute x1, waiting for transfers between devices: 1.28 us -> 5.26 us  [shards(): zh = lax.ppermute(z_edges, 'tm', down)]
    pallas_call x6, Pallas kernels: 24.5 us -> 20.5 us  [call(): pl.pallas_call(body, out_shape=shapes, in_specs=in_specs, out_specs=[FAR...]
    ppermute x1, starting transfers between devices: 4.63 us -> 1.91 us  [shards(): by = lax.ppermute(b_send[edge:], axes, plane(pair_b, True))]
    ppermute x1, starting transfers between devices: 2.64 us -> 5.36 us  [shards(): bg = lax.ppermute(b_send, axes, plane(pair_b, False))]
    ppermute x1, waiting for transfers between devices: 3.78 us -> 1.43 us  [shards(): bg = lax.ppermute(b_send, axes, plane(pair_b, False))]
    all_to_all x1, starting transfers between devices: 13.9 us -> 15.6 us  [shards(): sums = lax.all_to_all(send, ('tm', 'gx', 'gy'), 0, 0, tiled=True)]
    ppermute x1, starting transfers between devices: 5.58 us -> 7.1 us  [shards(): z_f2 = lax.ppermute(f21, 'tm', up)]
    unnamed x44 -> x40, local copies, waits for them, and re-layouts: 1.76 us -> 1.45 us
  transfers between devices with their start and end apart: 11 -> 11, of which waited for: 3 -> 3; matrix products, arithmetic and copies ran while one was open for 0% -> 1% of each run, Pallas kernels for 23% -> 16%
where the time goes in v2:
time: 82.6 us; the launch traced here: 82.2 us
  starting transfers between devices  39 us (47%)
  Pallas kernels  20.5 us (25%)
  waiting for transfers between devices  19.4 us (23%)
  local copies, waits for them, and re-layouts  2.21 us (3%)
  between operations  1.01 us (1%)
    pallas_call x6, Pallas kernels, call(): pl.pallas_call(body, out_shape=shapes, in_specs=in_specs, out_specs=[FAR...  20.5 us
    all_to_all x1, starting transfers between devices, shards(): sums = lax.all_to_all(send, ('tm', 'gx', 'gy'), 0, 0, tiled=True)  15.6 us
    all_to_all x1, waiting for transfers between devices, shards(): sums = lax.all_to_all(send, ('tm', 'gx', 'gy'), 0, 0, tiled=True)  12.7 us
    ppermute x1, starting transfers between devices, shards(): z_f2 = lax.ppermute(f21, 'tm', up)  7.1 us
    ppermute x1, starting transfers between devices, shards(): bg = lax.ppermute(b_send, axes, plane(pair_b, False))  5.36 us
    ppermute x1, waiting for transfers between devices, shards(): zh = lax.ppermute(z_edges, 'tm', down)  5.26 us
    ppermute x1, starting transfers between devices, shards(): even = lax.ppermute(even_send, 'tm', swap(0))  2.76 us
    ppermute x1, starting transfers between devices, shards(): got = lax.ppermute(own, axes, plane(lambda i: i, True))  2.21 us
  transfers between devices with their start and end apart: 11, of which 3 were waited for; matrix products, arithmetic and copies ran while one was open for 1% of the time, Pallas kernels for 16%

profile of v2, /device:TPU:1, one launch (start us, length us, event | category | flops | bytes accessed | tf_op | source)
XLA Modules:
  0.0 82.2 jit_solution(7195602541705706516)
XLA Ops:
  0.7 4.6 %shard_map.154 = (f32[86,8,128]{2,1,0:T(8,128)}, f32[86,8,128]{2,1,0:T(8,128)}, f32[6,64,128]{2,1,0:T(8,128)}, f32[136,8,128]{2,1,0:T(8,128)}, f32[2,8,64,128]{3,2,1,0:T(8,128)}, /*index=5*/f32[8,64,128]{2,1,0:T(8,128)}) custom-call(s32[2,1,1,1024]{3,2,1,0:T(1,128)} %cells.2, f32[2,1,1,1024]{3,2,1,0:T(1,128)} %m.3, f32[2,8,64,128]{3,2,1,0:T(8,128)} %l.3, ...), custom_call_target="tpu_custom_call" | custom-call | flops 2750000128 | bytes 5406720 | tf_op jit(solution)/shard_map/pallas_call | solution.py:37
  5.3 2.2 %collective-permute-start = (f32[6,64,128]{2,1,0:T(8,128)}, f32[6,64,128]{2,1,0:T(8,128)S(1)}, u32[]{:S(2)}, u32[]{:S(2)}) collective-permute-start(f32[6,64,128]{2,1,0:T(8,128)} %get-tuple-element.34.own), channel_id=1, source_target_pairs={{0,1},{1,0},{2,3},{3,2},{4,5},{5,4},{6,7},{7,6},{8,9},{9,8},{10,11... | collective-permute-start | bytes 589832 | tf_op jit(solution)/shard_map/ppermute | solution.py:636
  7.5 5.4 %collective-permute-start.1 = (f32[86,8,128]{2,1,0:T(8,128)}, f32[86,8,128]{2,1,0:T(8,128)S(1)}, u32[]{:S(2)}, u32[]{:S(2)}) collective-permute-start(f32[86,8,128]{2,1,0:T(8,128)} %get-tuple-element.35), channel_id=1, source_target_pairs={{2,4},{3,5},{4,2},{5,3},{6,8},{7,9},{8,6},{9,7},{10,12},{11,13},{1... | collective-permute-start | bytes 1056776 | tf_op jit(solution)/shard_map/ppermute | solution.py:637
  12.8 0.8 slice.36
  13.6 1.9 %collective-permute-start.3 = (f32[6,8,128]{2,1,0:T(8,128)S(1)}, f32[6,8,128]{2,1,0:T(8,128)S(1)}, u32[]{:S(2)}, u32[]{:S(2)}) collective-permute-start(f32[6,8,128]{2,1,0:T(8,128)S(1)} %slice.36), channel_id=1, source_target_pairs={{2,5},{3,4},{4,3},{5,2},{6,9},{7,8},{8,7},{9,6},{10,13},{11,12},{1... | collective-permute-start | bytes 73736 | tf_op jit(solution)/shard_map/ppermute | solution.py:639
  15.5 0.1 collective-permute-start.2
  15.6 1.3 %collective-permute-start.7 = (f32[136,8,128]{2,1,0:T(8,128)}, f32[136,8,128]{2,1,0:T(8,128)S(1)}, u32[]{:S(2)}, u32[]{:S(2)}) collective-permute-start(f32[136,8,128]{2,1,0:T(8,128)} %get-tuple-element.41.z_own), channel_id=1, source_target_pairs={{32,0},{64,32},{96,64},{128,96},{160,128},{192,160},{224,192},{33,... | collective-permute-start | bytes 1671176 | tf_op jit(solution)/shard_map/ppermute | solution.py:640
  17.0 0.0 copy-start.2
  17.0 0.6 collective-permute-start.4
  17.6 2.4 %shard_map.156 = (f32[2,1,1,1024]{3,2,1,0:T(1,128)S(1)}, f32[2,8,64,128]{3,2,1,0:T(8,128)S(1)}) custom-call(s32[2,1,1,1024]{3,2,1,0:T(1,128)S(1)} %copy-done.11, f32[2,1,1,1024]{3,2,1,0:T(1,128)S(1)} %copy-done.1, f32[2,8,64,128]{3,2,1,0:T(8,128)S(1)} %copy-done.5, f32[2,1,1,1024]{3,2,1,0:T(1,128)S(1)} %copy-done.10, f32[2,1,1,1024]{3,2,1,0:T(1,128)S(1)} %copy-done.12), custom_call_target="tpu_custom_call" | custom-call | flops 2640000000 | bytes 1089536 | tf_op jit(solution)/shard_map/pallas_call | solution.py:37
  20.1 1.4 %collective-permute-done.1.bg = f32[86,8,128]{2,1,0:T(8,128)S(1)} collective-permute-done((f32[86,8,128]{2,1,0:T(8,128)}, f32[86,8,128]{2,1,0:T(8,128)S(1)}, u32[]{:S(2)}, u32[]{:S(2)}) %collective-permute-start.1) | collective-permute-done | bytes 352288 | tf_op jit(solution)/shard_map/ppermute | solution.py:637
  21.6 1.3 %collective-permute-start.8 = (f32[45,8,128]{2,1,0:T(8,128)S(1)}, f32[45,8,128]{2,1,0:T(8,128)S(1)}, u32[]{:S(2)}, u32[]{:S(2)}) collective-permute-start(f32[45,8,128]{2,1,0:T(8,128)S(1)} %fusion), channel_id=1, source_target_pairs={{32,0},{64,32},{96,64},{128,96},{160,128},{192,160},{224,192},{33,... | collective-permute-start | bytes 552968 | tf_op jit(solution)/shard_map/ppermute | solution.py:655
  23.0 3.9 %shard_map.155 = (f32[3,9,80,128]{3,2,1,0:T(8,128)S(1)}, f32[2,8,64,128]{3,2,1,0:T(8,128)S(1)}, f32[2,8,64,128]{3,2,1,0:T(8,128)S(1)}, f32[2,8,64,128]{3,2,1,0:T(8,128)S(1)}) custom-call(s32[2]{0:T(128)S(1)} %copy-done.13, f32[2,8,64,128]{3,2,1,0:T(8,128)S(1)} %copy-done.5, f32[2,8,64,128]{3,2,1,0:T(8,128)S(1)} %copy-done.6, ...), custom_call_target="tpu_custom_call" | custom-call | flops 5500000256 | bytes 7258120 | tf_op jit(solution)/shard_map/pallas_call | solution.py:37
  26.9 2.8 %collective-permute-start.5 = (f32[2,8,64,128]{3,2,1,0:T(8,128)S(1)}, f32[2,8,64,128]{3,2,1,0:T(8,128)S(1)}, u32[]{:S(2)}, u32[]{:S(2)}) collective-permute-start(f32[2,8,64,128]{3,2,1,0:T(8,128)S(1)} %get-tuple-element.38), channel_id=1, source_target_pairs={{0,32},{64,96},{128,160},{192,224},{32,0},{96,64},{160,128},{224,1... | collective-permute-start | bytes 1572872 | tf_op jit(solution)/shard_map/ppermute | solution.py:670
  29.6 0.9 %collective-permute-start.6 = (f32[2,8,64,128]{3,2,1,0:T(8,128)S(1)}, f32[2,8,64,128]{3,2,1,0:T(8,128)S(1)}, u32[]{:S(2)}, u32[]{:S(2)}) collective-permute-start(f32[2,8,64,128]{3,2,1,0:T(8,128)S(1)} %get-tuple-element.39), channel_id=1, source_target_pairs={{32,64},{96,128},{160,192},{64,32},{128,96},{192,160},{33,65},{97,... | collective-permute-start | bytes 1572872 | tf_op jit(solution)/shard_map/ppermute | solution.py:671
  30.5 5.3 %collective-permute-done.8.zh = f32[45,8,128]{2,1,0:T(8,128)S(1)} collective-permute-done((f32[45,8,128]{2,1,0:T(8,128)S(1)}, f32[45,8,128]{2,1,0:T(8,128)S(1)}, u32[]{:S(2)}, u32[]{:S(2)}) %collective-permute-start.8) | collective-permute-done | bytes 184352 | tf_op jit(solution)/shard_map/ppermute | solution.py:655
  35.8 6.2 %shard_map.157 = (f32[8,64,128]{2,1,0:T(8,128)S(1)}, f32[8,64,128]{2,1,0:T(8,128)S(1)}, f32[8,64,128]{2,1,0:T(8,128)S(1)}, f32[8,64,128]{2,1,0:T(8,128)S(1)}, f3...) custom-call(s32[2]{0:T(128)S(1)} %copy-done.13, ...), custom_call_target="tpu_custom_call" | custom-call | flops 9900000256 | bytes 7516168 | tf_op jit(solution)/shard_map/pallas_call | solution.py:37
  42.0 7.1 %collective-permute-start.9 = (f32[8,64,128]{2,1,0:T(8,128)S(1)}, f32[8,64,128]{2,1,0:T(8,128)}, u32[]{:S(2)}, u32[]{:S(2)}) collective-permute-start(f32[8,64,128]{2,1,0:T(8,128)S(1)} %get-tuple-element.46.f21), channel_id=1, source_target_pairs={{0,32},{32,64},{64,96},{96,128},{128,160},{160,192},{192,224},{1,3... | collective-permute-start | bytes 786440 | tf_op jit(solution)/shard_map/ppermute | solution.py:679
  49.1 1.0 %shard_map.158 = (f32[6,8,64,128]{3,2,1,0:T(8,128)S(1)}, f32[6,1,1,1024]{3,2,1,0:T(1,128)S(1)}, f32[256,128]{1,0:T(8,128)}) custom-call(f32[2,8,64,128]{3,2,1,0:T(8,128)S(1)} %collective-permute-done.5.even, f32[2,8,64,128]{3,2,1,0:T(8,128)S(1)} %collective-permute-done.6.odd, f32[8,64,128]{2,1,0:T(8,128)S(1)} %get-tuple-element.45.rl2, ...), custom_call_target="tpu_custom_call" | custom-call | flops 440000000 | bytes 6250496 | tf_op jit(solution)/shard_map/pallas_call | solution.py:37
  50.1 0.6 copy-done.8
  50.7 15.6 %all-to-all-start = ((f32[256,1,128]{2,1,0:T(1,128)}), f32[256,1,128]{2,1,0:T(1,128)S(1)}, u32[]{:S(2)}, u32[]{:S(2)}) async-start(f32[256,1,128]{2,1,0:T(1,128)} %bitcast.3), calls=%async_computation | async-start | bytes 262144 | tf_op jit(solution)/shard_map/all_to_all | solution.py:687
  66.3 12.7 %all-to-all-done = f32[256,1,128]{2,1,0:T(1,128)S(1)} async-done(((f32[256,1,128]{2,1,0:T(1,128)}), f32[256,1,128]{2,1,0:T(1,128)S(1)}, u32[]{:S(2)}, u32[]{:S(2)}) %all-to-all-start) | async-done | bytes 131104 | tf_op jit(solution)/shard_map/all_to_all | solution.py:687
  79.0 0.7 copy-done.9
  79.7 2.4 %shard_map.159 = (f32[2,8,64,128]{3,2,1,0:T(8,128)}, f32[2,1,1,1024]{3,2,1,0:T(1,128)}, f32[2,8,64,128]{3,2,1,0:T(8,128)}, f32[2,8,64,128]{3,2,1,0:T(8,128)}, f3...) custom-call(f32[256,128]{1,0:T(8,128)S(1)} %bitcast.12, f32[2,8,64,128]{3,2,1,0:T(8,128)S(1)} %copy-done.6, ...), custom_call_target="tpu_custom_call" | custom-call | flops 1650000000 | bytes 5677056 | tf_op jit(solution)/shard_map/pallas_call | solution.py:37
  (48 shorter events, 0.1 us)
Async XLA Ops:
  0.6 17.0 %copy-start.5 = (f32[2,8,64,128]{3,2,1,0:T(8,128)S(1)}, f32[2,8,64,128]{3,2,1,0:T(8,128)}, u32[]{:S(2)}) copy-start(f32[2,8,64,128]{3,2,1,0:T(8,128)} %v.5) | copy-start | bytes 1572868
  0.6 17.0 %copy-start.11 = (s32[2,1,1,1024]{3,2,1,0:T(1,128)S(1)}, s32[2,1,1,1024]{3,2,1,0:T(1,128)}, u32[]{:S(2)}) copy-start(s32[2,1,1,1024]{3,2,1,0:T(1,128)} %cells.2) | copy-start | bytes 24580
  0.7 17.0 %copy-start.1 = (f32[2,1,1,1024]{3,2,1,0:T(1,128)S(1)}, f32[2,1,1,1024]{3,2,1,0:T(1,128)}, u32[]{:S(2)}) copy-start(f32[2,1,1,1024]{3,2,1,0:T(1,128)} %m.3) | copy-start | bytes 24580
  0.7 17.0 %copy-start.12 = (f32[2,1,1,1024]{3,2,1,0:T(1,128)S(1)}, f32[2,1,1,1024]{3,2,1,0:T(1,128)}, u32[]{:S(2)}) copy-start(f32[2,1,1,1024]{3,2,1,0:T(1,128)} %ov.3) | copy-start | bytes 24580
  0.7 17.0 %copy-start.10 = (f32[2,1,1,1024]{3,2,1,0:T(1,128)S(1)}, f32[2,1,1,1024]{3,2,1,0:T(1,128)}, u32[]{:S(2)}) copy-start(f32[2,1,1,1024]{3,2,1,0:T(1,128)} %dep.1) | copy-start | bytes 24580
  5.3 11.6 %collective-permute-start = (f32[6,64,128]{2,1,0:T(8,128)}, f32[6,64,128]{2,1,0:T(8,128)S(1)}, u32[]{:S(2)}, u32[]{:S(2)}) collective-permute-start(f32[6,64,128]{2,1,0:T(8,128)} %get-tuple-element.34.own), channel_id=1, source_target_pairs={{0,1},{1,0},{2,3},{3,2},{4,5},{5,4},{6,7},{7,6},{8,9},{9,8},{10,11... | collective-permute-start | bytes 589832 | tf_op jit(solution)/shard_map/ppermute | solution.py:636
  7.5 14.0 %collective-permute-start.1 = (f32[86,8,128]{2,1,0:T(8,128)}, f32[86,8,128]{2,1,0:T(8,128)S(1)}, u32[]{:S(2)}, u32[]{:S(2)}) collective-permute-start(f32[86,8,128]{2,1,0:T(8,128)} %get-tuple-element.35), channel_id=1, source_target_pairs={{2,4},{3,5},{4,2},{5,3},{6,8},{7,9},{8,6},{9,7},{10,12},{11,13},{1... | collective-permute-start | bytes 1056776 | tf_op jit(solution)/shard_map/ppermute | solution.py:637
  13.6 8.0 %collective-permute-start.3 = (f32[6,8,128]{2,1,0:T(8,128)S(1)}, f32[6,8,128]{2,1,0:T(8,128)S(1)}, u32[]{:S(2)}, u32[]{:S(2)}) collective-permute-start(f32[6,8,128]{2,1,0:T(8,128)S(1)} %slice.36), channel_id=1, source_target_pairs={{2,5},{3,4},{4,3},{5,2},{6,9},{7,8},{8,7},{9,6},{10,13},{11,12},{1... | collective-permute-start | bytes 73736 | tf_op jit(solution)/shard_map/ppermute | solution.py:639
  15.5 6.0 %collective-permute-start.2 = (f32[86,8,128]{2,1,0:T(8,128)}, f32[86,8,128]{2,1,0:T(8,128)S(1)}, u32[]{:S(2)}, u32[]{:S(2)}) collective-permute-start(f32[86,8,128]{2,1,0:T(8,128)} %get-tuple-element.36), channel_id=1, source_target_pairs={{0,2},{1,3},{2,0},{3,1},{4,6},{5,7},{6,4},{7,5},{8,10},{9,11},{10,... | collective-permute-start | bytes 1056776 | tf_op jit(solution)/shard_map/ppermute | solution.py:638
  15.6 20.2 %collective-permute-start.7 = (f32[136,8,128]{2,1,0:T(8,128)}, f32[136,8,128]{2,1,0:T(8,128)S(1)}, u32[]{:S(2)}, u32[]{:S(2)}) collective-permute-start(f32[136,8,128]{2,1,0:T(8,128)} %get-tuple-element.41.z_own), channel_id=1, source_target_pairs={{32,0},{64,32},{96,64},{128,96},{160,128},{192,160},{224,192},{33,... | collective-permute-start | bytes 1671176 | tf_op jit(solution)/shard_map/ppermute | solution.py:640
  17.0 6.0 %copy-start.2 = (f32[2,8,64,128]{3,2,1,0:T(8,128)S(1)}, f32[2,8,64,128]{3,2,1,0:T(8,128)}, u32[]{:S(2)}) copy-start(f32[2,8,64,128]{3,2,1,0:T(8,128)} %we.3) | copy-start | bytes 1572868
  17.0 6.0 %copy-start.3 = (f32[2,8,64,128]{3,2,1,0:T(8,128)S(1)}, f32[2,8,64,128]{3,2,1,0:T(8,128)}, u32[]{:S(2)}) copy-start(f32[2,8,64,128]{3,2,1,0:T(8,128)} %wn.3) | copy-start | bytes 1572868
  17.0 6.0 %copy-start.4 = (f32[2,8,64,128]{3,2,1,0:T(8,128)S(1)}, f32[2,8,64,128]{3,2,1,0:T(8,128)}, u32[]{:S(2)}) copy-start(f32[2,8,64,128]{3,2,1,0:T(8,128)} %mv.3) | copy-start | bytes 1572868
  17.0 6.0 %copy-start.6 = (f32[2,8,64,128]{3,2,1,0:T(8,128)S(1)}, f32[2,8,64,128]{3,2,1,0:T(8,128)}, u32[]{:S(2)}) copy-start(f32[2,8,64,128]{3,2,1,0:T(8,128)} %l.3) | copy-start | bytes 1572868
  17.0 6.0 %copy-start.7 = (f32[6,64,128]{2,1,0:T(8,128)S(1)}, f32[6,64,128]{2,1,0:T(8,128)}, u32[]{:S(2)}) copy-start(f32[6,64,128]{2,1,0:T(8,128)} %get-tuple-element.34.own) | copy-start | bytes 589828
  17.0 6.0 %copy-start.13 = (s32[2]{0:T(128)S(1)}, s32[2]{0:T(128)}, u32[]{:S(2)}) copy-start(s32[2]{0:T(128)} %counts.3) | copy-start | bytes 28
  17.0 6.0 %copy-start.14 = (f32[2,8,64,128]{3,2,1,0:T(8,128)S(1)}, f32[2,8,64,128]{3,2,1,0:T(8,128)}, u32[]{:S(2)}) copy-start(f32[2,8,64,128]{3,2,1,0:T(8,128)} %get-tuple-element.32.lh) | copy-start | bytes 1572868
  17.0 4.5 %collective-permute-start.4 = (f32[6,16,128]{2,1,0:T(8,128)S(1)}, f32[6,16,128]{2,1,0:T(8,128)S(1)}, u32[]{:S(2)}, u32[]{:S(2)}) collective-permute-start(f32[6,16,128]{2,1,0:T(8,128)S(1)} %pad_maximum_fusion), channel_id=1, source_target_pairs={{0,2},{1,3},{2,0},{3,1},{4,6},{5,7},{6,4},{7,5},{8,10},{9,11},{10,... | collective-permute-start | bytes 147464 | tf_op jit(solution)/shard_map/ppermute | solution.py:643
  21.6 14.2 %collective-permute-start.8 = (f32[45,8,128]{2,1,0:T(8,128)S(1)}, f32[45,8,128]{2,1,0:T(8,128)S(1)}, u32[]{:S(2)}, u32[]{:S(2)}) collective-permute-start(f32[45,8,128]{2,1,0:T(8,128)S(1)} %fusion), channel_id=1, source_target_pairs={{32,0},{64,32},{96,64},{128,96},{160,128},{192,160},{224,192},{33,... | collective-permute-start | bytes 552968 | tf_op jit(solution)/shard_map/ppermute | solution.py:655
  26.9 22.2 %collective-permute-start.5 = (f32[2,8,64,128]{3,2,1,0:T(8,128)S(1)}, f32[2,8,64,128]{3,2,1,0:T(8,128)S(1)}, u32[]{:S(2)}, u32[]{:S(2)}) collective-permute-start(f32[2,8,64,128]{3,2,1,0:T(8,128)S(1)} %get-tuple-element.38), channel_id=1, source_target_pairs={{0,32},{64,96},{128,160},{192,224},{32,0},{96,64},{160,128},{224,1... | collective-permute-start | bytes 1572872 | tf_op jit(solution)/shard_map/ppermute | solution.py:670
  29.6 19.4 %collective-permute-start.6 = (f32[2,8,64,128]{3,2,1,0:T(8,128)S(1)}, f32[2,8,64,128]{3,2,1,0:T(8,128)S(1)}, u32[]{:S(2)}, u32[]{:S(2)}) collective-permute-start(f32[2,8,64,128]{3,2,1,0:T(8,128)S(1)} %get-tuple-element.39), channel_id=1, source_target_pairs={{32,64},{96,128},{160,192},{64,32},{128,96},{192,160},{33,65},{97,... | collective-permute-start | bytes 1572872 | tf_op jit(solution)/shard_map/ppermute | solution.py:671
  35.8 13.3 %copy-start = (f32[136,8,128]{2,1,0:T(8,128)S(1)}, f32[136,8,128]{2,1,0:T(8,128)}, u32[]{:S(2)}) copy-start(f32[136,8,128]{2,1,0:T(8,128)} %get-tuple-element.41.z_own) | copy-start | bytes 1671172
  42.0 24.3 %collective-permute-start.9 = (f32[8,64,128]{2,1,0:T(8,128)S(1)}, f32[8,64,128]{2,1,0:T(8,128)}, u32[]{:S(2)}, u32[]{:S(2)}) collective-permute-start(f32[8,64,128]{2,1,0:T(8,128)S(1)} %get-tuple-element.46.f21), channel_id=1, source_target_pairs={{0,32},{32,64},{64,96},{96,128},{128,160},{160,192},{192,224},{1,3... | collective-permute-start | bytes 786440 | tf_op jit(solution)/shard_map/ppermute | solution.py:679
  50.7 28.3 %all-to-all-start = ((f32[256,1,128]{2,1,0:T(1,128)}), f32[256,1,128]{2,1,0:T(1,128)S(1)}, u32[]{:S(2)}, u32[]{:S(2)}) async-start(f32[256,1,128]{2,1,0:T(1,128)} %bitcast.3), calls=%async_computation | async-start | bytes 262144 | tf_op jit(solution)/shard_map/all_to_all | solution.py:687
  (3 other events, 7.3 us)

commit v3 on v2

--- a/solution.py
+++ b/solution.py
@@ -225,10 +225,24 @@
 DOWN = slice(TOP - 1, TOP + EXT - 1)
 
 
-def injected(strip, gy):
-    lane = iota((EXT, CY), 1) & 15
-    moved = jnp.where(gy == 0, pltpu.roll(strip, 119, 1), pltpu.roll(strip, 121, 1))
-    return jnp.where(lane == jnp.where(gy == 0, 15, 0), moved, 0.0)
+def inject(place, state, strip):
+    lane = iota((EXT, CY), 1)
+    edge = jnp.where(place.gy == 0, lane, CY - 1 - lane) >= CY - 4
+    for z in range(LEV):
+        moved = pltpu.roll(strip[ROWS], (120 - 16 * z) % CY, 1)
+        state[z + 1, ROWS] = jnp.where(edge, moved, state[z + 1, ROWS])
+
+
+def extract(place, state, strip):
+    lane = iota((EXT, CY), 1)
+    half = own_half((EXT, CY), place.gy)
+    group = jnp.where(half, lane >> 4, LEV)
+    packed = strip[ROWS]
+    for z in range(LEV):
+        packed = jnp.where(
+            group == z, pltpu.roll(state[z + 1, ROWS], (16 * z + 8) % CY, 1), packed
+        )
+    strip[ROWS] = packed
 
 
 def coefficients(place, wind, strip, coef, scoef, adjoint):
@@ -238,24 +252,22 @@
             east, north = 0.5 * wind[0, z, ROWS], 0.5 * wind[1, z, ROWS]
             coef[0, z] = DIFFUSION - east
             coef[1, z] = DIFFUSION + east
-            coef[2, z] = DIFFUSION - north
-            coef[3, z] = DIFFUSION + north
+            coef[2, z] = jnp.where(lane == CY - 1, 0.0, DIFFUSION - north)
+            coef[3, z] = jnp.where(lane == 0, 0.0, DIFFUSION + north)
         east, north = 0.5 * strip[0, ROWS], 0.5 * strip[1, ROWS]
         scoef[0] = DIFFUSION - east
         scoef[1] = DIFFUSION + east
         scoef[2] = DIFFUSION - north
         scoef[3] = DIFFUSION + north
         return
-    inj = injected(strip[1, ROWS], place.gy)
     for z in range(LEV):
         north = wind[1, z, ROWS]
-        edge = pltpu.roll(inj, (CY - 16 * z) % CY, 1)
-        after = jnp.where(lane == CY - 1, edge, pltpu.roll(north, CY - 1, 1))
-        before = jnp.where(lane == 0, edge, pltpu.roll(north, 1, 1))
+        after = pltpu.roll(north, CY - 1, 1)
+        before = pltpu.roll(north, 1, 1)
         coef[0, z] = DIFFUSION + 0.5 * wind[0, z, UP]
         coef[1, z] = DIFFUSION - 0.5 * wind[0, z, DOWN]
-        coef[2, z] = DIFFUSION + 0.5 * after
-        coef[3, z] = DIFFUSION - 0.5 * before
+        coef[2, z] = jnp.where(lane == CY - 1, 0.0, DIFFUSION + 0.5 * after)
+        coef[3, z] = jnp.where(lane == 0, 0.0, DIFFUSION - 0.5 * before)
     scoef[0] = DIFFUSION + 0.5 * strip[0, UP]
     scoef[1] = DIFFUSION - 0.5 * strip[0, DOWN]
     scoef[2] = DIFFUSION + 0.5 * pltpu.roll(strip[1, ROWS], CY - 1, 1)
@@ -275,12 +287,10 @@
 def one_step(place, src, dst, ssrc, sdst, coef, scoef):
     lane = iota((EXT, CY), 1)
     own = ssrc[ROWS]
-    inj = injected(own, place.gy)
     for z in range(LEV):
         mid = src[z + 1, ROWS]
-        edge = pltpu.roll(inj, (CY - 16 * z) % CY, 1)
-        after = jnp.where(lane == CY - 1, edge, pltpu.roll(mid, CY - 1, 1))
-        before = jnp.where(lane == 0, edge, pltpu.roll(mid, 1, 1))
+        after = pltpu.roll(mid, CY - 1, 1)
+        before = pltpu.roll(mid, 1, 1)
         out = (
             CENTRE * mid
             + coef[0, z] * src[z + 1, UP]
@@ -319,6 +329,7 @@
         return 0
 
     lax.fori_loop(0, 2, two, 0)
+    inject(place, state.at[0], strip.at[0, 0])
 
 
 STATE = pltpu.VMEM((2, LEV + 2, BUF, CY), F32)
@@ -481,6 +492,8 @@
         rl2_out[z] = rl[tile]
     s_f[slot, 0, ROWS] = s_b[end, 0, ROWS] - estrip[0, ROWS]
     s_b[slot, 0, ROWS] = (estrip[1, ROWS] + ext[2, LEV]) * follows
+    extract(place, x_f.at[slot], s_f.at[slot, 0])
+    extract(place, x_b.at[slot], s_b.at[slot, 0])
 
     sweep(place, x_b, s_b, coef, scoef, counts[1])
     cross = jnp.zeros((8, CY), F32)
@@ -509,6 +522,8 @@
         x_b[slot, z + 1, ROWS] = ext[1, z]
     s_f[slot, 0, ROWS] = ext[0, LEV]
     s_b[slot, 0, ROWS] = ext[1, LEV]
+    extract(place, x_f.at[slot], s_f.at[slot, 0])
+    extract(place, x_b.at[slot], s_b.at[slot, 0])
     sweep(place, x_f, s_f, coef, scoef, counts[0])
     for z in range(LEV):
         rl1 = ext[1, z, tile]

time: 82.6 us -> 81.3 us (0.984)
  starting transfers between devices: 39 us -> 35.7 us
  Pallas kernels: 20.5 us -> 21.8 us
    ppermute x1, starting transfers between devices: 7.1 us -> 3.96 us  [shards(): z_f2 = lax.ppermute(f21, 'tm', up)]
    pallas_call x6, Pallas kernels: 20.5 us -> 21.8 us  [call(): pl.pallas_call(body, out_shape=shapes, in_specs=in_specs, out_specs=[FAR...]
  transfers between devices with their start and end apart: 11 -> 11, of which waited for: 3 -> 4; matrix products, arithmetic and copies ran while one was open for 1% -> 1% of each run, Pallas kernels for 16% -> 18%
where the time goes in v3:
time: 81.3 us; the launch traced here: 80.1 us
  starting transfers between devices  35.7 us (44%)
  Pallas kernels  21.8 us (27%)
  waiting for transfers between devices  19.3 us (24%)
  local copies, waits for them, and re-layouts  2.21 us (3%)
  between operations  1.01 us (1%)
    pallas_call x6, Pallas kernels, call(): pl.pallas_call(body, out_shape=shapes, in_specs=in_specs, out_specs=[FAR...  21.8 us
    all_to_all x1, starting transfers between devices, shards(): sums = lax.all_to_all(send, ('tm', 'gx', 'gy'), 0, 0, tiled=True)  15.6 us
    all_to_all x1, waiting for transfers between devices, shards(): sums = lax.all_to_all(send, ('tm', 'gx', 'gy'), 0, 0, tiled=True)  12.7 us
    ppermute x1, starting transfers between devices, shards(): bg = lax.ppermute(b_send, axes, plane(pair_b, False))  5.36 us
    ppermute x1, waiting for transfers between devices, shards(): zh = lax.ppermute(z_edges, 'tm', down)  5.01 us
    ppermute x1, starting transfers between devices, shards(): z_f2 = lax.ppermute(f21, 'tm', up)  3.96 us
    ppermute x1, starting transfers between devices, shards(): even = lax.ppermute(even_send, 'tm', swap(0))  2.64 us
    ppermute x1, starting transfers between devices, shards(): got = lax.ppermute(own, axes, plane(lambda i: i, True))  2.21 us
  transfers between devices with their start and end apart: 11, of which 4 were waited for; matrix products, arithmetic and copies ran while one was open for 1% of the time, Pallas kernels for 18%

profile of v3, /device:TPU:1, one launch (start us, length us, event | category | flops | bytes accessed | tf_op | source)
XLA Modules:
  0.0 80.1 jit_solution(17834526743045058907)
XLA Ops:
  0.7 4.6 %shard_map.154 = (f32[86,8,128]{2,1,0:T(8,128)}, f32[86,8,128]{2,1,0:T(8,128)}, f32[6,64,128]{2,1,0:T(8,128)}, f32[136,8,128]{2,1,0:T(8,128)}, f32[2,8,64,128]{3,2,1,0:T(8,128)}, /*index=5*/f32[8,64,128]{2,1,0:T(8,128)}) custom-call(s32[2,1,1,1024]{3,2,1,0:T(1,128)} %cells.2, f32[2,1,1,1024]{3,2,1,0:T(1,128)} %m.3, f32[2,8,64,128]{3,2,1,0:T(8,128)} %l.3, ...), custom_call_target="tpu_custom_call" | custom-call | flops 2750000128 | bytes 5406720 | tf_op jit(solution)/shard_map/pallas_call | solution.py:37
  5.3 2.2 %collective-permute-start = (f32[6,64,128]{2,1,0:T(8,128)}, f32[6,64,128]{2,1,0:T(8,128)S(1)}, u32[]{:S(2)}, u32[]{:S(2)}) collective-permute-start(f32[6,64,128]{2,1,0:T(8,128)} %get-tuple-element.34.own), channel_id=1, source_target_pairs={{0,1},{1,0},{2,3},{3,2},{4,5},{5,4},{6,7},{7,6},{8,9},{9,8},{10,11... | collective-permute-start | bytes 589832 | tf_op jit(solution)/shard_map/ppermute | solution.py:651
  7.5 5.4 %collective-permute-start.1 = (f32[86,8,128]{2,1,0:T(8,128)}, f32[86,8,128]{2,1,0:T(8,128)S(1)}, u32[]{:S(2)}, u32[]{:S(2)}) collective-permute-start(f32[86,8,128]{2,1,0:T(8,128)} %get-tuple-element.35), channel_id=1, source_target_pairs={{2,4},{3,5},{4,2},{5,3},{6,8},{7,9},{8,6},{9,7},{10,12},{11,13},{1... | collective-permute-start | bytes 1056776 | tf_op jit(solution)/shard_map/ppermute | solution.py:652
  12.8 0.8 slice.36
  13.6 1.9 %collective-permute-start.3 = (f32[6,8,128]{2,1,0:T(8,128)S(1)}, f32[6,8,128]{2,1,0:T(8,128)S(1)}, u32[]{:S(2)}, u32[]{:S(2)}) collective-permute-start(f32[6,8,128]{2,1,0:T(8,128)S(1)} %slice.36), channel_id=1, source_target_pairs={{2,5},{3,4},{4,3},{5,2},{6,9},{7,8},{8,7},{9,6},{10,13},{11,12},{1... | collective-permute-start | bytes 73736 | tf_op jit(solution)/shard_map/ppermute | solution.py:654
  15.5 0.1 collective-permute-start.2
  15.6 1.3 %collective-permute-start.7 = (f32[136,8,128]{2,1,0:T(8,128)}, f32[136,8,128]{2,1,0:T(8,128)S(1)}, u32[]{:S(2)}, u32[]{:S(2)}) collective-permute-start(f32[136,8,128]{2,1,0:T(8,128)} %get-tuple-element.41.z_own), channel_id=1, source_target_pairs={{32,0},{64,32},{96,64},{128,96},{160,128},{192,160},{224,192},{33,... | collective-permute-start | bytes 1671176 | tf_op jit(solution)/shard_map/ppermute | solution.py:655
  17.0 0.6 collective-permute-start.4
  17.6 2.4 %shard_map.156 = (f32[2,1,1,1024]{3,2,1,0:T(1,128)S(1)}, f32[2,8,64,128]{3,2,1,0:T(8,128)S(1)}) custom-call(s32[2,1,1,1024]{3,2,1,0:T(1,128)S(1)} %copy-done.11, f32[2,1,1,1024]{3,2,1,0:T(1,128)S(1)} %copy-done.1, f32[2,8,64,128]{3,2,1,0:T(8,128)S(1)} %copy-done.5, f32[2,1,1,1024]{3,2,1,0:T(1,128)S(1)} %copy-done.10, f32[2,1,1,1024]{3,2,1,0:T(1,128)S(1)} %copy-done.12), custom_call_target="tpu_custom_call" | custom-call | flops 2640000000 | bytes 1089536 | tf_op jit(solution)/shard_map/pallas_call | solution.py:37
  20.1 1.4 %collective-permute-done.1.bg = f32[86,8,128]{2,1,0:T(8,128)S(1)} collective-permute-done((f32[86,8,128]{2,1,0:T(8,128)}, f32[86,8,128]{2,1,0:T(8,128)S(1)}, u32[]{:S(2)}, u32[]{:S(2)}) %collective-permute-start.1) | collective-permute-done | bytes 352288 | tf_op jit(solution)/shard_map/ppermute | solution.py:652
  21.6 1.3 %collective-permute-start.8 = (f32[45,8,128]{2,1,0:T(8,128)S(1)}, f32[45,8,128]{2,1,0:T(8,128)S(1)}, u32[]{:S(2)}, u32[]{:S(2)}) collective-permute-start(f32[45,8,128]{2,1,0:T(8,128)S(1)} %fusion), channel_id=1, source_target_pairs={{32,0},{64,32},{96,64},{128,96},{160,128},{192,160},{224,192},{33,... | collective-permute-start | bytes 552968 | tf_op jit(solution)/shard_map/ppermute | solution.py:670
  23.0 4.2 %shard_map.155 = (f32[3,9,80,128]{3,2,1,0:T(8,128)S(1)}, f32[2,8,64,128]{3,2,1,0:T(8,128)S(1)}, f32[2,8,64,128]{3,2,1,0:T(8,128)S(1)}, f32[2,8,64,128]{3,2,1,0:T(8,128)S(1)}) custom-call(s32[2]{0:T(128)S(1)} %copy-done.13, f32[2,8,64,128]{3,2,1,0:T(8,128)S(1)} %copy-done.5, f32[2,8,64,128]{3,2,1,0:T(8,128)S(1)} %copy-done.6, ...), custom_call_target="tpu_custom_call" | custom-call | flops 5500000256 | bytes 7258120 | tf_op jit(solution)/shard_map/pallas_call | solution.py:37
  27.3 2.6 %collective-permute-start.5 = (f32[2,8,64,128]{3,2,1,0:T(8,128)S(1)}, f32[2,8,64,128]{3,2,1,0:T(8,128)S(1)}, u32[]{:S(2)}, u32[]{:S(2)}) collective-permute-start(f32[2,8,64,128]{3,2,1,0:T(8,128)S(1)} %get-tuple-element.38), channel_id=1, source_target_pairs={{0,32},{64,96},{128,160},{192,224},{32,0},{96,64},{160,128},{224,1... | collective-permute-start | bytes 1572872 | tf_op jit(solution)/shard_map/ppermute | solution.py:685
  29.9 0.9 %collective-permute-start.6 = (f32[2,8,64,128]{3,2,1,0:T(8,128)S(1)}, f32[2,8,64,128]{3,2,1,0:T(8,128)S(1)}, u32[]{:S(2)}, u32[]{:S(2)}) collective-permute-start(f32[2,8,64,128]{3,2,1,0:T(8,128)S(1)} %get-tuple-element.39), channel_id=1, source_target_pairs={{32,64},{96,128},{160,192},{64,32},{128,96},{192,160},{33,65},{97,... | collective-permute-start | bytes 1572872 | tf_op jit(solution)/shard_map/ppermute | solution.py:686
  30.8 5.0 %collective-permute-done.8.zh = f32[45,8,128]{2,1,0:T(8,128)S(1)} collective-permute-done((f32[45,8,128]{2,1,0:T(8,128)S(1)}, f32[45,8,128]{2,1,0:T(8,128)S(1)}, u32[]{:S(2)}, u32[]{:S(2)}) %collective-permute-start.8) | collective-permute-done | bytes 184352 | tf_op jit(solution)/shard_map/ppermute | solution.py:670
  35.8 7.1 %shard_map.157 = (f32[8,64,128]{2,1,0:T(8,128)S(1)}, f32[8,64,128]{2,1,0:T(8,128)S(1)}, f32[8,64,128]{2,1,0:T(8,128)S(1)}, f32[8,64,128]{2,1,0:T(8,128)S(1)}, f3...) custom-call(s32[2]{0:T(128)S(1)} %copy-done.13, ...), custom_call_target="tpu_custom_call" | custom-call | flops 9900000256 | bytes 7516168 | tf_op jit(solution)/shard_map/pallas_call | solution.py:37
  42.8 4.0 %collective-permute-start.9 = (f32[8,64,128]{2,1,0:T(8,128)S(1)}, f32[8,64,128]{2,1,0:T(8,128)}, u32[]{:S(2)}, u32[]{:S(2)}) collective-permute-start(f32[8,64,128]{2,1,0:T(8,128)S(1)} %get-tuple-element.46.f21), channel_id=1, source_target_pairs={{0,32},{32,64},{64,96},{96,128},{128,160},{160,192},{192,224},{1,3... | collective-permute-start | bytes 786440 | tf_op jit(solution)/shard_map/ppermute | solution.py:694
  46.8 0.2 collective-permute-done.5.even
  47.0 1.0 %shard_map.158 = (f32[6,8,64,128]{3,2,1,0:T(8,128)S(1)}, f32[6,1,1,1024]{3,2,1,0:T(1,128)S(1)}, f32[256,128]{1,0:T(8,128)}) custom-call(f32[2,8,64,128]{3,2,1,0:T(8,128)S(1)} %collective-permute-done.5.even, f32[2,8,64,128]{3,2,1,0:T(8,128)S(1)} %collective-permute-done.6.odd, f32[8,64,128]{2,1,0:T(8,128)S(1)} %get-tuple-element.45.rl2, ...), custom_call_target="tpu_custom_call" | custom-call | flops 440000000 | bytes 6250496 | tf_op jit(solution)/shard_map/pallas_call | solution.py:37
  48.0 0.6 copy-done.8
  48.6 15.6 %all-to-all-start = ((f32[256,1,128]{2,1,0:T(1,128)}), f32[256,1,128]{2,1,0:T(1,128)S(1)}, u32[]{:S(2)}, u32[]{:S(2)}) async-start(f32[256,1,128]{2,1,0:T(1,128)} %bitcast.3), calls=%async_computation | async-start | bytes 262144 | tf_op jit(solution)/shard_map/all_to_all | solution.py:702
  64.2 12.7 %all-to-all-done = f32[256,1,128]{2,1,0:T(1,128)S(1)} async-done(((f32[256,1,128]{2,1,0:T(1,128)}), f32[256,1,128]{2,1,0:T(1,128)S(1)}, u32[]{:S(2)}, u32[]{:S(2)}) %all-to-all-start) | async-done | bytes 131104 | tf_op jit(solution)/shard_map/all_to_all | solution.py:702
  76.9 0.7 copy-done.9
  77.6 2.4 %shard_map.159 = (f32[2,8,64,128]{3,2,1,0:T(8,128)}, f32[2,1,1,1024]{3,2,1,0:T(1,128)}, f32[2,8,64,128]{3,2,1,0:T(8,128)}, f32[2,8,64,128]{3,2,1,0:T(8,128)}, f3...) custom-call(f32[256,128]{1,0:T(8,128)S(1)} %bitcast.12, f32[2,8,64,128]{3,2,1,0:T(8,128)S(1)} %copy-done.6, ...), custom_call_target="tpu_custom_call" | custom-call | flops 1650000000 | bytes 5677056 | tf_op jit(solution)/shard_map/pallas_call | solution.py:37
  (48 shorter events, 0.1 us)
Async XLA Ops:
  0.6 17.0 %copy-start.5 = (f32[2,8,64,128]{3,2,1,0:T(8,128)S(1)}, f32[2,8,64,128]{3,2,1,0:T(8,128)}, u32[]{:S(2)}) copy-start(f32[2,8,64,128]{3,2,1,0:T(8,128)} %v.5) | copy-start | bytes 1572868
  0.6 17.0 %copy-start.11 = (s32[2,1,1,1024]{3,2,1,0:T(1,128)S(1)}, s32[2,1,1,1024]{3,2,1,0:T(1,128)}, u32[]{:S(2)}) copy-start(s32[2,1,1,1024]{3,2,1,0:T(1,128)} %cells.2) | copy-start | bytes 24580
  0.7 17.0 %copy-start.1 = (f32[2,1,1,1024]{3,2,1,0:T(1,128)S(1)}, f32[2,1,1,1024]{3,2,1,0:T(1,128)}, u32[]{:S(2)}) copy-start(f32[2,1,1,1024]{3,2,1,0:T(1,128)} %m.3) | copy-start | bytes 24580
  0.7 17.0 %copy-start.12 = (f32[2,1,1,1024]{3,2,1,0:T(1,128)S(1)}, f32[2,1,1,1024]{3,2,1,0:T(1,128)}, u32[]{:S(2)}) copy-start(f32[2,1,1,1024]{3,2,1,0:T(1,128)} %ov.3) | copy-start | bytes 24580
  0.7 17.0 %copy-start.10 = (f32[2,1,1,1024]{3,2,1,0:T(1,128)S(1)}, f32[2,1,1,1024]{3,2,1,0:T(1,128)}, u32[]{:S(2)}) copy-start(f32[2,1,1,1024]{3,2,1,0:T(1,128)} %dep.1) | copy-start | bytes 24580
  5.3 11.6 %collective-permute-start = (f32[6,64,128]{2,1,0:T(8,128)}, f32[6,64,128]{2,1,0:T(8,128)S(1)}, u32[]{:S(2)}, u32[]{:S(2)}) collective-permute-start(f32[6,64,128]{2,1,0:T(8,128)} %get-tuple-element.34.own), channel_id=1, source_target_pairs={{0,1},{1,0},{2,3},{3,2},{4,5},{5,4},{6,7},{7,6},{8,9},{9,8},{10,11... | collective-permute-start | bytes 589832 | tf_op jit(solution)/shard_map/ppermute | solution.py:651
  7.5 14.0 %collective-permute-start.1 = (f32[86,8,128]{2,1,0:T(8,128)}, f32[86,8,128]{2,1,0:T(8,128)S(1)}, u32[]{:S(2)}, u32[]{:S(2)}) collective-permute-start(f32[86,8,128]{2,1,0:T(8,128)} %get-tuple-element.35), channel_id=1, source_target_pairs={{2,4},{3,5},{4,2},{5,3},{6,8},{7,9},{8,6},{9,7},{10,12},{11,13},{1... | collective-permute-start | bytes 1056776 | tf_op jit(solution)/shard_map/ppermute | solution.py:652
  13.6 8.0 %collective-permute-start.3 = (f32[6,8,128]{2,1,0:T(8,128)S(1)}, f32[6,8,128]{2,1,0:T(8,128)S(1)}, u32[]{:S(2)}, u32[]{:S(2)}) collective-permute-start(f32[6,8,128]{2,1,0:T(8,128)S(1)} %slice.36), channel_id=1, source_target_pairs={{2,5},{3,4},{4,3},{5,2},{6,9},{7,8},{8,7},{9,6},{10,13},{11,12},{1... | collective-permute-start | bytes 73736 | tf_op jit(solution)/shard_map/ppermute | solution.py:654
  15.5 6.0 %collective-permute-start.2 = (f32[86,8,128]{2,1,0:T(8,128)}, f32[86,8,128]{2,1,0:T(8,128)S(1)}, u32[]{:S(2)}, u32[]{:S(2)}) collective-permute-start(f32[86,8,128]{2,1,0:T(8,128)} %get-tuple-element.36), channel_id=1, source_target_pairs={{0,2},{1,3},{2,0},{3,1},{4,6},{5,7},{6,4},{7,5},{8,10},{9,11},{10,... | collective-permute-start | bytes 1056776 | tf_op jit(solution)/shard_map/ppermute | solution.py:653
  15.6 20.2 %collective-permute-start.7 = (f32[136,8,128]{2,1,0:T(8,128)}, f32[136,8,128]{2,1,0:T(8,128)S(1)}, u32[]{:S(2)}, u32[]{:S(2)}) collective-permute-start(f32[136,8,128]{2,1,0:T(8,128)} %get-tuple-element.41.z_own), channel_id=1, source_target_pairs={{32,0},{64,32},{96,64},{128,96},{160,128},{192,160},{224,192},{33,... | collective-permute-start | bytes 1671176 | tf_op jit(solution)/shard_map/ppermute | solution.py:655
  17.0 6.0 %copy-start.2 = (f32[2,8,64,128]{3,2,1,0:T(8,128)S(1)}, f32[2,8,64,128]{3,2,1,0:T(8,128)}, u32[]{:S(2)}) copy-start(f32[2,8,64,128]{3,2,1,0:T(8,128)} %we.3) | copy-start | bytes 1572868
  17.0 6.0 %copy-start.3 = (f32[2,8,64,128]{3,2,1,0:T(8,128)S(1)}, f32[2,8,64,128]{3,2,1,0:T(8,128)}, u32[]{:S(2)}) copy-start(f32[2,8,64,128]{3,2,1,0:T(8,128)} %wn.3) | copy-start | bytes 1572868
  17.0 6.0 %copy-start.4 = (f32[2,8,64,128]{3,2,1,0:T(8,128)S(1)}, f32[2,8,64,128]{3,2,1,0:T(8,128)}, u32[]{:S(2)}) copy-start(f32[2,8,64,128]{3,2,1,0:T(8,128)} %mv.3) | copy-start | bytes 1572868
  17.0 6.0 %copy-start.6 = (f32[2,8,64,128]{3,2,1,0:T(8,128)S(1)}, f32[2,8,64,128]{3,2,1,0:T(8,128)}, u32[]{:S(2)}) copy-start(f32[2,8,64,128]{3,2,1,0:T(8,128)} %l.3) | copy-start | bytes 1572868
  17.0 6.0 %copy-start.7 = (f32[6,64,128]{2,1,0:T(8,128)S(1)}, f32[6,64,128]{2,1,0:T(8,128)}, u32[]{:S(2)}) copy-start(f32[6,64,128]{2,1,0:T(8,128)} %get-tuple-element.34.own) | copy-start | bytes 589828
  17.0 6.0 %copy-start.13 = (s32[2]{0:T(128)S(1)}, s32[2]{0:T(128)}, u32[]{:S(2)}) copy-start(s32[2]{0:T(128)} %counts.3) | copy-start | bytes 28
  17.0 6.0 %copy-start.14 = (f32[2,8,64,128]{3,2,1,0:T(8,128)S(1)}, f32[2,8,64,128]{3,2,1,0:T(8,128)}, u32[]{:S(2)}) copy-start(f32[2,8,64,128]{3,2,1,0:T(8,128)} %get-tuple-element.32.lh) | copy-start | bytes 1572868
  17.0 4.5 %collective-permute-start.4 = (f32[6,16,128]{2,1,0:T(8,128)S(1)}, f32[6,16,128]{2,1,0:T(8,128)S(1)}, u32[]{:S(2)}, u32[]{:S(2)}) collective-permute-start(f32[6,16,128]{2,1,0:T(8,128)S(1)} %pad_maximum_fusion), channel_id=1, source_target_pairs={{0,2},{1,3},{2,0},{3,1},{4,6},{5,7},{6,4},{7,5},{8,10},{9,11},{10,... | collective-permute-start | bytes 147464 | tf_op jit(solution)/shard_map/ppermute | solution.py:658
  21.6 14.2 %collective-permute-start.8 = (f32[45,8,128]{2,1,0:T(8,128)S(1)}, f32[45,8,128]{2,1,0:T(8,128)S(1)}, u32[]{:S(2)}, u32[]{:S(2)}) collective-permute-start(f32[45,8,128]{2,1,0:T(8,128)S(1)} %fusion), channel_id=1, source_target_pairs={{32,0},{64,32},{96,64},{128,96},{160,128},{192,160},{224,192},{33,... | collective-permute-start | bytes 552968 | tf_op jit(solution)/shard_map/ppermute | solution.py:670
  27.3 19.7 %collective-permute-start.5 = (f32[2,8,64,128]{3,2,1,0:T(8,128)S(1)}, f32[2,8,64,128]{3,2,1,0:T(8,128)S(1)}, u32[]{:S(2)}, u32[]{:S(2)}) collective-permute-start(f32[2,8,64,128]{3,2,1,0:T(8,128)S(1)} %get-tuple-element.38), channel_id=1, source_target_pairs={{0,32},{64,96},{128,160},{192,224},{32,0},{96,64},{160,128},{224,1... | collective-permute-start | bytes 1572872 | tf_op jit(solution)/shard_map/ppermute | solution.py:685
  29.9 17.1 %collective-permute-start.6 = (f32[2,8,64,128]{3,2,1,0:T(8,128)S(1)}, f32[2,8,64,128]{3,2,1,0:T(8,128)S(1)}, u32[]{:S(2)}, u32[]{:S(2)}) collective-permute-start(f32[2,8,64,128]{3,2,1,0:T(8,128)S(1)} %get-tuple-element.39), channel_id=1, source_target_pairs={{32,64},{96,128},{160,192},{64,32},{128,96},{192,160},{33,65},{97,... | collective-permute-start | bytes 1572872 | tf_op jit(solution)/shard_map/ppermute | solution.py:686
  35.8 11.2 %copy-start = (f32[136,8,128]{2,1,0:T(8,128)S(1)}, f32[136,8,128]{2,1,0:T(8,128)}, u32[]{:S(2)}) copy-start(f32[136,8,128]{2,1,0:T(8,128)} %get-tuple-element.41.z_own) | copy-start | bytes 1671172
  42.8 21.4 %collective-permute-start.9 = (f32[8,64,128]{2,1,0:T(8,128)S(1)}, f32[8,64,128]{2,1,0:T(8,128)}, u32[]{:S(2)}, u32[]{:S(2)}) collective-permute-start(f32[8,64,128]{2,1,0:T(8,128)S(1)} %get-tuple-element.46.f21), channel_id=1, source_target_pairs={{0,32},{32,64},{64,96},{96,128},{128,160},{160,192},{192,224},{1,3... | collective-permute-start | bytes 786440 | tf_op jit(solution)/shard_map/ppermute | solution.py:694
  48.6 28.3 %all-to-all-start = ((f32[256,1,128]{2,1,0:T(1,128)}), f32[256,1,128]{2,1,0:T(1,128)S(1)}, u32[]{:S(2)}, u32[]{:S(2)}) async-start(f32[256,1,128]{2,1,0:T(1,128)} %bitcast.3), calls=%async_computation | async-start | bytes 262144 | tf_op jit(solution)/shard_map/all_to_all | solution.py:702
  (3 other events, 7.3 us)

commit v4 on v3

--- a/solution.py
+++ b/solution.py
@@ -556,13 +556,14 @@
 
 def dots_kernel(
     even, odd, rl2, f21, b20, z_own, h2, rv0, dots_in, rl1, rv1, qv1, ql1, qm, rm, m,
-    keep_out, obs_out, send_out,
+    keep_out, send_out,
 ):
     follows = jnp.where(lax.axis_index("tm") == lax.axis_size("tm") - 1, 0.0, 1.0)
     starts = jnp.where(lax.axis_index("tm") == 0, 1.0, 0.0)
-    obs_out[0:2] = rm[...]
-    obs_out[2:4] = qm[...]
-    obs_out[4:6] = m[...]
+    for i, kept in enumerate((rm, qm, m)):
+        for s in range(2):
+            for k in range(m.shape[-1] // CY):
+                keep_out[6, 2 * i + s, k : k + 1] = kept[s, 0, :, k * CY : (k + 1) * CY]
     cross, square = dots_in[0], dots_in[1]
     is_odd = lax.axis_index("tm") % 2 == 1
 
@@ -590,7 +591,7 @@
 
 
 def last_kernel(
-    sums, l, v, rv0, z_f2, keep, obs_pair,
+    sums, l, v, rv0, z_f2, keep,
     l_out, m_out, v_out, a_out, b_out, c_out,
 ):
     total = jnp.sum(sums[...], 0, keepdims=True)
@@ -598,9 +599,11 @@
     cross = jnp.sum(jnp.where(lane == 0, total, 0.0), 1, keepdims=True)
     square = jnp.sum(jnp.where(lane == 1, total, 0.0), 1, keepdims=True)
     alpha = cross / (square + 1e-06)
-    rm, qm = obs_pair[0:2], obs_pair[2:4]
-    m_out[...] = obs_pair[4:6] + alpha * rm
-    b_out[...] = rm - alpha * qm
+    for s in range(2):
+        for k in range(m_out.shape[-1] // CY):
+            rm, qm, m = (keep[6, 2 * i + s, k : k + 1] for i in range(3))
+            m_out[s, 0, :, k * CY : (k + 1) * CY] = m + alpha * rm
+            b_out[s, 0, :, k * CY : (k + 1) * CY] = rm - alpha * qm
     for z in range(LEV):
         rl0, rl1, rv1, qv0, qv1, ql1 = (keep[i, z] for i in range(6))
         ql0 = rv0[1, z] * rl0 + rv0[0, z] - z_f2[z]
@@ -651,10 +654,10 @@
     got = lax.ppermute(own, axes, plane(lambda i: i, True))
     bg = lax.ppermute(b_send, axes, plane(pair_b, False))
     ag = lax.ppermute(a_send, axes, plane(lambda i: i ^ 1, False))
-    by = lax.ppermute(b_send[edge:], axes, plane(pair_b, True))
     zt = lax.ppermute(z_send, "tm", down)
     ay_send = jnp.concatenate([got[:, :8], got[:, CX - 8 :]], 1)
-    ay_send, late_cells = lax.optimization_barrier((ay_send, cells4))
+    ay_send, late_cells, by_send = lax.optimization_barrier((ay_send, cells4, b_send[edge:]))
+    by = lax.ppermute(by_send, axes, plane(pair_b, True))
     ay = lax.ppermute(ay_send, axes, plane(lambda i: i ^ 1, False))
     rm, h2 = call(obs_kernel, [obs, (2,) + tile], [late_cells, m4, v4, d4, ov4], micros=2.4)
 
@@ -691,19 +694,20 @@
         scratch,
         micros=9.0,
     )
-    z_f2 = lax.ppermute(f21, "tm", up)
     n = ntm * ngx * ngy
-    keep, obs_pair, send = call(
+    keep, send = call(
         dots_kernel,
-        [(6,) + tile, (6,) + obs[1:], (n, CY)],
+        [(7,) + tile, (n, CY)],
         [even, odd, rl2, f21, b20, z_send, h2, rv0, dots, rl1, rv1, qv1, ql1, qm, rm, m4],
         micros=0.4,
     )
+    send, late_f21 = lax.optimization_barrier((send, f21))
     sums = lax.all_to_all(send, ("tm", "gx", "gy"), 0, 0, tiled=True)
+    z_f2 = lax.ppermute(late_f21, "tm", up)
     return call(
         last_kernel,
         [l4.shape, obs, l4.shape, l4.shape, obs, l4.shape],
-        [sums, l4, v4, rv0, z_f2, keep, obs_pair],
+        [sums, l4, v4, rv0, z_f2, keep],
         micros=1.5,
     )
 

time: 81.3 us -> 78.4 us (0.964); the launches traced: 80.1 us -> 78.1 us
  blocking collectives: 0 us -> 27 us
  waiting for transfers between devices: 19.3 us -> 5.41 us
  starting transfers between devices: 35.7 us -> 24.7 us
  Pallas kernels: 21.8 us -> 19.1 us
  local copies, waits for them, and re-layouts: 2.21 us -> 0.86 us
    all_to_all x0 -> x1, blocking collectives: none -> 27 us  [shards(): sums = lax.all_to_all(send, ('tm', 'gx', 'gy'), 0, 0, tiled=True)]
    all_to_all x1 -> x0, starting transfers between devices: 15.6 us -> none  [shards(): sums = lax.all_to_all(send, ('tm', 'gx', 'gy'), 0, 0, tiled=True)]
    all_to_all x1 -> x0, waiting for transfers between devices: 12.7 us -> none  [shards(): sums = lax.all_to_all(send, ('tm', 'gx', 'gy'), 0, 0, tiled=True)]
    ppermute x2, starting transfers between devices: 5.87 us -> 11.1 us  [the longest x1 6.82 us: shards(): z_f2 = lax.ppermute(late_f21, 'tm', up)]
    ppermute x1, waiting for transfers between devices: 0.21 us -> 5.31 us  [shards(): even = lax.ppermute(even_send, 'tm', swap(0))]
    ppermute x1, waiting for transfers between devices: 5.01 us -> 0.08 us  [shards(): zh = lax.ppermute(z_edges, 'tm', down)]
    pallas_call x6, Pallas kernels: 21.8 us -> 19.1 us  [call(): pl.pallas_call(body, out_shape=shapes, in_specs=in_specs, out_specs=[FAR...]
    ppermute x1, waiting for transfers between devices: 1.43 us -> 0.01 us  [shards(): bg = lax.ppermute(b_send, axes, plane(pair_b, False))]
  transfers between devices with their start and end apart: 11 -> 10, of which waited for: 4 -> 2; matrix products, arithmetic and copies ran while one was open for 1% -> 1% of each run, Pallas kernels for 18% -> 16%
where the time goes in v4:
time: 78.4 us; the launch traced here: 78.1 us
  blocking collectives  27 us (34%)
  starting transfers between devices  24.7 us (32%)
  Pallas kernels  19.1 us (24%)
  waiting for transfers between devices  5.41 us (7%)
  between operations  1.05 us (1%)
  local copies, waits for them, and re-layouts  0.86 us (1%)
    all_to_all x1, blocking collectives, shards(): sums = lax.all_to_all(send, ('tm', 'gx', 'gy'), 0, 0, tiled=True)  27 us
    pallas_call x6, Pallas kernels, call(): pl.pallas_call(body, out_shape=shapes, in_specs=in_specs, out_specs=[FAR...  19.1 us
    ppermute x1, starting transfers between devices, shards(): z_f2 = lax.ppermute(late_f21, 'tm', up)  6.82 us
    ppermute x1, waiting for transfers between devices, shards(): even = lax.ppermute(even_send, 'tm', swap(0))  5.31 us
    ppermute x1, starting transfers between devices, shards(): by = lax.ppermute(by_send, axes, plane(pair_b, True))  4.24 us
    ppermute x1, starting transfers between devices, shards(): bg = lax.ppermute(b_send, axes, plane(pair_b, False))  4.15 us
    ppermute x1, starting transfers between devices, shards(): even = lax.ppermute(even_send, 'tm', swap(0))  2.54 us
    ppermute x1, starting transfers between devices, shards(): got = lax.ppermute(own, axes, plane(lambda i: i, True))  2.21 us
  transfers between devices with their start and end apart: 10, of which 2 were waited for; matrix products, arithmetic and copies ran while one was open for 1% of the time, Pallas kernels for 16%

profile of v4, /device:TPU:1, one launch (start us, length us, event | category | flops | bytes accessed | tf_op | source)
XLA Modules:
  0.0 78.1 jit_solution(5526426193441593570)
XLA Ops:
  0.7 4.6 %shard_map.154 = (f32[86,8,128]{2,1,0:T(8,128)}, f32[86,8,128]{2,1,0:T(8,128)}, f32[6,64,128]{2,1,0:T(8,128)}, f32[136,8,128]{2,1,0:T(8,128)}, f32[2,8,64,128]{3,2,1,0:T(8,128)}, /*index=5*/f32[8,64,128]{2,1,0:T(8,128)}) custom-call(s32[2,1,1,1024]{3,2,1,0:T(1,128)} %cells.2, f32[2,1,1,1024]{3,2,1,0:T(1,128)} %m.3, f32[2,8,64,128]{3,2,1,0:T(8,128)} %l.3, ...), custom_call_target="tpu_custom_call" | custom-call | flops 2750000128 | bytes 5406720 | tf_op jit(solution)/shard_map/pallas_call | solution.py:37
  5.3 2.2 %collective-permute-start = (f32[6,64,128]{2,1,0:T(8,128)}, f32[6,64,128]{2,1,0:T(8,128)S(1)}, u32[]{:S(2)}, u32[]{:S(2)}) collective-permute-start(f32[6,64,128]{2,1,0:T(8,128)} %get-tuple-element.36.own), channel_id=1, source_target_pairs={{0,1},{1,0},{2,3},{3,2},{4,5},{5,4},{6,7},{7,6},{8,9},{9,8},{10,11... | collective-permute-start | bytes 589832 | tf_op jit(solution)/shard_map/ppermute | solution.py:654
  7.5 1.2 %collective-permute-start.2 = (f32[86,8,128]{2,1,0:T(8,128)}, f32[86,8,128]{2,1,0:T(8,128)S(1)}, u32[]{:S(2)}, u32[]{:S(2)}) collective-permute-start(f32[86,8,128]{2,1,0:T(8,128)} %get-tuple-element.38), channel_id=1, source_target_pairs={{0,2},{1,3},{2,0},{3,1},{4,6},{5,7},{6,4},{7,5},{8,10},{9,11},{10,... | collective-permute-start | bytes 1056776 | tf_op jit(solution)/shard_map/ppermute | solution.py:656
  8.7 4.1 %collective-permute-start.1 = (f32[86,8,128]{2,1,0:T(8,128)}, f32[86,8,128]{2,1,0:T(8,128)S(1)}, u32[]{:S(2)}, u32[]{:S(2)}) collective-permute-start(f32[86,8,128]{2,1,0:T(8,128)} %get-tuple-element.37), channel_id=1, source_target_pairs={{2,4},{3,5},{4,2},{5,3},{6,8},{7,9},{8,6},{9,7},{10,12},{11,13},{1... | collective-permute-start | bytes 1056776 | tf_op jit(solution)/shard_map/ppermute | solution.py:655
  12.9 1.3 %collective-permute-start.7 = (f32[136,8,128]{2,1,0:T(8,128)}, f32[136,8,128]{2,1,0:T(8,128)S(1)}, u32[]{:S(2)}, u32[]{:S(2)}) collective-permute-start(f32[136,8,128]{2,1,0:T(8,128)} %get-tuple-element.44.z_own), channel_id=1, source_target_pairs={{32,0},{64,32},{96,64},{128,96},{160,128},{192,160},{224,192},{33,... | collective-permute-start | bytes 1671176 | tf_op jit(solution)/shard_map/ppermute | solution.py:657
  14.2 0.7 slice.38
  14.9 0.0 copy-start.2
  14.9 0.0 copy-start.3
  15.0 0.0 copy-start.6
  15.0 0.0 copy-start.11
  15.0 4.2 %collective-permute-start.3 = (f32[6,8,128]{2,1,0:T(8,128)S(1)}, f32[6,8,128]{2,1,0:T(8,128)S(1)}, u32[]{:S(2)}, u32[]{:S(2)}) collective-permute-start(f32[6,8,128]{2,1,0:T(8,128)S(1)} %slice.38), channel_id=1, source_target_pairs={{2,5},{3,4},{4,3},{5,2},{6,9},{7,8},{8,7},{9,6},{10,13},{11,12},{1... | collective-permute-start | bytes 73736 | tf_op jit(solution)/shard_map/ppermute | solution.py:660
  19.3 0.1 collective-permute-start.4
  19.4 2.4 %shard_map.156 = (f32[2,1,1,1024]{3,2,1,0:T(1,128)S(1)}, f32[2,8,64,128]{3,2,1,0:T(8,128)S(1)}) custom-call(s32[2,1,1,1024]{3,2,1,0:T(1,128)S(1)} %copy-done.9, f32[2,1,1,1024]{3,2,1,0:T(1,128)S(1)} %copy-done.1, f32[2,8,64,128]{3,2,1,0:T(8,128)S(1)} %copy-done.5, f32[2,1,1,1024]{3,2,1,0:T(1,128)S(1)} %copy-done.8, f32[2,1,1,1024]{3,2,1,0:T(1,128)S(1)} %copy-done.10), custom_call_target="tpu_custom_call" | custom-call | flops 2640000000 | bytes 1089536 | tf_op jit(solution)/shard_map/pallas_call | solution.py:37
  22.0 1.3 %collective-permute-start.8 = (f32[45,8,128]{2,1,0:T(8,128)S(1)}, f32[45,8,128]{2,1,0:T(8,128)S(1)}, u32[]{:S(2)}, u32[]{:S(2)}) collective-permute-start(f32[45,8,128]{2,1,0:T(8,128)S(1)} %fusion), channel_id=1, source_target_pairs={{32,0},{64,32},{96,64},{128,96},{160,128},{192,160},{224,192},{33,... | collective-permute-start | bytes 552968 | tf_op jit(solution)/shard_map/ppermute | solution.py:673
  23.4 4.0 %shard_map.155 = (f32[3,9,80,128]{3,2,1,0:T(8,128)S(1)}, f32[2,8,64,128]{3,2,1,0:T(8,128)S(1)}, f32[2,8,64,128]{3,2,1,0:T(8,128)S(1)}, f32[2,8,64,128]{3,2,1,0:T(8,128)S(1)}) custom-call(s32[2]{0:T(128)S(1)} %copy-done.11, f32[2,8,64,128]{3,2,1,0:T(8,128)S(1)} %copy-done.5, f32[2,8,64,128]{3,2,1,0:T(8,128)S(1)} %copy-done.6, ...), custom_call_target="tpu_custom_call" | custom-call | flops 5500000256 | bytes 7258120 | tf_op jit(solution)/shard_map/pallas_call | solution.py:37
  27.4 2.5 %collective-permute-start.5 = (f32[2,8,64,128]{3,2,1,0:T(8,128)S(1)}, f32[2,8,64,128]{3,2,1,0:T(8,128)S(1)}, u32[]{:S(2)}, u32[]{:S(2)}) collective-permute-start(f32[2,8,64,128]{3,2,1,0:T(8,128)S(1)} %get-tuple-element.41), channel_id=1, source_target_pairs={{0,32},{64,96},{128,160},{192,224},{32,0},{96,64},{160,128},{224,1... | collective-permute-start | bytes 1572872 | tf_op jit(solution)/shard_map/ppermute | solution.py:688
  29.9 0.9 %collective-permute-start.6 = (f32[2,8,64,128]{3,2,1,0:T(8,128)S(1)}, f32[2,8,64,128]{3,2,1,0:T(8,128)S(1)}, u32[]{:S(2)}, u32[]{:S(2)}) collective-permute-start(f32[2,8,64,128]{3,2,1,0:T(8,128)S(1)} %get-tuple-element.42), channel_id=1, source_target_pairs={{32,64},{96,128},{160,192},{64,32},{128,96},{192,160},{33,65},{97,... | collective-permute-start | bytes 1572872 | tf_op jit(solution)/shard_map/ppermute | solution.py:689
  30.8 0.1 collective-permute-done.8.zh
  30.9 6.2 %shard_map.157 = (f32[8,64,128]{2,1,0:T(8,128)S(1)}, f32[8,64,128]{2,1,0:T(8,128)S(1)}, f32[8,64,128]{2,1,0:T(8,128)S(1)}, f32[8,64,128]{2,1,0:T(8,128)S(1)}, f3...) custom-call(s32[2]{0:T(128)S(1)} %copy-done.11, ...), custom_call_target="tpu_custom_call" | custom-call | flops 9900000256 | bytes 7516168 | tf_op jit(solution)/shard_map/pallas_call | solution.py:37
  37.1 5.3 %collective-permute-done.5.even = f32[2,8,64,128]{3,2,1,0:T(8,128)S(1)} collective-permute-done((f32[2,8,64,128]{3,2,1,0:T(8,128)S(1)}, f32[2,8,64,128]{3,2,1,0:T(8,128)S(1)}, u32[]{:S(2)}, u32[]{:S(2)}) %collective-permute-start.5) | collective-permute-done | bytes 524320 | tf_op jit(solution)/shard_map/ppermute | solution.py:688
  42.4 0.4 shard_map.158
  42.8 6.8 %collective-permute-start.9 = (f32[8,64,128]{2,1,0:T(8,128)S(1)}, f32[8,64,128]{2,1,0:T(8,128)S(1)}, u32[]{:S(2)}, u32[]{:S(2)}) collective-permute-start(f32[8,64,128]{2,1,0:T(8,128)S(1)} %get-tuple-element.60.f21), channel_id=1, source_target_pairs={{0,32},{32,64},{64,96},{96,128},{128,160},{160,192},{192,224},{1,3... | collective-permute-start | bytes 786440 | tf_op jit(solution)/shard_map/ppermute | solution.py:706
  49.6 27.0 %all_to_all.11 = f32[256,1,128]{2,1,0:T(1,128)S(1)} all-to-all(f32[256,1,128]{2,1,0:T(1,128)S(1)} %bitcast.12), channel_id=1, replica_groups=mesh['tm'=8,'gx'=16,'gy'=2] {'tm','gx','gy'}, dimensions={0} | all-to-all | bytes 262144 | tf_op jit(solution)/shard_map/all_to_all | solution.py:705
  76.6 1.5 %shard_map.159 = (f32[2,8,64,128]{3,2,1,0:T(8,128)}, f32[2,1,1,1024]{3,2,1,0:T(1,128)}, f32[2,8,64,128]{3,2,1,0:T(8,128)}, f32[2,8,64,128]{3,2,1,0:T(8,128)}, f3...) custom-call(f32[256,128]{1,0:T(8,128)S(1)} %bitcast.13, f32[2,8,64,128]{3,2,1,0:T(8,128)S(1)} %copy-done.6, ...), custom_call_target="tpu_custom_call" | custom-call | flops 1650000000 | bytes 5914624 | tf_op jit(solution)/shard_map/pallas_call | solution.py:37
  (43 shorter events, 0.1 us)
Async XLA Ops:
  0.6 18.7 %copy-start.5 = (f32[2,8,64,128]{3,2,1,0:T(8,128)S(1)}, f32[2,8,64,128]{3,2,1,0:T(8,128)}, u32[]{:S(2)}) copy-start(f32[2,8,64,128]{3,2,1,0:T(8,128)} %v.5) | copy-start | bytes 1572868
  0.6 18.7 %copy-start.9 = (s32[2,1,1,1024]{3,2,1,0:T(1,128)S(1)}, s32[2,1,1,1024]{3,2,1,0:T(1,128)}, u32[]{:S(2)}) copy-start(s32[2,1,1,1024]{3,2,1,0:T(1,128)} %cells.2) | copy-start | bytes 24580
  0.7 18.7 %copy-start.1 = (f32[2,1,1,1024]{3,2,1,0:T(1,128)S(1)}, f32[2,1,1,1024]{3,2,1,0:T(1,128)}, u32[]{:S(2)}) copy-start(f32[2,1,1,1024]{3,2,1,0:T(1,128)} %m.3) | copy-start | bytes 24580
  0.7 18.7 %copy-start.10 = (f32[2,1,1,1024]{3,2,1,0:T(1,128)S(1)}, f32[2,1,1,1024]{3,2,1,0:T(1,128)}, u32[]{:S(2)}) copy-start(f32[2,1,1,1024]{3,2,1,0:T(1,128)} %ov.3) | copy-start | bytes 24580
  0.7 18.7 %copy-start.8 = (f32[2,1,1,1024]{3,2,1,0:T(1,128)S(1)}, f32[2,1,1,1024]{3,2,1,0:T(1,128)}, u32[]{:S(2)}) copy-start(f32[2,1,1,1024]{3,2,1,0:T(1,128)} %dep.1) | copy-start | bytes 24580
  5.3 9.6 %collective-permute-start = (f32[6,64,128]{2,1,0:T(8,128)}, f32[6,64,128]{2,1,0:T(8,128)S(1)}, u32[]{:S(2)}, u32[]{:S(2)}) collective-permute-start(f32[6,64,128]{2,1,0:T(8,128)} %get-tuple-element.36.own), channel_id=1, source_target_pairs={{0,1},{1,0},{2,3},{3,2},{4,5},{5,4},{6,7},{7,6},{8,9},{9,8},{10,11... | collective-permute-start | bytes 589832 | tf_op jit(solution)/shard_map/ppermute | solution.py:654
  7.5 14.4 %collective-permute-start.2 = (f32[86,8,128]{2,1,0:T(8,128)}, f32[86,8,128]{2,1,0:T(8,128)S(1)}, u32[]{:S(2)}, u32[]{:S(2)}) collective-permute-start(f32[86,8,128]{2,1,0:T(8,128)} %get-tuple-element.38), channel_id=1, source_target_pairs={{0,2},{1,3},{2,0},{3,1},{4,6},{5,7},{6,4},{7,5},{8,10},{9,11},{10,... | collective-permute-start | bytes 1056776 | tf_op jit(solution)/shard_map/ppermute | solution.py:656
  8.7 13.1 %collective-permute-start.1 = (f32[86,8,128]{2,1,0:T(8,128)}, f32[86,8,128]{2,1,0:T(8,128)S(1)}, u32[]{:S(2)}, u32[]{:S(2)}) collective-permute-start(f32[86,8,128]{2,1,0:T(8,128)} %get-tuple-element.37), channel_id=1, source_target_pairs={{2,4},{3,5},{4,2},{5,3},{6,8},{7,9},{8,6},{9,7},{10,12},{11,13},{1... | collective-permute-start | bytes 1056776 | tf_op jit(solution)/shard_map/ppermute | solution.py:655
  12.9 18.0 %collective-permute-start.7 = (f32[136,8,128]{2,1,0:T(8,128)}, f32[136,8,128]{2,1,0:T(8,128)S(1)}, u32[]{:S(2)}, u32[]{:S(2)}) collective-permute-start(f32[136,8,128]{2,1,0:T(8,128)} %get-tuple-element.44.z_own), channel_id=1, source_target_pairs={{32,0},{64,32},{96,64},{128,96},{160,128},{192,160},{224,192},{33,... | collective-permute-start | bytes 1671176 | tf_op jit(solution)/shard_map/ppermute | solution.py:657
  14.9 8.4 %copy-start.2 = (f32[2,8,64,128]{3,2,1,0:T(8,128)S(1)}, f32[2,8,64,128]{3,2,1,0:T(8,128)}, u32[]{:S(2)}) copy-start(f32[2,8,64,128]{3,2,1,0:T(8,128)} %we.3) | copy-start | bytes 1572868
  14.9 8.4 %copy-start.3 = (f32[2,8,64,128]{3,2,1,0:T(8,128)S(1)}, f32[2,8,64,128]{3,2,1,0:T(8,128)}, u32[]{:S(2)}) copy-start(f32[2,8,64,128]{3,2,1,0:T(8,128)} %wn.3) | copy-start | bytes 1572868
  14.9 8.4 %copy-start.4 = (f32[2,8,64,128]{3,2,1,0:T(8,128)S(1)}, f32[2,8,64,128]{3,2,1,0:T(8,128)}, u32[]{:S(2)}) copy-start(f32[2,8,64,128]{3,2,1,0:T(8,128)} %mv.3) | copy-start | bytes 1572868
  15.0 8.4 %copy-start.6 = (f32[2,8,64,128]{3,2,1,0:T(8,128)S(1)}, f32[2,8,64,128]{3,2,1,0:T(8,128)}, u32[]{:S(2)}) copy-start(f32[2,8,64,128]{3,2,1,0:T(8,128)} %l.3) | copy-start | bytes 1572868
  15.0 8.4 %copy-start.7 = (f32[6,64,128]{2,1,0:T(8,128)S(1)}, f32[6,64,128]{2,1,0:T(8,128)}, u32[]{:S(2)}) copy-start(f32[6,64,128]{2,1,0:T(8,128)} %get-tuple-element.36.own) | copy-start | bytes 589828
  15.0 8.4 %copy-start.11 = (s32[2]{0:T(128)S(1)}, s32[2]{0:T(128)}, u32[]{:S(2)}) copy-start(s32[2]{0:T(128)} %counts.3) | copy-start | bytes 28
  15.0 8.4 %copy-start.12 = (f32[2,8,64,128]{3,2,1,0:T(8,128)S(1)}, f32[2,8,64,128]{3,2,1,0:T(8,128)}, u32[]{:S(2)}) copy-start(f32[2,8,64,128]{3,2,1,0:T(8,128)} %get-tuple-element.34.lh) | copy-start | bytes 1572868
  15.0 8.4 %copy-start.13 = (f32[8,64,128]{2,1,0:T(8,128)S(1)}, f32[8,64,128]{2,1,0:T(8,128)}, u32[]{:S(2)}) copy-start(f32[8,64,128]{2,1,0:T(8,128)} %get-tuple-element.35.g1) | copy-start | bytes 786436
  15.0 6.9 %collective-permute-start.3 = (f32[6,8,128]{2,1,0:T(8,128)S(1)}, f32[6,8,128]{2,1,0:T(8,128)S(1)}, u32[]{:S(2)}, u32[]{:S(2)}) collective-permute-start(f32[6,8,128]{2,1,0:T(8,128)S(1)} %slice.38), channel_id=1, source_target_pairs={{2,5},{3,4},{4,3},{5,2},{6,9},{7,8},{8,7},{9,6},{10,13},{11,12},{1... | collective-permute-start | bytes 73736 | tf_op jit(solution)/shard_map/ppermute | solution.py:660
  19.3 2.7 %collective-permute-start.4 = (f32[6,16,128]{2,1,0:T(8,128)S(1)}, f32[6,16,128]{2,1,0:T(8,128)S(1)}, u32[]{:S(2)}, u32[]{:S(2)}) collective-permute-start(f32[6,16,128]{2,1,0:T(8,128)S(1)} %pad_maximum_fusion), channel_id=1, source_target_pairs={{0,2},{1,3},{2,0},{3,1},{4,6},{5,7},{6,4},{7,5},{8,10},{9,11},{10,... | collective-permute-start | bytes 147464 | tf_op jit(solution)/shard_map/ppermute | solution.py:661
  22.0 8.9 %collective-permute-start.8 = (f32[45,8,128]{2,1,0:T(8,128)S(1)}, f32[45,8,128]{2,1,0:T(8,128)S(1)}, u32[]{:S(2)}, u32[]{:S(2)}) collective-permute-start(f32[45,8,128]{2,1,0:T(8,128)S(1)} %fusion), channel_id=1, source_target_pairs={{32,0},{64,32},{96,64},{128,96},{160,128},{192,160},{224,192},{33,... | collective-permute-start | bytes 552968 | tf_op jit(solution)/shard_map/ppermute | solution.py:673
  27.4 15.0 %collective-permute-start.5 = (f32[2,8,64,128]{3,2,1,0:T(8,128)S(1)}, f32[2,8,64,128]{3,2,1,0:T(8,128)S(1)}, u32[]{:S(2)}, u32[]{:S(2)}) collective-permute-start(f32[2,8,64,128]{3,2,1,0:T(8,128)S(1)} %get-tuple-element.41), channel_id=1, source_target_pairs={{0,32},{64,96},{128,160},{192,224},{32,0},{96,64},{160,128},{224,1... | collective-permute-start | bytes 1572872 | tf_op jit(solution)/shard_map/ppermute | solution.py:688
  29.9 12.5 %collective-permute-start.6 = (f32[2,8,64,128]{3,2,1,0:T(8,128)S(1)}, f32[2,8,64,128]{3,2,1,0:T(8,128)S(1)}, u32[]{:S(2)}, u32[]{:S(2)}) collective-permute-start(f32[2,8,64,128]{3,2,1,0:T(8,128)S(1)} %get-tuple-element.42), channel_id=1, source_target_pairs={{32,64},{96,128},{160,192},{64,32},{128,96},{192,160},{33,65},{97,... | collective-permute-start | bytes 1572872 | tf_op jit(solution)/shard_map/ppermute | solution.py:689
  30.9 11.5 %copy-start = (f32[136,8,128]{2,1,0:T(8,128)S(1)}, f32[136,8,128]{2,1,0:T(8,128)}, u32[]{:S(2)}) copy-start(f32[136,8,128]{2,1,0:T(8,128)} %get-tuple-element.44.z_own) | copy-start | bytes 1671172
  42.8 33.9 %collective-permute-start.9 = (f32[8,64,128]{2,1,0:T(8,128)S(1)}, f32[8,64,128]{2,1,0:T(8,128)S(1)}, u32[]{:S(2)}, u32[]{:S(2)}) collective-permute-start(f32[8,64,128]{2,1,0:T(8,128)S(1)} %get-tuple-element.60.f21), channel_id=1, source_target_pairs={{0,32},{32,64},{64,96},{96,128},{128,160},{160,192},{192,224},{1,3... | collective-permute-start | bytes 786440 | tf_op jit(solution)/shard_map/ppermute | solution.py:706

commit v5 on v4

--- a/solution.py
+++ b/solution.py
@@ -99,7 +99,7 @@
 
 def pack_kernel(
     cells_h, m_h, l_h, f_h, mv_h, v_h, we_h, wn_h,
-    b_out, a_out, strip_out, z_out, lh_out, g1_out,
+    b_out, a_out, by_out, strip_out, z_out, lh_out, g1_out,
     g_s, cells, m, l, f, mv, v, we, wn, sems,
 ):
     far = (cells_h, m_h, l_h, f_h, mv_h, v_h, we_h, wn_h)
@@ -160,15 +160,18 @@
                 g_edge = pltpu.roll(g_s[s, z, edge, :], 4, 0)
                 out[(8 + s) * LEV + z] = jnp.where(keep, lh_edge, g_edge)
         out[pl.ds(10 * LEV, 6)] = strip_out[:, edge, :]
-
-
-def obs_kernel(cells, m, v, dep, ov, rm_out, h2_out):
+    by_out[...] = b_out[10 * LEV :]
+
+
+def obs_kernel(cells, m, v, dep, ov, rv0, rv1, rm_out, qm_out, h2_out):
     for s in range(2):
         rows, lanes = one_hots(cells[s, 0])
         seen = gather(rows, lanes, v[s].reshape(LEV * CX, CY))
         rm = dep[s, 0] - (ov[s, 0] * m[s, 0] + seen)
         rm_out[s, 0] = rm
         h2_out[s] = scatter(rows, lanes, rm).reshape(LEV, CX, CY)
+        rv = rv0[0] if s == 0 else rv1[...]
+        qm_out[s, 0] = ov[s, 0] * rm + gather(rows, lanes, rv.reshape(LEV * CX, CY))
 
 
 class Place:
@@ -442,9 +445,9 @@
 
 
 def second_kernel(
-    counts, cells, ext, we, wn, lh, own, got, bg, ag, by, ay, zt, zh,
-    mv, h2, rm, ov,
-    rv1_out, rl1_out, rl2_out, f21_out, b20_out, ql1_out, qv1_out, qm_out, dots_out,
+    counts, ext, we, wn, lh, own, got, bg, ag, by, ay, zt, zh,
+    mv,
+    rv1_out, rl1_out, rl2_out, f21_out, b20_out, ql1_out, b21_out, dots_out,
     x_f, x_b, s_f, s_b, coef, scoef, wind, wstrip, extra, estrip,
 ):
     place = Place()
@@ -505,10 +508,7 @@
     for z in range(LEV):
         rl1 = ext[1, z, tile]
         rl1_out[z] = rl1
-        qv = rl1 - x_b[end, z + 1, TOP + HALO : TOP + HALO + CX] + h2[1, z]
-        qv1_out[z] = qv
-        c, q = dots(rv1_out[z], qv)
-        cross, square = cross + c, square + q
+        b21_out[z] = x_b[end, z + 1, TOP + HALO : TOP + HALO + CX]
     coefficients(place, wind, wstrip, coef, scoef, False)
     sweep(place, x_f, s_f, coef, scoef, counts[1])
     for z in range(LEV):
@@ -536,26 +536,12 @@
     for z in range(LEV):
         b20_out[z] = x_b[end, z + 1, TOP + HALO : TOP + HALO + CX]
 
-    for s in range(2):
-        rows, lanes = one_hots(cells[s, 0])
-        if s == 0:
-            field = ext[0, 0:LEV, tile].reshape(LEV * CX, CY)
-        else:
-            field = rv1_out[...].reshape(LEV * CX, CY)
-        seen = gather(rows, lanes, field)
-        r = rm[s, 0]
-        q = ov[s, 0] * r + seen
-        qm_out[s, 0] = q
-        c, q = lane_sum(r * q), lane_sum(q * q)
-        first = iota((8, CY), 0) == 0
-        cross = cross + jnp.where(first, c, 0.0)
-        square = square + jnp.where(first, q, 0.0)
     dots_out[0] = cross
     dots_out[1] = square
 
 
 def dots_kernel(
-    even, odd, rl2, f21, b20, z_own, h2, rv0, dots_in, rl1, rv1, qv1, ql1, qm, rm, m,
+    even, odd, rl2, f21, b20, z_own, h2, rv0, dots_in, rl1, rv1, b21, ql1, qm, rm, m,
     keep_out, send_out,
 ):
     follows = jnp.where(lax.axis_index("tm") == lax.axis_size("tm") - 1, 0.0, 1.0)
@@ -564,7 +550,9 @@
         for s in range(2):
             for k in range(m.shape[-1] // CY):
                 keep_out[6, 2 * i + s, k : k + 1] = kept[s, 0, :, k * CY : (k + 1) * CY]
-    cross, square = dots_in[0], dots_in[1]
+    rm_rows, qm_rows = keep_out[6, 0:2, 0:8], keep_out[6, 2:4, 0:8]
+    cross = dots_in[0] + jnp.sum(rm_rows * qm_rows, 0)
+    square = dots_in[1] + jnp.sum(qm_rows * qm_rows, 0)
     is_odd = lax.axis_index("tm") % 2 == 1
 
     def total(x):
@@ -574,8 +562,11 @@
         rl0 = z_own[64 + 8 * z : 72 + 8 * z].reshape(CX, CY) + jnp.where(is_odd, even[0, z], odd[0, z])
         rv = rv0[0, z]
         qv = rl0 - b20[z] + h2[0, z]
-        for i, kept in enumerate((rl0, rl1[z], rv1[z], qv, qv1[z], ql1[z])):
+        qv1 = rl1[z] - b21[z] + h2[1, z]
+        for i, kept in enumerate((rl0, rl1[z], rv1[z], qv, qv1, ql1[z])):
             keep_out[i, z] = kept
+        cross += total(rv1[z] * qv1)
+        square += total(qv1 * qv1)
         ql = (rv0[1, z] * rl0 + rv) * starts
         rl2z = rl2[z]
         next_mv = jnp.where(is_odd, odd[1, z], even[1, z])
@@ -640,9 +631,9 @@
     edge = 10 * LEV
 
     fields = pltpu.VMEM((2,) + tile, F32)
-    b_send, a_send, own, z_send, lh, g1 = call(
+    b_send, a_send, by_send, own, z_send, lh, g1 = call(
         pack_kernel,
-        [(NBLOCKS, 8, CY)] * 2 + [(6, CX, CY), (136, 8, CY), (2,) + tile, tile],
+        [(NBLOCKS, 8, CY)] * 2 + [(6, 8, CY), (6, CX, CY), (136, 8, CY), (2,) + tile, tile],
         [cells4, m4, l4, f4, mv4, v4, we4, wn4],
         [fields, pltpu.VMEM(obs, jnp.int32), pltpu.VMEM(obs, F32)]
         + [fields] * 6
@@ -656,10 +647,9 @@
     ag = lax.ppermute(a_send, axes, plane(lambda i: i ^ 1, False))
     zt = lax.ppermute(z_send, "tm", down)
     ay_send = jnp.concatenate([got[:, :8], got[:, CX - 8 :]], 1)
-    ay_send, late_cells, by_send = lax.optimization_barrier((ay_send, cells4, b_send[edge:]))
+    ay_send, by_send = lax.optimization_barrier((ay_send, by_send))
     by = lax.ppermute(by_send, axes, plane(pair_b, True))
     ay = lax.ppermute(ay_send, axes, plane(lambda i: i ^ 1, False))
-    rm, h2 = call(obs_kernel, [obs, (2,) + tile], [late_cells, m4, v4, d4, ov4], micros=2.4)
 
     z_edges = jnp.concatenate(
         [
@@ -687,23 +677,25 @@
     ]
     even = lax.ppermute(even_send, "tm", swap(0))
     odd = lax.ppermute(odd_send, "tm", swap(1))
-    rv1, rl1, rl2, f21, b20, ql1, qv1, qm, dots = call(
+    rv1, rl1, rl2, f21, b20, ql1, b21, dots = call(
         second_kernel,
-        [tile] * 7 + [obs, (2, 8, CY)],
-        [counts, cells4, ext, we4, wn4, lh, own, got, bg, ag, by, ay, zt, zh, mv4, h2, rm, ov4],
+        [tile] * 7 + [(2, 8, CY)],
+        [counts, ext, we4, wn4, lh, own, got, bg, ag, by, ay, zt, zh, mv4],
         scratch,
         micros=9.0,
+    )
+    z_f2 = lax.ppermute(f21, "tm", up)
+    rm, qm, h2 = call(
+        obs_kernel, [obs, obs, (2,) + tile], [cells4, m4, v4, d4, ov4, rv0, rv1], micros=3.4
     )
     n = ntm * ngx * ngy
     keep, send = call(
         dots_kernel,
         [(7,) + tile, (n, CY)],
-        [even, odd, rl2, f21, b20, z_send, h2, rv0, dots, rl1, rv1, qv1, ql1, qm, rm, m4],
+        [even, odd, rl2, f21, b20, z_send, h2, rv0, dots, rl1, rv1, b21, ql1, qm, rm, m4],
         micros=0.4,
     )
-    send, late_f21 = lax.optimization_barrier((send, f21))
     sums = lax.all_to_all(send, ("tm", "gx", "gy"), 0, 0, tiled=True)
-    z_f2 = lax.ppermute(late_f21, "tm", up)
     return call(
         last_kernel,
         [l4.shape, obs, l4.shape, l4.shape, obs, l4.shape],

time: 78.4 us -> 81.5 us (1.040); the launches traced: 78.1 us -> 80.2 us
  blocking collectives: 27 us -> 0 us
  starting transfers between devices: 24.7 us -> 42.5 us
  waiting for transfers between devices: 5.41 us -> 15.8 us
  local copies, waits for them, and re-layouts: 0.86 us -> 4.06 us
  Pallas kernels: 19.1 us -> 16.7 us
    all_to_all x1 -> x0, blocking collectives: 27 us -> none  [shards(): sums = lax.all_to_all(send, ('tm', 'gx', 'gy'), 0, 0, tiled=True)]
    all_to_all x0 -> x1, starting transfers between devices: none -> 14.5 us  [shards(): sums = lax.all_to_all(send, ('tm', 'gx', 'gy'), 0, 0, tiled=True)]
    all_to_all x0 -> x1, waiting for transfers between devices: none -> 12.7 us  [shards(): sums = lax.all_to_all(send, ('tm', 'gx', 'gy'), 0, 0, tiled=True)]
    ppermute x1, waiting for transfers between devices: 5.31 us -> 0.01 us  [shards(): even = lax.ppermute(even_send, 'tm', swap(0))]
    unnamed x36 -> x42, local copies, waits for them, and re-layouts: 0.11 us -> 4.05 us
    ppermute x1, waiting for transfers between devices: 0.01 us -> 3.13 us  [shards(): bg = lax.ppermute(b_send, axes, plane(pair_b, False))]
    pallas_call x6, Pallas kernels: 19.1 us -> 16.7 us  [call(): pl.pallas_call(body, out_shape=shapes, in_specs=in_specs, out_specs=[FAR...]
    ppermute x1, starting transfers between devices: 6.82 us -> 8.8 us  [shards(): z_f2 = lax.ppermute(f21, 'tm', up)]
  transfers between devices with their start and end apart: 10 -> 11, of which waited for: 2 -> 2; matrix products, arithmetic and copies ran while one was open for 1% -> 0% of each run, Pallas kernels for 16% -> 13%
where the time goes in v5:
time: 81.5 us; the launch traced here: 80.2 us
  starting transfers between devices  42.5 us (52%)
  Pallas kernels  16.7 us (20%)
  waiting for transfers between devices  15.8 us (19%)
  local copies, waits for them, and re-layouts  4.06 us (5%)
  between operations  1.08 us (1%)
    pallas_call x6, Pallas kernels, call(): pl.pallas_call(body, out_shape=shapes, in_specs=in_specs, out_specs=[FAR...  16.7 us
    all_to_all x1, starting transfers between devices, shards(): sums = lax.all_to_all(send, ('tm', 'gx', 'gy'), 0, 0, tiled=True)  14.5 us
    all_to_all x1, waiting for transfers between devices, shards(): sums = lax.all_to_all(send, ('tm', 'gx', 'gy'), 0, 0, tiled=True)  12.7 us
    ppermute x1, starting transfers between devices, shards(): z_f2 = lax.ppermute(f21, 'tm', up)  8.8 us
    ppermute x1, starting transfers between devices, shards(): bg = lax.ppermute(b_send, axes, plane(pair_b, False))  5.35 us
    unnamed x42, local copies, waits for them, and re-layouts  4.05 us
    ppermute x1, starting transfers between devices, shards(): even = lax.ppermute(even_send, 'tm', swap(0))  4.01 us
    ppermute x1, starting transfers between devices, shards(): by = lax.ppermute(by_send, axes, plane(pair_b, True))  3.98 us
  transfers between devices with their start and end apart: 11, of which 2 were waited for; matrix products, arithmetic and copies ran while one was open for 0% of the time, Pallas kernels for 13%

profile of v5, /device:TPU:1, one launch (start us, length us, event | category | flops | bytes accessed | tf_op | source)
XLA Modules:
  0.0 80.2 jit_solution(14683713648556529575)
XLA Ops:
  0.7 0.0 copy-start.6
  0.7 4.7 %shard_map.154 = (f32[86,8,128]{2,1,0:T(8,128)}, f32[86,8,128]{2,1,0:T(8,128)}, f32[6,8,128]{2,1,0:T(8,128)}, f32[6,64,128]{2,1,0:T(8,128)}, f32[136,8,128]{2,1,...) custom-call(s32[2,1,1,1024]{3,2,1,0:T(1,128)} %cells.1, f32[2,1,1,1024]{3,2,1,0:T(1,128)} %m.3, ...), custom_call_target="tpu_custom_call" | custom-call | flops 2750000128 | bytes 5431296 | tf_op jit(solution)/shard_map/pallas_call | solution.py:37
  5.4 2.2 %collective-permute-start = (f32[6,64,128]{2,1,0:T(8,128)}, f32[6,64,128]{2,1,0:T(8,128)S(1)}, u32[]{:S(2)}, u32[]{:S(2)}) collective-permute-start(f32[6,64,128]{2,1,0:T(8,128)} %get-tuple-element.34.own), channel_id=1, source_target_pairs={{0,1},{1,0},{2,3},{3,2},{4,5},{5,4},{6,7},{7,6},{8,9},{9,8},{10,11... | collective-permute-start | bytes 589832 | tf_op jit(solution)/shard_map/ppermute | solution.py:645
  7.6 5.3 %collective-permute-start.1 = (f32[86,8,128]{2,1,0:T(8,128)}, f32[86,8,128]{2,1,0:T(8,128)S(1)}, u32[]{:S(2)}, u32[]{:S(2)}) collective-permute-start(f32[86,8,128]{2,1,0:T(8,128)} %get-tuple-element.35), channel_id=1, source_target_pairs={{2,4},{3,5},{4,2},{5,3},{6,8},{7,9},{8,6},{9,7},{10,12},{11,13},{1... | collective-permute-start | bytes 1056776 | tf_op jit(solution)/shard_map/ppermute | solution.py:646
  12.9 0.1 collective-permute-start.2
  13.0 1.3 %collective-permute-start.7 = (f32[136,8,128]{2,1,0:T(8,128)}, f32[136,8,128]{2,1,0:T(8,128)S(1)}, u32[]{:S(2)}, u32[]{:S(2)}) collective-permute-start(f32[136,8,128]{2,1,0:T(8,128)} %get-tuple-element.43.z_own), channel_id=1, source_target_pairs={{32,0},{64,32},{96,64},{128,96},{160,128},{192,160},{224,192},{33,... | collective-permute-start | bytes 1671176 | tf_op jit(solution)/shard_map/ppermute | solution.py:648
  14.4 4.0 %collective-permute-start.3 = (f32[6,8,128]{2,1,0:T(8,128)}, f32[6,8,128]{2,1,0:T(8,128)S(1)}, u32[]{:S(2)}, u32[]{:S(2)}) collective-permute-start(f32[6,8,128]{2,1,0:T(8,128)} %get-tuple-element.38), channel_id=1, source_target_pairs={{2,5},{3,4},{4,3},{5,2},{6,9},{7,8},{8,7},{9,6},{10,13},{11,12},{1... | collective-permute-start | bytes 73736 | tf_op jit(solution)/shard_map/ppermute | solution.py:651
  18.4 0.1 collective-permute-start.4
  18.5 3.1 %collective-permute-done.1.bg = f32[86,8,128]{2,1,0:T(8,128)S(1)} collective-permute-done((f32[86,8,128]{2,1,0:T(8,128)}, f32[86,8,128]{2,1,0:T(8,128)S(1)}, u32[]{:S(2)}, u32[]{:S(2)}) %collective-permute-start.1) | collective-permute-done | bytes 352288 | tf_op jit(solution)/shard_map/ppermute | solution.py:646
  21.7 1.3 %collective-permute-start.8 = (f32[45,8,128]{2,1,0:T(8,128)S(1)}, f32[45,8,128]{2,1,0:T(8,128)S(1)}, u32[]{:S(2)}, u32[]{:S(2)}) collective-permute-start(f32[45,8,128]{2,1,0:T(8,128)S(1)} %fusion), channel_id=1, source_target_pairs={{32,0},{64,32},{96,64},{128,96},{160,128},{192,160},{224,192},{33,... | collective-permute-start | bytes 552968 | tf_op jit(solution)/shard_map/ppermute | solution.py:663
  23.1 0.9 %copy-done.8 = f32[6,64,128]{2,1,0:T(8,128)S(1)} copy-done((f32[6,64,128]{2,1,0:T(8,128)S(1)}, f32[6,64,128]{2,1,0:T(8,128)}, u32[]{:S(2)}) %copy-start.8) | copy-done | bytes 196632
  24.0 1.0 %copy-done.14 = f32[2,8,64,128]{3,2,1,0:T(8,128)S(1)} copy-done((f32[2,8,64,128]{3,2,1,0:T(8,128)S(1)}, f32[2,8,64,128]{3,2,1,0:T(8,128)}, u32[]{:S(2)}) %copy-start.14) | copy-done | bytes 524312
  25.0 0.9 %copy-done.16 = f32[8,64,128]{2,1,0:T(8,128)S(1)} copy-done((f32[8,64,128]{2,1,0:T(8,128)S(1)}, f32[8,64,128]{2,1,0:T(8,128)}, u32[]{:S(2)}) %copy-start.16) | copy-done | bytes 262168
  26.0 2.9 %shard_map.155 = (f32[3,9,80,128]{3,2,1,0:T(8,128)S(1)}, f32[2,8,64,128]{3,2,1,0:T(8,128)S(1)}, f32[2,8,64,128]{3,2,1,0:T(8,128)S(1)}, f32[2,8,64,128]{3,2,1,0:T(8,128)S(1)}) custom-call(s32[2]{0:T(128)S(1)} %copy-done.13, f32[2,8,64,128]{3,2,1,0:T(8,128)S(1)} %copy-done.5, f32[2,8,64,128]{3,2,1,0:T(8,128)S(1)} %copy-done.6, ...), custom_call_target="tpu_custom_call" | custom-call | flops 5500000256 | bytes 7258120 | tf_op jit(solution)/shard_map/pallas_call | solution.py:37
  28.9 4.0 %collective-permute-start.5 = (f32[2,8,64,128]{3,2,1,0:T(8,128)S(1)}, f32[2,8,64,128]{3,2,1,0:T(8,128)S(1)}, u32[]{:S(2)}, u32[]{:S(2)}) collective-permute-start(f32[2,8,64,128]{3,2,1,0:T(8,128)S(1)} %get-tuple-element.40), channel_id=1, source_target_pairs={{0,32},{64,96},{128,160},{192,224},{32,0},{96,64},{160,128},{224,1... | collective-permute-start | bytes 1572872 | tf_op jit(solution)/shard_map/ppermute | solution.py:678
  32.9 0.9 %collective-permute-start.6 = (f32[2,8,64,128]{3,2,1,0:T(8,128)S(1)}, f32[2,8,64,128]{3,2,1,0:T(8,128)S(1)}, u32[]{:S(2)}, u32[]{:S(2)}) collective-permute-start(f32[2,8,64,128]{3,2,1,0:T(8,128)S(1)} %get-tuple-element.41), channel_id=1, source_target_pairs={{32,64},{96,128},{160,192},{64,32},{128,96},{192,160},{33,65},{97,... | collective-permute-start | bytes 1572872 | tf_op jit(solution)/shard_map/ppermute | solution.py:679
  33.8 4.2 %shard_map.156 = (f32[8,64,128]{2,1,0:T(8,128)S(1)}, f32[8,64,128]{2,1,0:T(8,128)S(1)}, f32[8,64,128]{2,1,0:T(8,128)S(1)}, f32[8,64,128]{2,1,0:T(8,128)S(1)}, f3...) custom-call(s32[2]{0:T(128)S(1)} %copy-done.13, ...), custom_call_target="tpu_custom_call" | custom-call | flops 9900000256 | bytes 6959112 | tf_op jit(solution)/shard_map/pallas_call | solution.py:37
  38.1 8.8 %collective-permute-start.9 = (f32[8,64,128]{2,1,0:T(8,128)S(1)}, f32[8,64,128]{2,1,0:T(8,128)S(1)}, u32[]{:S(2)}, u32[]{:S(2)}) collective-permute-start(f32[8,64,128]{2,1,0:T(8,128)S(1)} %get-tuple-element.45.f21), channel_id=1, source_target_pairs={{0,32},{32,64},{64,96},{96,128},{128,160},{160,192},{192,224},{1,3... | collective-permute-start | bytes 786440 | tf_op jit(solution)/shard_map/ppermute | solution.py:687
  46.9 2.4 %shard_map.157 = (f32[2,1,1,1024]{3,2,1,0:T(1,128)S(1)}, f32[2,1,1,1024]{3,2,1,0:T(1,128)S(1)}, f32[2,8,64,128]{3,2,1,0:T(8,128)S(1)}) custom-call(s32[2,1,1,1024]{3,2,1,0:T(1,128)S(1)} %copy-done.10, f32[2,1,1,1024]{3,2,1,0:T(1,128)S(1)} %copy-done.1, f32[2,8,64,128]{3,2,1,0:T(8,128)S(1)} %copy-done.5, f32[2,1,1,1024]{3,2,1,0:T(1,128)S(1)} %copy-done.11, ...), custom_call_target="tpu_custom_call" | custom-call | flops 3740000000 | bytes 1884160 | tf_op jit(solution)/shard_map/pallas_call | solution.py:37
  49.3 1.1 %shard_map.158 = (f32[7,8,64,128]{3,2,1,0:T(8,128)S(1)}, f32[256,128]{1,0:T(8,128)}) custom-call(f32[2,8,64,128]{3,2,1,0:T(8,128)S(1)} %collective-permute-done.5.even, f32[2,8,64,128]{3,2,1,0:T(8,128)S(1)} %collective-permute-done.6.odd, f32[8,64,128]{2,1,0:T(8,128)S(1)} %get-tuple-element.44.rl2, f32[8,64,128]{2,1,0:T(8,128)S(1)} %get-tuple-element.45.f21, ...), custom_call_target="tpu_custom_call" | custom-call | flops 440000000 | bytes 6488064 | tf_op jit(solution)/shard_map/pallas_call | solution.py:37
  50.4 14.5 %all-to-all-start = ((f32[256,1,128]{2,1,0:T(1,128)}), f32[256,1,128]{2,1,0:T(1,128)S(1)}, u32[]{:S(2)}, u32[]{:S(2)}) async-start(f32[256,1,128]{2,1,0:T(1,128)} %bitcast.3), calls=%async_computation | async-start | bytes 262144 | tf_op jit(solution)/shard_map/all_to_all | solution.py:698
  64.9 12.7 %all-to-all-done = f32[256,1,128]{2,1,0:T(1,128)S(1)} async-done(((f32[256,1,128]{2,1,0:T(1,128)}), f32[256,1,128]{2,1,0:T(1,128)S(1)}, u32[]{:S(2)}, u32[]{:S(2)}) %all-to-all-start) | async-done | bytes 131104 | tf_op jit(solution)/shard_map/all_to_all | solution.py:698
  77.6 1.0 %copy-done.7 = f32[2,8,64,128]{3,2,1,0:T(8,128)S(1)} copy-done((f32[2,8,64,128]{3,2,1,0:T(8,128)S(1)}, f32[2,8,64,128]{3,2,1,0:T(8,128)}, u32[]{:S(2)}) %copy-start.7) | copy-done | bytes 524312
  78.7 1.5 %shard_map.159 = (f32[2,8,64,128]{3,2,1,0:T(8,128)}, f32[2,1,1,1024]{3,2,1,0:T(1,128)}, f32[2,8,64,128]{3,2,1,0:T(8,128)}, f32[2,8,64,128]{3,2,1,0:T(8,128)}, f3...) custom-call(f32[256,128]{1,0:T(8,128)S(1)} %bitcast.12, f32[2,8,64,128]{3,2,1,0:T(8,128)S(1)} %copy-done.7, ...), custom_call_target="tpu_custom_call" | custom-call | flops 1650000000 | bytes 5914624 | tf_op jit(solution)/shard_map/pallas_call | solution.py:37
  (49 shorter events, 0.1 us)
Async XLA Ops:
  0.6 22.4 %copy-start.5 = (f32[2,8,64,128]{3,2,1,0:T(8,128)S(1)}, f32[2,8,64,128]{3,2,1,0:T(8,128)}, u32[]{:S(2)}) copy-start(f32[2,8,64,128]{3,2,1,0:T(8,128)} %v.5) | copy-start | bytes 1572868
  0.6 22.4 %copy-start.3 = (f32[2,8,64,128]{3,2,1,0:T(8,128)S(1)}, f32[2,8,64,128]{3,2,1,0:T(8,128)}, u32[]{:S(2)}) copy-start(f32[2,8,64,128]{3,2,1,0:T(8,128)} %wn.3) | copy-start | bytes 1572868
  0.7 22.4 %copy-start.2 = (f32[2,8,64,128]{3,2,1,0:T(8,128)S(1)}, f32[2,8,64,128]{3,2,1,0:T(8,128)}, u32[]{:S(2)}) copy-start(f32[2,8,64,128]{3,2,1,0:T(8,128)} %we.3) | copy-start | bytes 1572868
  0.7 22.4 %copy-start.4 = (f32[2,8,64,128]{3,2,1,0:T(8,128)S(1)}, f32[2,8,64,128]{3,2,1,0:T(8,128)}, u32[]{:S(2)}) copy-start(f32[2,8,64,128]{3,2,1,0:T(8,128)} %mv.3) | copy-start | bytes 1572868
  0.7 22.4 %copy-start.6 = (f32[2,8,64,128]{3,2,1,0:T(8,128)S(1)}, f32[2,8,64,128]{3,2,1,0:T(8,128)}, u32[]{:S(2)}) copy-start(f32[2,8,64,128]{3,2,1,0:T(8,128)} %l.3) | copy-start | bytes 1572868
  0.7 22.4 %copy-start.13 = (s32[2]{0:T(128)S(1)}, s32[2]{0:T(128)}, u32[]{:S(2)}) copy-start(s32[2]{0:T(128)} %counts.3) | copy-start | bytes 28
  5.4 9.0 %collective-permute-start = (f32[6,64,128]{2,1,0:T(8,128)}, f32[6,64,128]{2,1,0:T(8,128)S(1)}, u32[]{:S(2)}, u32[]{:S(2)}) collective-permute-start(f32[6,64,128]{2,1,0:T(8,128)} %get-tuple-element.34.own), channel_id=1, source_target_pairs={{0,1},{1,0},{2,3},{3,2},{4,5},{5,4},{6,7},{7,6},{8,9},{9,8},{10,11... | collective-permute-start | bytes 589832 | tf_op jit(solution)/shard_map/ppermute | solution.py:645
  7.6 14.0 %collective-permute-start.1 = (f32[86,8,128]{2,1,0:T(8,128)}, f32[86,8,128]{2,1,0:T(8,128)S(1)}, u32[]{:S(2)}, u32[]{:S(2)}) collective-permute-start(f32[86,8,128]{2,1,0:T(8,128)} %get-tuple-element.35), channel_id=1, source_target_pairs={{2,4},{3,5},{4,2},{5,3},{6,8},{7,9},{8,6},{9,7},{10,12},{11,13},{1... | collective-permute-start | bytes 1056776 | tf_op jit(solution)/shard_map/ppermute | solution.py:646
  12.9 8.7 %collective-permute-start.2 = (f32[86,8,128]{2,1,0:T(8,128)}, f32[86,8,128]{2,1,0:T(8,128)S(1)}, u32[]{:S(2)}, u32[]{:S(2)}) collective-permute-start(f32[86,8,128]{2,1,0:T(8,128)} %get-tuple-element.36), channel_id=1, source_target_pairs={{0,2},{1,3},{2,0},{3,1},{4,6},{5,7},{6,4},{7,5},{8,10},{9,11},{10,... | collective-permute-start | bytes 1056776 | tf_op jit(solution)/shard_map/ppermute | solution.py:647
  13.0 20.7 %collective-permute-start.7 = (f32[136,8,128]{2,1,0:T(8,128)}, f32[136,8,128]{2,1,0:T(8,128)S(1)}, u32[]{:S(2)}, u32[]{:S(2)}) collective-permute-start(f32[136,8,128]{2,1,0:T(8,128)} %get-tuple-element.43.z_own), channel_id=1, source_target_pairs={{32,0},{64,32},{96,64},{128,96},{160,128},{192,160},{224,192},{33,... | collective-permute-start | bytes 1671176 | tf_op jit(solution)/shard_map/ppermute | solution.py:648
  14.4 7.3 %collective-permute-start.3 = (f32[6,8,128]{2,1,0:T(8,128)}, f32[6,8,128]{2,1,0:T(8,128)S(1)}, u32[]{:S(2)}, u32[]{:S(2)}) collective-permute-start(f32[6,8,128]{2,1,0:T(8,128)} %get-tuple-element.38), channel_id=1, source_target_pairs={{2,5},{3,4},{4,3},{5,2},{6,9},{7,8},{8,7},{9,6},{10,13},{11,12},{1... | collective-permute-start | bytes 73736 | tf_op jit(solution)/shard_map/ppermute | solution.py:651
  18.4 3.3 %collective-permute-start.4 = (f32[6,16,128]{2,1,0:T(8,128)S(1)}, f32[6,16,128]{2,1,0:T(8,128)S(1)}, u32[]{:S(2)}, u32[]{:S(2)}) collective-permute-start(f32[6,16,128]{2,1,0:T(8,128)S(1)} %pad_maximum_fusion), channel_id=1, source_target_pairs={{0,2},{1,3},{2,0},{3,1},{4,6},{5,7},{6,4},{7,5},{8,10},{9,11},{10,... | collective-permute-start | bytes 147464 | tf_op jit(solution)/shard_map/ppermute | solution.py:652
  21.7 12.0 %collective-permute-start.8 = (f32[45,8,128]{2,1,0:T(8,128)S(1)}, f32[45,8,128]{2,1,0:T(8,128)S(1)}, u32[]{:S(2)}, u32[]{:S(2)}) collective-permute-start(f32[45,8,128]{2,1,0:T(8,128)S(1)} %fusion), channel_id=1, source_target_pairs={{32,0},{64,32},{96,64},{128,96},{160,128},{192,160},{224,192},{33,... | collective-permute-start | bytes 552968 | tf_op jit(solution)/shard_map/ppermute | solution.py:663
  26.0 7.8 %copy-start.9 = (f32[6,64,128]{2,1,0:T(8,128)S(1)}, f32[6,64,128]{2,1,0:T(8,128)}, u32[]{:S(2)}) copy-start(f32[6,64,128]{2,1,0:T(8,128)} %get-tuple-element.34.own) | copy-start | bytes 589828
  26.0 7.8 %copy-start.15 = (f32[2,8,64,128]{3,2,1,0:T(8,128)S(1)}, f32[2,8,64,128]{3,2,1,0:T(8,128)}, u32[]{:S(2)}) copy-start(f32[2,8,64,128]{3,2,1,0:T(8,128)} %get-tuple-element.32.lh) | copy-start | bytes 1572868
  28.9 20.4 %collective-permute-start.5 = (f32[2,8,64,128]{3,2,1,0:T(8,128)S(1)}, f32[2,8,64,128]{3,2,1,0:T(8,128)S(1)}, u32[]{:S(2)}, u32[]{:S(2)}) collective-permute-start(f32[2,8,64,128]{3,2,1,0:T(8,128)S(1)} %get-tuple-element.40), channel_id=1, source_target_pairs={{0,32},{64,96},{128,160},{192,224},{32,0},{96,64},{160,128},{224,1... | collective-permute-start | bytes 1572872 | tf_op jit(solution)/shard_map/ppermute | solution.py:678
  32.9 16.4 %collective-permute-start.6 = (f32[2,8,64,128]{3,2,1,0:T(8,128)S(1)}, f32[2,8,64,128]{3,2,1,0:T(8,128)S(1)}, u32[]{:S(2)}, u32[]{:S(2)}) collective-permute-start(f32[2,8,64,128]{3,2,1,0:T(8,128)S(1)} %get-tuple-element.41), channel_id=1, source_target_pairs={{32,64},{96,128},{160,192},{64,32},{128,96},{192,160},{33,65},{97,... | collective-permute-start | bytes 1572872 | tf_op jit(solution)/shard_map/ppermute | solution.py:679
  33.8 13.1 %copy-start.1 = (f32[2,1,1,1024]{3,2,1,0:T(1,128)S(1)}, f32[2,1,1,1024]{3,2,1,0:T(1,128)}, u32[]{:S(2)}) copy-start(f32[2,1,1,1024]{3,2,1,0:T(1,128)} %m.3) | copy-start | bytes 24580
  33.8 13.1 %copy-start.10 = (s32[2,1,1,1024]{3,2,1,0:T(1,128)S(1)}, s32[2,1,1,1024]{3,2,1,0:T(1,128)}, u32[]{:S(2)}) copy-start(s32[2,1,1,1024]{3,2,1,0:T(1,128)} %cells.1) | copy-start | bytes 24580
  33.8 13.1 %copy-start.11 = (f32[2,1,1,1024]{3,2,1,0:T(1,128)S(1)}, f32[2,1,1,1024]{3,2,1,0:T(1,128)}, u32[]{:S(2)}) copy-start(f32[2,1,1,1024]{3,2,1,0:T(1,128)} %dep.1) | copy-start | bytes 24580
  33.8 13.1 %copy-start.12 = (f32[2,1,1,1024]{3,2,1,0:T(1,128)S(1)}, f32[2,1,1,1024]{3,2,1,0:T(1,128)}, u32[]{:S(2)}) copy-start(f32[2,1,1,1024]{3,2,1,0:T(1,128)} %ov.1) | copy-start | bytes 24580
  38.1 26.8 %collective-permute-start.9 = (f32[8,64,128]{2,1,0:T(8,128)S(1)}, f32[8,64,128]{2,1,0:T(8,128)S(1)}, u32[]{:S(2)}, u32[]{:S(2)}) collective-permute-start(f32[8,64,128]{2,1,0:T(8,128)S(1)} %get-tuple-element.45.f21), channel_id=1, source_target_pairs={{0,32},{32,64},{64,96},{96,128},{128,160},{160,192},{192,224},{1,3... | collective-permute-start | bytes 786440 | tf_op jit(solution)/shard_map/ppermute | solution.py:687
  46.9 2.4 %copy-start = (f32[136,8,128]{2,1,0:T(8,128)S(1)}, f32[136,8,128]{2,1,0:T(8,128)}, u32[]{:S(2)}) copy-start(f32[136,8,128]{2,1,0:T(8,128)} %get-tuple-element.43.z_own) | copy-start | bytes 1671172
  50.4 27.2 %all-to-all-start = ((f32[256,1,128]{2,1,0:T(1,128)}), f32[256,1,128]{2,1,0:T(1,128)S(1)}, u32[]{:S(2)}, u32[]{:S(2)}) async-start(f32[256,1,128]{2,1,0:T(1,128)} %bitcast.3), calls=%async_computation | async-start | bytes 262144 | tf_op jit(solution)/shard_map/all_to_all | solution.py:698
  (4 other events, 4.0 us)

commit v6 on v5

--- a/solution.py
+++ b/solution.py
@@ -99,8 +99,8 @@
 
 def pack_kernel(
     cells_h, m_h, l_h, f_h, mv_h, v_h, we_h, wn_h,
-    b_out, a_out, by_out, strip_out, z_out, lh_out, g1_out,
-    g_s, cells, m, l, f, mv, v, we, wn, sems,
+    b_out, a_out, by_out, strip_out, z_out,
+    lh_out, g_s, cells, m, l, f, mv, v, we, wn, sems,
 ):
     far = (cells_h, m_h, l_h, f_h, mv_h, v_h, we_h, wn_h)
     near = (cells, m, l, f, mv, v, we, wn)
@@ -120,7 +120,6 @@
                 copy.wait()
         lh_out[s] = l[s] + h.reshape(LEV, CX, CY)
         g_s[s] = f[s] - mv[s] * l[s] - v[s]
-    g1_out[...] = g_s[1]
     for z in range(LEV):
         for i in range(CX // 8):
             z_out[z * 8 + i] = l[0, z, 8 * i : 8 * i + 8]
@@ -161,6 +160,14 @@
                 out[(8 + s) * LEV + z] = jnp.where(keep, lh_edge, g_edge)
         out[pl.ds(10 * LEV, 6)] = strip_out[:, edge, :]
     by_out[...] = b_out[10 * LEV :]
+
+
+def local_kernel(cells, m, l, f, mv, v, strips, lh_out, g1_out, own_out):
+    for s in range(2):
+        rows, lanes = one_hots(cells[s, 0])
+        lh_out[s] = l[s] + scatter(rows, lanes, m[s, 0]).reshape(LEV, CX, CY)
+    g1_out[...] = f[1] - mv[1] * l[1] - v[1]
+    own_out[...] = strips[...]
 
 
 def obs_kernel(cells, m, v, dep, ov, rv0, rv1, rm_out, qm_out, h2_out):
@@ -631,26 +638,32 @@
     edge = 10 * LEV
 
     fields = pltpu.VMEM((2,) + tile, F32)
-    b_send, a_send, by_send, own, z_send, lh, g1 = call(
+    b_send, a_send, by_send, strips, z_send = call(
         pack_kernel,
-        [(NBLOCKS, 8, CY)] * 2 + [(6, 8, CY), (6, CX, CY), (136, 8, CY), (2,) + tile, tile],
+        [(NBLOCKS, 8, CY)] * 2 + [(6, 8, CY), (6, CX, CY), (136, 8, CY)],
         [cells4, m4, l4, f4, mv4, v4, we4, wn4],
-        [fields, pltpu.VMEM(obs, jnp.int32), pltpu.VMEM(obs, F32)]
+        [fields, fields, pltpu.VMEM(obs, jnp.int32), pltpu.VMEM(obs, F32)]
         + [fields] * 6
         + [pltpu.SemaphoreType.DMA((8,))],
         micros=2.5,
         fetched=range(8),
         limit=PACK_LIMIT,
     )
-    got = lax.ppermute(own, axes, plane(lambda i: i, True))
+    got = lax.ppermute(strips, axes, plane(lambda i: i, True))
     bg = lax.ppermute(b_send, axes, plane(pair_b, False))
     ag = lax.ppermute(a_send, axes, plane(lambda i: i ^ 1, False))
     zt = lax.ppermute(z_send, "tm", down)
     ay_send = jnp.concatenate([got[:, :8], got[:, CX - 8 :]], 1)
-    ay_send, by_send = lax.optimization_barrier((ay_send, by_send))
+    ay_send, by_send, late_cells = lax.optimization_barrier((ay_send, by_send, cells4))
     by = lax.ppermute(by_send, axes, plane(pair_b, True))
     ay = lax.ppermute(ay_send, axes, plane(lambda i: i ^ 1, False))
 
+    lh, g1, own = call(
+        local_kernel,
+        [(2,) + tile, tile, strips.shape],
+        [late_cells, m4, l4, f4, mv4, v4, strips],
+        micros=1.0,
+    )
     z_edges = jnp.concatenate(
         [
             bg[2 * LEV : 3 * LEV], bg[8 * LEV : 9 * LEV],

time: 81.5 us -> 80.1 us (0.983)
  Pallas kernels: 16.7 us -> 24.1 us
  starting transfers between devices: 42.5 us -> 35.2 us
  local copies, waits for them, and re-layouts: 4.06 us -> 2.06 us
  waiting for transfers between devices: 15.8 us -> 17 us
    ppermute x1, starting transfers between devices: 8.8 us -> 1.36 us  [shards(): z_f2 = lax.ppermute(f21, 'tm', up)]
    pallas_call x6 -> x7, Pallas kernels: 16.7 us -> 24.1 us  [call(): pl.pallas_call(body, out_shape=shapes, in_specs=in_specs, out_specs=[FAR...]
    all_to_all x1, starting transfers between devices: 14.5 us -> 17.8 us  [shards(): sums = lax.all_to_all(send, ('tm', 'gx', 'gy'), 0, 0, tiled=True)]
    ppermute x1, starting transfers between devices: 4.01 us -> 0.75 us  [shards(): even = lax.ppermute(even_send, 'tm', swap(0))]
    ppermute x1, waiting for transfers between devices: 0.01 us -> 3.16 us  [shards(): zh = lax.ppermute(z_edges, 'tm', down)]
    ppermute x1, waiting for transfers between devices: 3.13 us -> 1.11 us  [shards(): bg = lax.ppermute(b_send, axes, plane(pair_b, False))]
    unnamed x42 -> x36, local copies, waits for them, and re-layouts: 4.05 us -> 2.05 us
  transfers between devices with their start and end apart: 11 -> 11, of which waited for: 2 -> 3; matrix products, arithmetic and copies ran while one was open for 0% -> 0% of each run, Pallas kernels for 13% -> 23%
where the time goes in v6:
time: 80.1 us; the launch traced here: 79.4 us
  starting transfers between devices  35.2 us (44%)
  Pallas kernels  24.1 us (30%)
  waiting for transfers between devices  17 us (21%)
  local copies, waits for them, and re-layouts  2.06 us (3%)
  between operations  1.05 us (1%)
    pallas_call x7, Pallas kernels, call(): pl.pallas_call(body, out_shape=shapes, in_specs=in_specs, out_specs=[FAR...  24.1 us
    all_to_all x1, starting transfers between devices, shards(): sums = lax.all_to_all(send, ('tm', 'gx', 'gy'), 0, 0, tiled=True)  17.8 us
    all_to_all x1, waiting for transfers between devices, shards(): sums = lax.all_to_all(send, ('tm', 'gx', 'gy'), 0, 0, tiled=True)  12.7 us
    ppermute x1, starting transfers between devices, shards(): bg = lax.ppermute(b_send, axes, plane(pair_b, False))  5.35 us
    ppermute x1, starting transfers between devices, shards(): by = lax.ppermute(by_send, axes, plane(pair_b, True))  4.11 us
    ppermute x1, waiting for transfers between devices, shards(): zh = lax.ppermute(z_edges, 'tm', down)  3.16 us
    ppermute x1, starting transfers between devices, shards(): got = lax.ppermute(strips, axes, plane(lambda i: i, True))  2.21 us
    unnamed x36, local copies, waits for them, and re-layouts  2.05 us
  transfers between devices with their start and end apart: 11, of which 3 were waited for; matrix products, arithmetic and copies ran while one was open for 0% of the time, Pallas kernels for 23%

profile of v6, /device:TPU:1, one launch (start us, length us, event | category | flops | bytes accessed | tf_op | source)
XLA Modules:
  0.0 79.4 jit_solution(2956267845480932266)
XLA Ops:
  0.7 4.5 %shard_map.154 = (f32[86,8,128]{2,1,0:T(8,128)}, f32[86,8,128]{2,1,0:T(8,128)}, f32[6,8,128]{2,1,0:T(8,128)}, f32[6,64,128]{2,1,0:T(8,128)}, f32[136,8,128]{2,1,0:T(8,128)}) custom-call(s32[2,1,1,1024]{3,2,1,0:T(1,128)} %cells.2, f32[2,1,1,1024]{3,2,1,0:T(1,128)} %m.5, f32[2,8,64,128]{3,2,1,0:T(8,128)} %l.5, f32[2,8,64,128]{3,2,1,0:T(8,128)} %f.1, ...), custom_call_target="tpu_custom_call" | custom-call | flops 2750000128 | bytes 4644864 | tf_op jit(solution)/shard_map/pallas_call | solution.py:37
  5.2 2.2 %collective-permute-start = (f32[6,64,128]{2,1,0:T(8,128)}, f32[6,64,128]{2,1,0:T(8,128)S(1)}, u32[]{:S(2)}, u32[]{:S(2)}) collective-permute-start(f32[6,64,128]{2,1,0:T(8,128)} %get-tuple-element.34.strips), channel_id=1, source_target_pairs={{0,1},{1,0},{2,3},{3,2},{4,5},{5,4},{6,7},{7,6},{8,9},{9,8},{10,11... | collective-permute-start | bytes 589832 | tf_op jit(solution)/shard_map/ppermute | solution.py:652
  7.4 5.3 %collective-permute-start.1 = (f32[86,8,128]{2,1,0:T(8,128)}, f32[86,8,128]{2,1,0:T(8,128)S(1)}, u32[]{:S(2)}, u32[]{:S(2)}) collective-permute-start(f32[86,8,128]{2,1,0:T(8,128)} %get-tuple-element.40), channel_id=1, source_target_pairs={{2,4},{3,5},{4,2},{5,3},{6,8},{7,9},{8,6},{9,7},{10,12},{11,13},{1... | collective-permute-start | bytes 1056776 | tf_op jit(solution)/shard_map/ppermute | solution.py:653
  12.8 0.1 collective-permute-start.2
  12.9 1.3 %collective-permute-start.7 = (f32[136,8,128]{2,1,0:T(8,128)}, f32[136,8,128]{2,1,0:T(8,128)S(1)}, u32[]{:S(2)}, u32[]{:S(2)}) collective-permute-start(f32[136,8,128]{2,1,0:T(8,128)} %get-tuple-element.47.z_own), channel_id=1, source_target_pairs={{32,0},{64,32},{96,64},{128,96},{160,128},{192,160},{224,192},{33,... | collective-permute-start | bytes 1671176 | tf_op jit(solution)/shard_map/ppermute | solution.py:655
  14.2 0.0 copy-start.13
  14.3 4.1 %collective-permute-start.3 = (f32[6,8,128]{2,1,0:T(8,128)}, f32[6,8,128]{2,1,0:T(8,128)S(1)}, u32[]{:S(2)}, u32[]{:S(2)}) collective-permute-start(f32[6,8,128]{2,1,0:T(8,128)} %get-tuple-element.42), channel_id=1, source_target_pairs={{2,5},{3,4},{4,3},{5,2},{6,9},{7,8},{8,7},{9,6},{10,13},{11,12},{1... | collective-permute-start | bytes 73736 | tf_op jit(solution)/shard_map/ppermute | solution.py:658
  18.4 0.1 collective-permute-start.4
  18.5 0.9 %copy-done.9 = f32[6,64,128]{2,1,0:T(8,128)S(1)} copy-done((f32[6,64,128]{2,1,0:T(8,128)S(1)}, f32[6,64,128]{2,1,0:T(8,128)}, u32[]{:S(2)}) %copy-start.9) | copy-done | bytes 196632
  19.5 0.9 %shard_map.155 = (f32[2,8,64,128]{3,2,1,0:T(8,128)S(1)}, f32[8,64,128]{2,1,0:T(8,128)S(1)}, f32[6,64,128]{2,1,0:T(8,128)S(1)}) custom-call(s32[2,1,1,1024]{3,2,1,0:T(1,128)S(1)} %copy-done.10, f32[2,1,1,1024]{3,2,1,0:T(1,128)S(1)} %copy-done.1, f32[2,8,64,128]{3,2,1,0:T(8,128)S(1)} %copy-done.7, f32[2,8,64,128]{3,2,1,0:T(8,128)S(1)} %copy-done.2, ...), custom_call_target="tpu_custom_call" | custom-call | flops 1100000000 | bytes 3293184 | tf_op jit(solution)/shard_map/pallas_call | solution.py:37
  20.3 1.1 %collective-permute-done.1.bg = f32[86,8,128]{2,1,0:T(8,128)S(1)} collective-permute-done((f32[86,8,128]{2,1,0:T(8,128)}, f32[86,8,128]{2,1,0:T(8,128)S(1)}, u32[]{:S(2)}, u32[]{:S(2)}) %collective-permute-start.1) | collective-permute-done | bytes 352288 | tf_op jit(solution)/shard_map/ppermute | solution.py:653
  21.6 1.3 %collective-permute-start.8 = (f32[45,8,128]{2,1,0:T(8,128)S(1)}, f32[45,8,128]{2,1,0:T(8,128)S(1)}, u32[]{:S(2)}, u32[]{:S(2)}) collective-permute-start(f32[45,8,128]{2,1,0:T(8,128)S(1)} %fusion), channel_id=1, source_target_pairs={{32,0},{64,32},{96,64},{128,96},{160,128},{192,160},{224,192},{33,... | collective-permute-start | bytes 552968 | tf_op jit(solution)/shard_map/ppermute | solution.py:676
  22.9 5.4 %shard_map.156 = (f32[3,9,80,128]{3,2,1,0:T(8,128)S(1)}, f32[2,8,64,128]{3,2,1,0:T(8,128)S(1)}, f32[2,8,64,128]{3,2,1,0:T(8,128)S(1)}, f32[2,8,64,128]{3,2,1,0:T(8,128)S(1)}) custom-call(s32[2]{0:T(128)S(1)} %copy-done.13, f32[2,8,64,128]{3,2,1,0:T(8,128)S(1)} %copy-done.6, f32[2,8,64,128]{3,2,1,0:T(8,128)S(1)} %copy-done.7, ...), custom_call_target="tpu_custom_call" | custom-call | flops 5500000256 | bytes 7258120 | tf_op jit(solution)/shard_map/pallas_call | solution.py:37
  28.3 0.7 collective-permute-start.5
  29.0 0.9 %collective-permute-start.6 = (f32[2,8,64,128]{3,2,1,0:T(8,128)S(1)}, f32[2,8,64,128]{3,2,1,0:T(8,128)S(1)}, u32[]{:S(2)}, u32[]{:S(2)}) collective-permute-start(f32[2,8,64,128]{3,2,1,0:T(8,128)S(1)} %get-tuple-element.45), channel_id=1, source_target_pairs={{32,64},{96,128},{160,192},{64,32},{128,96},{192,160},{33,65},{97,... | collective-permute-start | bytes 1572872 | tf_op jit(solution)/shard_map/ppermute | solution.py:692
  29.9 3.2 %collective-permute-done.8.zh = f32[45,8,128]{2,1,0:T(8,128)S(1)} collective-permute-done((f32[45,8,128]{2,1,0:T(8,128)S(1)}, f32[45,8,128]{2,1,0:T(8,128)S(1)}, u32[]{:S(2)}, u32[]{:S(2)}) %collective-permute-start.8) | collective-permute-done | bytes 184352 | tf_op jit(solution)/shard_map/ppermute | solution.py:676
  33.0 8.4 %shard_map.157 = (f32[8,64,128]{2,1,0:T(8,128)S(1)}, f32[8,64,128]{2,1,0:T(8,128)S(1)}, f32[8,64,128]{2,1,0:T(8,128)S(1)}, f32[8,64,128]{2,1,0:T(8,128)S(1)}, f3...) custom-call(s32[2]{0:T(128)S(1)} %copy-done.13, ...), custom_call_target="tpu_custom_call" | custom-call | flops 9900000256 | bytes 6959112 | tf_op jit(solution)/shard_map/pallas_call | solution.py:37
  41.5 1.4 %collective-permute-start.9 = (f32[8,64,128]{2,1,0:T(8,128)S(1)}, f32[8,64,128]{2,1,0:T(8,128)S(1)}, u32[]{:S(2)}, u32[]{:S(2)}) collective-permute-start(f32[8,64,128]{2,1,0:T(8,128)S(1)} %get-tuple-element.49.f21), channel_id=1, source_target_pairs={{0,32},{32,64},{64,96},{96,128},{128,160},{160,192},{192,224},{1,3... | collective-permute-start | bytes 786440 | tf_op jit(solution)/shard_map/ppermute | solution.py:700
  42.9 2.4 %shard_map.158 = (f32[2,1,1,1024]{3,2,1,0:T(1,128)S(1)}, f32[2,1,1,1024]{3,2,1,0:T(1,128)S(1)}, f32[2,8,64,128]{3,2,1,0:T(8,128)S(1)}) custom-call(s32[2,1,1,1024]{3,2,1,0:T(1,128)S(1)} %copy-done.10, f32[2,1,1,1024]{3,2,1,0:T(1,128)S(1)} %copy-done.1, f32[2,8,64,128]{3,2,1,0:T(8,128)S(1)} %copy-done.6, f32[2,1,1,1024]{3,2,1,0:T(1,128)S(1)} %copy-done.11, ...), custom_call_target="tpu_custom_call" | custom-call | flops 3740000000 | bytes 1884160 | tf_op jit(solution)/shard_map/pallas_call | solution.py:37
  45.2 1.1 %shard_map.159 = (f32[7,8,64,128]{3,2,1,0:T(8,128)S(1)}, f32[256,128]{1,0:T(8,128)}) custom-call(f32[2,8,64,128]{3,2,1,0:T(8,128)S(1)} %collective-permute-done.5.even, f32[2,8,64,128]{3,2,1,0:T(8,128)S(1)} %collective-permute-done.6.odd, f32[8,64,128]{2,1,0:T(8,128)S(1)} %get-tuple-element.48.rl2, f32[8,64,128]{2,1,0:T(8,128)S(1)} %get-tuple-element.49.f21, ...), custom_call_target="tpu_custom_call" | custom-call | flops 440000000 | bytes 6488064 | tf_op jit(solution)/shard_map/pallas_call | solution.py:37
  46.3 17.8 %all-to-all-start = ((f32[256,1,128]{2,1,0:T(1,128)}), f32[256,1,128]{2,1,0:T(1,128)S(1)}, u32[]{:S(2)}, u32[]{:S(2)}) async-start(f32[256,1,128]{2,1,0:T(1,128)} %bitcast.3), calls=%async_computation | async-start | bytes 262144 | tf_op jit(solution)/shard_map/all_to_all | solution.py:711
  64.1 12.7 %all-to-all-done = f32[256,1,128]{2,1,0:T(1,128)S(1)} async-done(((f32[256,1,128]{2,1,0:T(1,128)}), f32[256,1,128]{2,1,0:T(1,128)S(1)}, u32[]{:S(2)}, u32[]{:S(2)}) %all-to-all-start) | async-done | bytes 131104 | tf_op jit(solution)/shard_map/all_to_all | solution.py:711
  76.8 1.0 %copy-done.8 = f32[2,8,64,128]{3,2,1,0:T(8,128)S(1)} copy-done((f32[2,8,64,128]{3,2,1,0:T(8,128)S(1)}, f32[2,8,64,128]{3,2,1,0:T(8,128)}, u32[]{:S(2)}) %copy-start.8) | copy-done | bytes 524312
  77.8 1.5 %shard_map.160 = (f32[2,8,64,128]{3,2,1,0:T(8,128)}, f32[2,1,1,1024]{3,2,1,0:T(1,128)}, f32[2,8,64,128]{3,2,1,0:T(8,128)}, f32[2,8,64,128]{3,2,1,0:T(8,128)}, f3...) custom-call(f32[256,128]{1,0:T(8,128)S(1)} %bitcast.12, f32[2,8,64,128]{3,2,1,0:T(8,128)S(1)} %copy-done.8, ...), custom_call_target="tpu_custom_call" | custom-call | flops 1650000000 | bytes 5914624 | tf_op jit(solution)/shard_map/pallas_call | solution.py:37
  (44 shorter events, 0.1 us)
Async XLA Ops:
  0.6 17.8 %copy-start.6 = (f32[2,8,64,128]{3,2,1,0:T(8,128)S(1)}, f32[2,8,64,128]{3,2,1,0:T(8,128)}, u32[]{:S(2)}) copy-start(f32[2,8,64,128]{3,2,1,0:T(8,128)} %v.7) | copy-start | bytes 1572868
  0.6 17.8 %copy-start.5 = (f32[2,8,64,128]{3,2,1,0:T(8,128)S(1)}, f32[2,8,64,128]{3,2,1,0:T(8,128)}, u32[]{:S(2)}) copy-start(f32[2,8,64,128]{3,2,1,0:T(8,128)} %mv.5) | copy-start | bytes 1572868
  0.7 17.8 %copy-start.1 = (f32[2,1,1,1024]{3,2,1,0:T(1,128)S(1)}, f32[2,1,1,1024]{3,2,1,0:T(1,128)}, u32[]{:S(2)}) copy-start(f32[2,1,1,1024]{3,2,1,0:T(1,128)} %m.5) | copy-start | bytes 24580
  0.7 17.8 %copy-start.7 = (f32[2,8,64,128]{3,2,1,0:T(8,128)S(1)}, f32[2,8,64,128]{3,2,1,0:T(8,128)}, u32[]{:S(2)}) copy-start(f32[2,8,64,128]{3,2,1,0:T(8,128)} %l.5) | copy-start | bytes 1572868
  0.7 17.8 %copy-start.10 = (s32[2,1,1,1024]{3,2,1,0:T(1,128)S(1)}, s32[2,1,1,1024]{3,2,1,0:T(1,128)}, u32[]{:S(2)}) copy-start(s32[2,1,1,1024]{3,2,1,0:T(1,128)} %cells.2) | copy-start | bytes 24580
  0.7 17.8 %copy-start.2 = (f32[2,8,64,128]{3,2,1,0:T(8,128)S(1)}, f32[2,8,64,128]{3,2,1,0:T(8,128)}, u32[]{:S(2)}) copy-start(f32[2,8,64,128]{3,2,1,0:T(8,128)} %f.1) | copy-start | bytes 1572868
  5.2 9.0 %collective-permute-start = (f32[6,64,128]{2,1,0:T(8,128)}, f32[6,64,128]{2,1,0:T(8,128)S(1)}, u32[]{:S(2)}, u32[]{:S(2)}) collective-permute-start(f32[6,64,128]{2,1,0:T(8,128)} %get-tuple-element.34.strips), channel_id=1, source_target_pairs={{0,1},{1,0},{2,3},{3,2},{4,5},{5,4},{6,7},{7,6},{8,9},{9,8},{10,11... | collective-permute-start | bytes 589832 | tf_op jit(solution)/shard_map/ppermute | solution.py:652
  7.4 14.0 %collective-permute-start.1 = (f32[86,8,128]{2,1,0:T(8,128)}, f32[86,8,128]{2,1,0:T(8,128)S(1)}, u32[]{:S(2)}, u32[]{:S(2)}) collective-permute-start(f32[86,8,128]{2,1,0:T(8,128)} %get-tuple-element.40), channel_id=1, source_target_pairs={{2,4},{3,5},{4,2},{5,3},{6,8},{7,9},{8,6},{9,7},{10,12},{11,13},{1... | collective-permute-start | bytes 1056776 | tf_op jit(solution)/shard_map/ppermute | solution.py:653
  12.8 8.7 %collective-permute-start.2 = (f32[86,8,128]{2,1,0:T(8,128)}, f32[86,8,128]{2,1,0:T(8,128)S(1)}, u32[]{:S(2)}, u32[]{:S(2)}) collective-permute-start(f32[86,8,128]{2,1,0:T(8,128)} %get-tuple-element.41), channel_id=1, source_target_pairs={{0,2},{1,3},{2,0},{3,1},{4,6},{5,7},{6,4},{7,5},{8,10},{9,11},{10,... | collective-permute-start | bytes 1056776 | tf_op jit(solution)/shard_map/ppermute | solution.py:654
  12.9 20.2 %collective-permute-start.7 = (f32[136,8,128]{2,1,0:T(8,128)}, f32[136,8,128]{2,1,0:T(8,128)S(1)}, u32[]{:S(2)}, u32[]{:S(2)}) collective-permute-start(f32[136,8,128]{2,1,0:T(8,128)} %get-tuple-element.47.z_own), channel_id=1, source_target_pairs={{32,0},{64,32},{96,64},{128,96},{160,128},{192,160},{224,192},{33,... | collective-permute-start | bytes 1671176 | tf_op jit(solution)/shard_map/ppermute | solution.py:655
  14.2 8.6 %copy-start.13 = (s32[2]{0:T(128)S(1)}, s32[2]{0:T(128)}, u32[]{:S(2)}) copy-start(s32[2]{0:T(128)} %counts.3) | copy-start | bytes 28
  14.2 8.6 %copy-start.3 = (f32[2,8,64,128]{3,2,1,0:T(8,128)S(1)}, f32[2,8,64,128]{3,2,1,0:T(8,128)}, u32[]{:S(2)}) copy-start(f32[2,8,64,128]{3,2,1,0:T(8,128)} %we.3) | copy-start | bytes 1572868
  14.2 8.6 %copy-start.4 = (f32[2,8,64,128]{3,2,1,0:T(8,128)S(1)}, f32[2,8,64,128]{3,2,1,0:T(8,128)}, u32[]{:S(2)}) copy-start(f32[2,8,64,128]{3,2,1,0:T(8,128)} %wn.3) | copy-start | bytes 1572868
  14.3 7.2 %collective-permute-start.3 = (f32[6,8,128]{2,1,0:T(8,128)}, f32[6,8,128]{2,1,0:T(8,128)S(1)}, u32[]{:S(2)}, u32[]{:S(2)}) collective-permute-start(f32[6,8,128]{2,1,0:T(8,128)} %get-tuple-element.42), channel_id=1, source_target_pairs={{2,5},{3,4},{4,3},{5,2},{6,9},{7,8},{8,7},{9,6},{10,13},{11,12},{1... | collective-permute-start | bytes 73736 | tf_op jit(solution)/shard_map/ppermute | solution.py:658
  18.4 3.2 %collective-permute-start.4 = (f32[6,16,128]{2,1,0:T(8,128)S(1)}, f32[6,16,128]{2,1,0:T(8,128)S(1)}, u32[]{:S(2)}, u32[]{:S(2)}) collective-permute-start(f32[6,16,128]{2,1,0:T(8,128)S(1)} %pad_maximum_fusion), channel_id=1, source_target_pairs={{0,2},{1,3},{2,0},{3,1},{4,6},{5,7},{6,4},{7,5},{8,10},{9,11},{10,... | collective-permute-start | bytes 147464 | tf_op jit(solution)/shard_map/ppermute | solution.py:659
  21.6 11.5 %collective-permute-start.8 = (f32[45,8,128]{2,1,0:T(8,128)S(1)}, f32[45,8,128]{2,1,0:T(8,128)S(1)}, u32[]{:S(2)}, u32[]{:S(2)}) collective-permute-start(f32[45,8,128]{2,1,0:T(8,128)S(1)} %fusion), channel_id=1, source_target_pairs={{32,0},{64,32},{96,64},{128,96},{160,128},{192,160},{224,192},{33,... | collective-permute-start | bytes 552968 | tf_op jit(solution)/shard_map/ppermute | solution.py:676
  28.3 17.0 %collective-permute-start.5 = (f32[2,8,64,128]{3,2,1,0:T(8,128)S(1)}, f32[2,8,64,128]{3,2,1,0:T(8,128)S(1)}, u32[]{:S(2)}, u32[]{:S(2)}) collective-permute-start(f32[2,8,64,128]{3,2,1,0:T(8,128)S(1)} %get-tuple-element.44), channel_id=1, source_target_pairs={{0,32},{64,96},{128,160},{192,224},{32,0},{96,64},{160,128},{224,1... | collective-permute-start | bytes 1572872 | tf_op jit(solution)/shard_map/ppermute | solution.py:691
  29.0 16.2 %collective-permute-start.6 = (f32[2,8,64,128]{3,2,1,0:T(8,128)S(1)}, f32[2,8,64,128]{3,2,1,0:T(8,128)S(1)}, u32[]{:S(2)}, u32[]{:S(2)}) collective-permute-start(f32[2,8,64,128]{3,2,1,0:T(8,128)S(1)} %get-tuple-element.45), channel_id=1, source_target_pairs={{32,64},{96,128},{160,192},{64,32},{128,96},{192,160},{33,65},{97,... | collective-permute-start | bytes 1572872 | tf_op jit(solution)/shard_map/ppermute | solution.py:692
  33.0 9.8 %copy-start.11 = (f32[2,1,1,1024]{3,2,1,0:T(1,128)S(1)}, f32[2,1,1,1024]{3,2,1,0:T(1,128)}, u32[]{:S(2)}) copy-start(f32[2,1,1,1024]{3,2,1,0:T(1,128)} %dep.1) | copy-start | bytes 24580
  33.0 9.8 %copy-start.12 = (f32[2,1,1,1024]{3,2,1,0:T(1,128)S(1)}, f32[2,1,1,1024]{3,2,1,0:T(1,128)}, u32[]{:S(2)}) copy-start(f32[2,1,1,1024]{3,2,1,0:T(1,128)} %ov.1) | copy-start | bytes 24580
  41.5 22.7 %collective-permute-start.9 = (f32[8,64,128]{2,1,0:T(8,128)S(1)}, f32[8,64,128]{2,1,0:T(8,128)S(1)}, u32[]{:S(2)}, u32[]{:S(2)}) collective-permute-start(f32[8,64,128]{2,1,0:T(8,128)S(1)} %get-tuple-element.49.f21), channel_id=1, source_target_pairs={{0,32},{32,64},{64,96},{96,128},{128,160},{160,192},{192,224},{1,3... | collective-permute-start | bytes 786440 | tf_op jit(solution)/shard_map/ppermute | solution.py:700
  42.8 2.4 %copy-start = (f32[136,8,128]{2,1,0:T(8,128)S(1)}, f32[136,8,128]{2,1,0:T(8,128)}, u32[]{:S(2)}) copy-start(f32[136,8,128]{2,1,0:T(8,128)} %get-tuple-element.47.z_own) | copy-start | bytes 1671172
  46.3 30.5 %all-to-all-start = ((f32[256,1,128]{2,1,0:T(1,128)}), f32[256,1,128]{2,1,0:T(1,128)S(1)}, u32[]{:S(2)}, u32[]{:S(2)}) async-start(f32[256,1,128]{2,1,0:T(1,128)} %bitcast.3), calls=%async_computation | async-start | bytes 262144 | tf_op jit(solution)/shard_map/all_to_all | solution.py:711
  76.8 1.0 %copy-start.8 = (f32[2,8,64,128]{3,2,1,0:T(8,128)S(1)}, f32[2,8,64,128]{3,2,1,0:T(8,128)}, u32[]{:S(2)}) copy-start(f32[2,8,64,128]{3,2,1,0:T(8,128)} %l.5) | copy-start | bytes 1572868
  (1 other events, 0.9 us)

commit v7 on v6

--- a/solution.py
+++ b/solution.py
@@ -98,32 +98,18 @@
 
 
 def pack_kernel(
-    cells_h, m_h, l_h, f_h, mv_h, v_h, we_h, wn_h,
+    cells_h, m_h, v_h, we_h, wn_h, l_h, f_h, mv_h,
     b_out, a_out, by_out, strip_out, z_out,
-    lh_out, g_s, cells, m, l, f, mv, v, we, wn, sems,
+    lh_out, g_s, cells, m, v, we, wn, l, f, mv, sems,
 ):
-    far = (cells_h, m_h, l_h, f_h, mv_h, v_h, we_h, wn_h)
-    near = (cells, m, l, f, mv, v, we, wn)
+    far = (cells_h, m_h, v_h, we_h, wn_h, l_h, f_h, mv_h)
+    near = (cells, m, v, we, wn, l, f, mv)
     copies = [pltpu.make_async_copy(a, b, sems.at[i]) for i, (a, b) in enumerate(zip(far, near))]
     for copy in copies:
         copy.start()
-    copies[0].wait()
-    copies[1].wait()
     core = lax.axis_index("gx") % 2
     gy = lax.axis_index("gy")
     lane = iota((CX, CY), 1)
-    for s in range(2):
-        rows, lanes = one_hots(cells[s, 0])
-        h = scatter(rows, lanes, m[s, 0])
-        if s == 0:
-            for copy in copies[2:]:
-                copy.wait()
-        lh_out[s] = l[s] + h.reshape(LEV, CX, CY)
-        g_s[s] = f[s] - mv[s] * l[s] - v[s]
-    for z in range(LEV):
-        for i in range(CX // 8):
-            z_out[z * 8 + i] = l[0, z, 8 * i : 8 * i + 8]
-            z_out[64 + z * 8 + i] = g_s[0, z, 8 * i : 8 * i + 8]
 
     def own(get):
         packed = jnp.zeros((CX, CY), F32)
@@ -133,14 +119,35 @@
         return packed
 
     half = own_half((CX, CY), gy)
-    pairs = (
-        ((v, 0), (v, 1)), ((l, 0), (g_s, 0)), ((l, 1), (g_s, 1)),
-        ((lh_out, 0), (lh_out, 1)), ((we, 0), (wn, 0)), ((we, 1), (wn, 1)),
-    )
-    for p, (one, two) in enumerate(pairs):
-        first = own(lambda z, one=one: one[0][one[1], z])
-        second = own(lambda z, two=two: two[0][two[1], z])
+
+    def pack_strips(p, one, two):
+        first = own(lambda z: one[0][one[1], z])
+        second = own(lambda z: two[0][two[1], z])
         strip_out[p] = jnp.where(half, first, swap_halves(second))
+
+    copies[0].wait()
+    copies[1].wait()
+    for s in range(2):
+        rows, lanes = one_hots(cells[s, 0])
+        lh_out[s] = scatter(rows, lanes, m[s, 0]).reshape(LEV, CX, CY)
+    copies[2].wait()
+    pack_strips(0, (v, 0), (v, 1))
+    copies[3].wait()
+    copies[4].wait()
+    pack_strips(4, (we, 0), (wn, 0))
+    pack_strips(5, (we, 1), (wn, 1))
+    for copy in copies[5:]:
+        copy.wait()
+    for s in range(2):
+        lh_out[s] += l[s]
+        g_s[s] = f[s] - mv[s] * l[s] - v[s]
+    for z in range(LEV):
+        for i in range(CX // 8):
+            z_out[z * 8 + i] = l[0, z, 8 * i : 8 * i + 8]
+            z_out[64 + z * 8 + i] = g_s[0, z, 8 * i : 8 * i + 8]
+    pack_strips(1, (l, 0), (g_s, 0))
+    pack_strips(2, (l, 1), (g_s, 1))
+    pack_strips(3, (lh_out, 0), (lh_out, 1))
     for i in range(CX // 8):
         z_out[128 + i] = strip_out[1, 8 * i : 8 * i + 8]
 
@@ -641,7 +648,7 @@
     b_send, a_send, by_send, strips, z_send = call(
         pack_kernel,
         [(NBLOCKS, 8, CY)] * 2 + [(6, 8, CY), (6, CX, CY), (136, 8, CY)],
-        [cells4, m4, l4, f4, mv4, v4, we4, wn4],
+        [cells4, m4, v4, we4, wn4, l4, f4, mv4],
         [fields, fields, pltpu.VMEM(obs, jnp.int32), pltpu.VMEM(obs, F32)]
         + [fields] * 6
         + [pltpu.SemaphoreType.DMA((8,))],

time: 80.1 us -> 79.5 us (level); the launches traced: 79.4 us -> 80.1 us
  starting transfers between devices: 35.2 us -> 39.2 us
  Pallas kernels: 24.1 us -> 20.6 us
    pallas_call x7, Pallas kernels: 24.1 us -> 20.6 us  [call(): pl.pallas_call(body, out_shape=shapes, in_specs=in_specs, out_specs=[FAR...]
    ppermute x1, starting transfers between devices: 1.36 us -> 3.85 us  [shards(): z_f2 = lax.ppermute(f21, 'tm', up)]
    all_to_all x1, starting transfers between devices: 17.8 us -> 18.7 us  [shards(): sums = lax.all_to_all(send, ('tm', 'gx', 'gy'), 0, 0, tiled=True)]
  transfers between devices with their start and end apart: 11 -> 11, of which waited for: 3 -> 3; matrix products, arithmetic and copies ran while one was open for 0% -> 0% of each run, Pallas kernels for 23% -> 18%
where the time goes in v7:
time: 79.5 us; the launch traced here: 80.1 us
  starting transfers between devices  39.2 us (49%)
  Pallas kernels  20.6 us (26%)
  waiting for transfers between devices  17.3 us (22%)
  local copies, waits for them, and re-layouts  2.06 us (3%)
  between operations  1.05 us (1%)
    pallas_call x7, Pallas kernels, call(): pl.pallas_call(body, out_shape=shapes, in_specs=in_specs, out_specs=[FAR...  20.6 us
    all_to_all x1, starting transfers between devices, shards(): sums = lax.all_to_all(send, ('tm', 'gx', 'gy'), 0, 0, tiled=True)  18.7 us
    all_to_all x1, waiting for transfers between devices, shards(): sums = lax.all_to_all(send, ('tm', 'gx', 'gy'), 0, 0, tiled=True)  12.7 us
    ppermute x1, starting transfers between devices, shards(): bg = lax.ppermute(b_send, axes, plane(pair_b, False))  5.35 us
    ppermute x1, starting transfers between devices, shards(): by = lax.ppermute(by_send, axes, plane(pair_b, True))  4.11 us
    ppermute x1, starting transfers between devices, shards(): z_f2 = lax.ppermute(f21, 'tm', up)  3.85 us
    ppermute x1, waiting for transfers between devices, shards(): zh = lax.ppermute(z_edges, 'tm', down)  3.45 us
    ppermute x1, starting transfers between devices, shards(): got = lax.ppermute(strips, axes, plane(lambda i: i, True))  2.21 us
  transfers between devices with their start and end apart: 11, of which 3 were waited for; matrix products, arithmetic and copies ran while one was open for 0% of the time, Pallas kernels for 18%

profile of v7, /device:TPU:1, one launch (start us, length us, event | category | flops | bytes accessed | tf_op | source)
XLA Modules:
  0.0 80.1 jit_solution(4389630311703837893)
XLA Ops:
  0.7 4.3 %shard_map.154 = (f32[86,8,128]{2,1,0:T(8,128)}, f32[86,8,128]{2,1,0:T(8,128)}, f32[6,8,128]{2,1,0:T(8,128)}, f32[6,64,128]{2,1,0:T(8,128)}, f32[136,8,128]{2,1,0:T(8,128)}) custom-call(s32[2,1,1,1024]{3,2,1,0:T(1,128)} %cells.2, f32[2,1,1,1024]{3,2,1,0:T(1,128)} %m.5, f32[2,8,64,128]{3,2,1,0:T(8,128)} %v.7, f32[2,8,64,128]{3,2,1,0:T(8,128)} %we.3, ...), custom_call_target="tpu_custom_call" | custom-call | flops 2750000128 | bytes 4644864 | tf_op jit(solution)/shard_map/pallas_call | solution.py:37
  5.0 2.2 %collective-permute-start = (f32[6,64,128]{2,1,0:T(8,128)}, f32[6,64,128]{2,1,0:T(8,128)S(1)}, u32[]{:S(2)}, u32[]{:S(2)}) collective-permute-start(f32[6,64,128]{2,1,0:T(8,128)} %get-tuple-element.34.strips), channel_id=1, source_target_pairs={{0,1},{1,0},{2,3},{3,2},{4,5},{5,4},{6,7},{7,6},{8,9},{9,8},{10,11... | collective-permute-start | bytes 589832 | tf_op jit(solution)/shard_map/ppermute | solution.py:659
  7.3 5.3 %collective-permute-start.1 = (f32[86,8,128]{2,1,0:T(8,128)}, f32[86,8,128]{2,1,0:T(8,128)S(1)}, u32[]{:S(2)}, u32[]{:S(2)}) collective-permute-start(f32[86,8,128]{2,1,0:T(8,128)} %get-tuple-element.40), channel_id=1, source_target_pairs={{2,4},{3,5},{4,2},{5,3},{6,8},{7,9},{8,6},{9,7},{10,12},{11,13},{1... | collective-permute-start | bytes 1056776 | tf_op jit(solution)/shard_map/ppermute | solution.py:660
  12.6 0.1 collective-permute-start.2
  12.7 1.3 %collective-permute-start.7 = (f32[136,8,128]{2,1,0:T(8,128)}, f32[136,8,128]{2,1,0:T(8,128)S(1)}, u32[]{:S(2)}, u32[]{:S(2)}) collective-permute-start(f32[136,8,128]{2,1,0:T(8,128)} %get-tuple-element.47.z_own), channel_id=1, source_target_pairs={{32,0},{64,32},{96,64},{128,96},{160,128},{192,160},{224,192},{33,... | collective-permute-start | bytes 1671176 | tf_op jit(solution)/shard_map/ppermute | solution.py:662
  14.1 0.0 copy-start.13
  14.1 4.1 %collective-permute-start.3 = (f32[6,8,128]{2,1,0:T(8,128)}, f32[6,8,128]{2,1,0:T(8,128)S(1)}, u32[]{:S(2)}, u32[]{:S(2)}) collective-permute-start(f32[6,8,128]{2,1,0:T(8,128)} %get-tuple-element.42), channel_id=1, source_target_pairs={{2,5},{3,4},{4,3},{5,2},{6,9},{7,8},{8,7},{9,6},{10,13},{11,12},{1... | collective-permute-start | bytes 73736 | tf_op jit(solution)/shard_map/ppermute | solution.py:665
  18.2 0.1 collective-permute-start.4
  18.4 0.9 %copy-done.9 = f32[6,64,128]{2,1,0:T(8,128)S(1)} copy-done((f32[6,64,128]{2,1,0:T(8,128)S(1)}, f32[6,64,128]{2,1,0:T(8,128)}, u32[]{:S(2)}) %copy-start.9) | copy-done | bytes 196632
  19.3 0.9 %shard_map.155 = (f32[2,8,64,128]{3,2,1,0:T(8,128)S(1)}, f32[8,64,128]{2,1,0:T(8,128)S(1)}, f32[6,64,128]{2,1,0:T(8,128)S(1)}) custom-call(s32[2,1,1,1024]{3,2,1,0:T(1,128)S(1)} %copy-done.10, f32[2,1,1,1024]{3,2,1,0:T(1,128)S(1)} %copy-done.1, f32[2,8,64,128]{3,2,1,0:T(8,128)S(1)} %copy-done.7, f32[2,8,64,128]{3,2,1,0:T(8,128)S(1)} %copy-done.2, ...), custom_call_target="tpu_custom_call" | custom-call | flops 1100000000 | bytes 3293184 | tf_op jit(solution)/shard_map/pallas_call | solution.py:37
  20.2 1.1 %collective-permute-done.1.bg = f32[86,8,128]{2,1,0:T(8,128)S(1)} collective-permute-done((f32[86,8,128]{2,1,0:T(8,128)}, f32[86,8,128]{2,1,0:T(8,128)S(1)}, u32[]{:S(2)}, u32[]{:S(2)}) %collective-permute-start.1) | collective-permute-done | bytes 352288 | tf_op jit(solution)/shard_map/ppermute | solution.py:660
  21.4 1.3 %collective-permute-start.8 = (f32[45,8,128]{2,1,0:T(8,128)S(1)}, f32[45,8,128]{2,1,0:T(8,128)S(1)}, u32[]{:S(2)}, u32[]{:S(2)}) collective-permute-start(f32[45,8,128]{2,1,0:T(8,128)S(1)} %fusion), channel_id=1, source_target_pairs={{32,0},{64,32},{96,64},{128,96},{160,128},{192,160},{224,192},{33,... | collective-permute-start | bytes 552968 | tf_op jit(solution)/shard_map/ppermute | solution.py:683
  22.7 4.5 %shard_map.156 = (f32[3,9,80,128]{3,2,1,0:T(8,128)S(1)}, f32[2,8,64,128]{3,2,1,0:T(8,128)S(1)}, f32[2,8,64,128]{3,2,1,0:T(8,128)S(1)}, f32[2,8,64,128]{3,2,1,0:T(8,128)S(1)}) custom-call(s32[2]{0:T(128)S(1)} %copy-done.13, f32[2,8,64,128]{3,2,1,0:T(8,128)S(1)} %copy-done.6, f32[2,8,64,128]{3,2,1,0:T(8,128)S(1)} %copy-done.7, ...), custom_call_target="tpu_custom_call" | custom-call | flops 5500000256 | bytes 7258120 | tf_op jit(solution)/shard_map/pallas_call | solution.py:37
  27.3 1.3 %collective-permute-start.5 = (f32[2,8,64,128]{3,2,1,0:T(8,128)S(1)}, f32[2,8,64,128]{3,2,1,0:T(8,128)S(1)}, u32[]{:S(2)}, u32[]{:S(2)}) collective-permute-start(f32[2,8,64,128]{3,2,1,0:T(8,128)S(1)} %get-tuple-element.44), channel_id=1, source_target_pairs={{0,32},{64,96},{128,160},{192,224},{32,0},{96,64},{160,128},{224,1... | collective-permute-start | bytes 1572872 | tf_op jit(solution)/shard_map/ppermute | solution.py:698
  28.6 0.9 %collective-permute-start.6 = (f32[2,8,64,128]{3,2,1,0:T(8,128)S(1)}, f32[2,8,64,128]{3,2,1,0:T(8,128)S(1)}, u32[]{:S(2)}, u32[]{:S(2)}) collective-permute-start(f32[2,8,64,128]{3,2,1,0:T(8,128)S(1)} %get-tuple-element.45), channel_id=1, source_target_pairs={{32,64},{96,128},{160,192},{64,32},{128,96},{192,160},{33,65},{97,... | collective-permute-start | bytes 1572872 | tf_op jit(solution)/shard_map/ppermute | solution.py:699
  29.4 3.4 %collective-permute-done.8.zh = f32[45,8,128]{2,1,0:T(8,128)S(1)} collective-permute-done((f32[45,8,128]{2,1,0:T(8,128)S(1)}, f32[45,8,128]{2,1,0:T(8,128)S(1)}, u32[]{:S(2)}, u32[]{:S(2)}) %collective-permute-start.8) | collective-permute-done | bytes 184352 | tf_op jit(solution)/shard_map/ppermute | solution.py:683
  32.9 5.9 %shard_map.157 = (f32[8,64,128]{2,1,0:T(8,128)S(1)}, f32[8,64,128]{2,1,0:T(8,128)S(1)}, f32[8,64,128]{2,1,0:T(8,128)S(1)}, f32[8,64,128]{2,1,0:T(8,128)S(1)}, f3...) custom-call(s32[2]{0:T(128)S(1)} %copy-done.13, ...), custom_call_target="tpu_custom_call" | custom-call | flops 9900000256 | bytes 6959112 | tf_op jit(solution)/shard_map/pallas_call | solution.py:37
  38.8 3.9 %collective-permute-start.9 = (f32[8,64,128]{2,1,0:T(8,128)S(1)}, f32[8,64,128]{2,1,0:T(8,128)S(1)}, u32[]{:S(2)}, u32[]{:S(2)}) collective-permute-start(f32[8,64,128]{2,1,0:T(8,128)S(1)} %get-tuple-element.49.f21), channel_id=1, source_target_pairs={{0,32},{32,64},{64,96},{96,128},{128,160},{160,192},{192,224},{1,3... | collective-permute-start | bytes 786440 | tf_op jit(solution)/shard_map/ppermute | solution.py:707
  42.7 2.4 %shard_map.158 = (f32[2,1,1,1024]{3,2,1,0:T(1,128)S(1)}, f32[2,1,1,1024]{3,2,1,0:T(1,128)S(1)}, f32[2,8,64,128]{3,2,1,0:T(8,128)S(1)}) custom-call(s32[2,1,1,1024]{3,2,1,0:T(1,128)S(1)} %copy-done.10, f32[2,1,1,1024]{3,2,1,0:T(1,128)S(1)} %copy-done.1, f32[2,8,64,128]{3,2,1,0:T(8,128)S(1)} %copy-done.6, f32[2,1,1,1024]{3,2,1,0:T(1,128)S(1)} %copy-done.11, ...), custom_call_target="tpu_custom_call" | custom-call | flops 3740000000 | bytes 1884160 | tf_op jit(solution)/shard_map/pallas_call | solution.py:37
  45.1 1.1 %shard_map.159 = (f32[7,8,64,128]{3,2,1,0:T(8,128)S(1)}, f32[256,128]{1,0:T(8,128)}) custom-call(f32[2,8,64,128]{3,2,1,0:T(8,128)S(1)} %collective-permute-done.5.even, f32[2,8,64,128]{3,2,1,0:T(8,128)S(1)} %collective-permute-done.6.odd, f32[8,64,128]{2,1,0:T(8,128)S(1)} %get-tuple-element.48.rl2, f32[8,64,128]{2,1,0:T(8,128)S(1)} %get-tuple-element.49.f21, ...), custom_call_target="tpu_custom_call" | custom-call | flops 440000000 | bytes 6488064 | tf_op jit(solution)/shard_map/pallas_call | solution.py:37
  46.2 18.7 %all-to-all-start = ((f32[256,1,128]{2,1,0:T(1,128)}), f32[256,1,128]{2,1,0:T(1,128)S(1)}, u32[]{:S(2)}, u32[]{:S(2)}) async-start(f32[256,1,128]{2,1,0:T(1,128)} %bitcast.3), calls=%async_computation | async-start | bytes 262144 | tf_op jit(solution)/shard_map/all_to_all | solution.py:718
  64.9 12.7 %all-to-all-done = f32[256,1,128]{2,1,0:T(1,128)S(1)} async-done(((f32[256,1,128]{2,1,0:T(1,128)}), f32[256,1,128]{2,1,0:T(1,128)S(1)}, u32[]{:S(2)}, u32[]{:S(2)}) %all-to-all-start) | async-done | bytes 131104 | tf_op jit(solution)/shard_map/all_to_all | solution.py:718
  77.6 1.0 %copy-done.8 = f32[2,8,64,128]{3,2,1,0:T(8,128)S(1)} copy-done((f32[2,8,64,128]{3,2,1,0:T(8,128)S(1)}, f32[2,8,64,128]{3,2,1,0:T(8,128)}, u32[]{:S(2)}) %copy-start.8) | copy-done | bytes 524312
  78.6 1.5 %shard_map.160 = (f32[2,8,64,128]{3,2,1,0:T(8,128)}, f32[2,1,1,1024]{3,2,1,0:T(1,128)}, f32[2,8,64,128]{3,2,1,0:T(8,128)}, f32[2,8,64,128]{3,2,1,0:T(8,128)}, f3...) custom-call(f32[256,128]{1,0:T(8,128)S(1)} %bitcast.12, f32[2,8,64,128]{3,2,1,0:T(8,128)S(1)} %copy-done.8, ...), custom_call_target="tpu_custom_call" | custom-call | flops 1650000000 | bytes 5914624 | tf_op jit(solution)/shard_map/pallas_call | solution.py:37
  (44 shorter events, 0.1 us)
Async XLA Ops:
  0.6 17.7 %copy-start.6 = (f32[2,8,64,128]{3,2,1,0:T(8,128)S(1)}, f32[2,8,64,128]{3,2,1,0:T(8,128)}, u32[]{:S(2)}) copy-start(f32[2,8,64,128]{3,2,1,0:T(8,128)} %v.7) | copy-start | bytes 1572868
  0.6 17.7 %copy-start.5 = (f32[2,8,64,128]{3,2,1,0:T(8,128)S(1)}, f32[2,8,64,128]{3,2,1,0:T(8,128)}, u32[]{:S(2)}) copy-start(f32[2,8,64,128]{3,2,1,0:T(8,128)} %mv.5) | copy-start | bytes 1572868
  0.7 17.7 %copy-start.1 = (f32[2,1,1,1024]{3,2,1,0:T(1,128)S(1)}, f32[2,1,1,1024]{3,2,1,0:T(1,128)}, u32[]{:S(2)}) copy-start(f32[2,1,1,1024]{3,2,1,0:T(1,128)} %m.5) | copy-start | bytes 24580
  0.7 17.7 %copy-start.7 = (f32[2,8,64,128]{3,2,1,0:T(8,128)S(1)}, f32[2,8,64,128]{3,2,1,0:T(8,128)}, u32[]{:S(2)}) copy-start(f32[2,8,64,128]{3,2,1,0:T(8,128)} %l.5) | copy-start | bytes 1572868
  0.7 17.7 %copy-start.10 = (s32[2,1,1,1024]{3,2,1,0:T(1,128)S(1)}, s32[2,1,1,1024]{3,2,1,0:T(1,128)}, u32[]{:S(2)}) copy-start(s32[2,1,1,1024]{3,2,1,0:T(1,128)} %cells.2) | copy-start | bytes 24580
  0.7 17.7 %copy-start.2 = (f32[2,8,64,128]{3,2,1,0:T(8,128)S(1)}, f32[2,8,64,128]{3,2,1,0:T(8,128)}, u32[]{:S(2)}) copy-start(f32[2,8,64,128]{3,2,1,0:T(8,128)} %f.1) | copy-start | bytes 1572868
  5.0 9.0 %collective-permute-start = (f32[6,64,128]{2,1,0:T(8,128)}, f32[6,64,128]{2,1,0:T(8,128)S(1)}, u32[]{:S(2)}, u32[]{:S(2)}) collective-permute-start(f32[6,64,128]{2,1,0:T(8,128)} %get-tuple-element.34.strips), channel_id=1, source_target_pairs={{0,1},{1,0},{2,3},{3,2},{4,5},{5,4},{6,7},{7,6},{8,9},{9,8},{10,11... | collective-permute-start | bytes 589832 | tf_op jit(solution)/shard_map/ppermute | solution.py:659
  7.3 14.0 %collective-permute-start.1 = (f32[86,8,128]{2,1,0:T(8,128)}, f32[86,8,128]{2,1,0:T(8,128)S(1)}, u32[]{:S(2)}, u32[]{:S(2)}) collective-permute-start(f32[86,8,128]{2,1,0:T(8,128)} %get-tuple-element.40), channel_id=1, source_target_pairs={{2,4},{3,5},{4,2},{5,3},{6,8},{7,9},{8,6},{9,7},{10,12},{11,13},{1... | collective-permute-start | bytes 1056776 | tf_op jit(solution)/shard_map/ppermute | solution.py:660
  12.6 8.7 %collective-permute-start.2 = (f32[86,8,128]{2,1,0:T(8,128)}, f32[86,8,128]{2,1,0:T(8,128)S(1)}, u32[]{:S(2)}, u32[]{:S(2)}) collective-permute-start(f32[86,8,128]{2,1,0:T(8,128)} %get-tuple-element.41), channel_id=1, source_target_pairs={{0,2},{1,3},{2,0},{3,1},{4,6},{5,7},{6,4},{7,5},{8,10},{9,11},{10,... | collective-permute-start | bytes 1056776 | tf_op jit(solution)/shard_map/ppermute | solution.py:661
  12.7 20.2 %collective-permute-start.7 = (f32[136,8,128]{2,1,0:T(8,128)}, f32[136,8,128]{2,1,0:T(8,128)S(1)}, u32[]{:S(2)}, u32[]{:S(2)}) collective-permute-start(f32[136,8,128]{2,1,0:T(8,128)} %get-tuple-element.47.z_own), channel_id=1, source_target_pairs={{32,0},{64,32},{96,64},{128,96},{160,128},{192,160},{224,192},{33,... | collective-permute-start | bytes 1671176 | tf_op jit(solution)/shard_map/ppermute | solution.py:662
  14.1 8.6 %copy-start.13 = (s32[2]{0:T(128)S(1)}, s32[2]{0:T(128)}, u32[]{:S(2)}) copy-start(s32[2]{0:T(128)} %counts.3) | copy-start | bytes 28
  14.1 8.6 %copy-start.3 = (f32[2,8,64,128]{3,2,1,0:T(8,128)S(1)}, f32[2,8,64,128]{3,2,1,0:T(8,128)}, u32[]{:S(2)}) copy-start(f32[2,8,64,128]{3,2,1,0:T(8,128)} %we.3) | copy-start | bytes 1572868
  14.1 8.6 %copy-start.4 = (f32[2,8,64,128]{3,2,1,0:T(8,128)S(1)}, f32[2,8,64,128]{3,2,1,0:T(8,128)}, u32[]{:S(2)}) copy-start(f32[2,8,64,128]{3,2,1,0:T(8,128)} %wn.3) | copy-start | bytes 1572868
  14.1 7.2 %collective-permute-start.3 = (f32[6,8,128]{2,1,0:T(8,128)}, f32[6,8,128]{2,1,0:T(8,128)S(1)}, u32[]{:S(2)}, u32[]{:S(2)}) collective-permute-start(f32[6,8,128]{2,1,0:T(8,128)} %get-tuple-element.42), channel_id=1, source_target_pairs={{2,5},{3,4},{4,3},{5,2},{6,9},{7,8},{8,7},{9,6},{10,13},{11,12},{1... | collective-permute-start | bytes 73736 | tf_op jit(solution)/shard_map/ppermute | solution.py:665
  18.2 3.1 %collective-permute-start.4 = (f32[6,16,128]{2,1,0:T(8,128)S(1)}, f32[6,16,128]{2,1,0:T(8,128)S(1)}, u32[]{:S(2)}, u32[]{:S(2)}) collective-permute-start(f32[6,16,128]{2,1,0:T(8,128)S(1)} %pad_maximum_fusion), channel_id=1, source_target_pairs={{0,2},{1,3},{2,0},{3,1},{4,6},{5,7},{6,4},{7,5},{8,10},{9,11},{10,... | collective-permute-start | bytes 147464 | tf_op jit(solution)/shard_map/ppermute | solution.py:666
  21.4 11.5 %collective-permute-start.8 = (f32[45,8,128]{2,1,0:T(8,128)S(1)}, f32[45,8,128]{2,1,0:T(8,128)S(1)}, u32[]{:S(2)}, u32[]{:S(2)}) collective-permute-start(f32[45,8,128]{2,1,0:T(8,128)S(1)} %fusion), channel_id=1, source_target_pairs={{32,0},{64,32},{96,64},{128,96},{160,128},{192,160},{224,192},{33,... | collective-permute-start | bytes 552968 | tf_op jit(solution)/shard_map/ppermute | solution.py:683
  27.3 17.8 %collective-permute-start.5 = (f32[2,8,64,128]{3,2,1,0:T(8,128)S(1)}, f32[2,8,64,128]{3,2,1,0:T(8,128)S(1)}, u32[]{:S(2)}, u32[]{:S(2)}) collective-permute-start(f32[2,8,64,128]{3,2,1,0:T(8,128)S(1)} %get-tuple-element.44), channel_id=1, source_target_pairs={{0,32},{64,96},{128,160},{192,224},{32,0},{96,64},{160,128},{224,1... | collective-permute-start | bytes 1572872 | tf_op jit(solution)/shard_map/ppermute | solution.py:698
  28.6 16.5 %collective-permute-start.6 = (f32[2,8,64,128]{3,2,1,0:T(8,128)S(1)}, f32[2,8,64,128]{3,2,1,0:T(8,128)S(1)}, u32[]{:S(2)}, u32[]{:S(2)}) collective-permute-start(f32[2,8,64,128]{3,2,1,0:T(8,128)S(1)} %get-tuple-element.45), channel_id=1, source_target_pairs={{32,64},{96,128},{160,192},{64,32},{128,96},{192,160},{33,65},{97,... | collective-permute-start | bytes 1572872 | tf_op jit(solution)/shard_map/ppermute | solution.py:699
  32.9 9.8 %copy-start.11 = (f32[2,1,1,1024]{3,2,1,0:T(1,128)S(1)}, f32[2,1,1,1024]{3,2,1,0:T(1,128)}, u32[]{:S(2)}) copy-start(f32[2,1,1,1024]{3,2,1,0:T(1,128)} %dep.1) | copy-start | bytes 24580
  32.9 9.8 %copy-start.12 = (f32[2,1,1,1024]{3,2,1,0:T(1,128)S(1)}, f32[2,1,1,1024]{3,2,1,0:T(1,128)}, u32[]{:S(2)}) copy-start(f32[2,1,1,1024]{3,2,1,0:T(1,128)} %ov.1) | copy-start | bytes 24580
  38.8 26.1 %collective-permute-start.9 = (f32[8,64,128]{2,1,0:T(8,128)S(1)}, f32[8,64,128]{2,1,0:T(8,128)S(1)}, u32[]{:S(2)}, u32[]{:S(2)}) collective-permute-start(f32[8,64,128]{2,1,0:T(8,128)S(1)} %get-tuple-element.49.f21), channel_id=1, source_target_pairs={{0,32},{32,64},{64,96},{96,128},{128,160},{160,192},{192,224},{1,3... | collective-permute-start | bytes 786440 | tf_op jit(solution)/shard_map/ppermute | solution.py:707
  42.7 2.4 %copy-start = (f32[136,8,128]{2,1,0:T(8,128)S(1)}, f32[136,8,128]{2,1,0:T(8,128)}, u32[]{:S(2)}) copy-start(f32[136,8,128]{2,1,0:T(8,128)} %get-tuple-element.47.z_own) | copy-start | bytes 1671172
  46.2 31.4 %all-to-all-start = ((f32[256,1,128]{2,1,0:T(1,128)}), f32[256,1,128]{2,1,0:T(1,128)S(1)}, u32[]{:S(2)}, u32[]{:S(2)}) async-start(f32[256,1,128]{2,1,0:T(1,128)} %bitcast.3), calls=%async_computation | async-start | bytes 262144 | tf_op jit(solution)/shard_map/all_to_all | solution.py:718
  77.6 1.0 %copy-start.8 = (f32[2,8,64,128]{3,2,1,0:T(8,128)S(1)}, f32[2,8,64,128]{3,2,1,0:T(8,128)}, u32[]{:S(2)}) copy-start(f32[2,8,64,128]{3,2,1,0:T(8,128)} %l.5) | copy-start | bytes 1572868
  (1 other events, 0.9 us)

commit v8 on v7

--- a/solution.py
+++ b/solution.py
@@ -661,14 +661,14 @@
     ag = lax.ppermute(a_send, axes, plane(lambda i: i ^ 1, False))
     zt = lax.ppermute(z_send, "tm", down)
     ay_send = jnp.concatenate([got[:, :8], got[:, CX - 8 :]], 1)
-    ay_send, by_send, late_cells = lax.optimization_barrier((ay_send, by_send, cells4))
+    ay_send, by_send = lax.optimization_barrier((ay_send, by_send))
     by = lax.ppermute(by_send, axes, plane(pair_b, True))
     ay = lax.ppermute(ay_send, axes, plane(lambda i: i ^ 1, False))
 
     lh, g1, own = call(
         local_kernel,
         [(2,) + tile, tile, strips.shape],
-        [late_cells, m4, l4, f4, mv4, v4, strips],
+        [cells4, m4, l4, f4, mv4, v4, strips],
         micros=1.0,
     )
     z_edges = jnp.concatenate(

time: 79.5 us -> 78.9 us (level)
  Pallas kernels: 20.6 us -> 18.4 us
    pallas_call x7, Pallas kernels: 20.6 us -> 18.4 us  [call(): pl.pallas_call(body, out_shape=shapes, in_specs=in_specs, out_specs=[FAR...]
    ppermute x1, starting transfers between devices: 1.31 us -> 3.27 us  [shards(): even = lax.ppermute(even_send, 'tm', swap(0))]
    all_to_all x1, starting transfers between devices: 18.7 us -> 17.1 us  [shards(): sums = lax.all_to_all(send, ('tm', 'gx', 'gy'), 0, 0, tiled=True)]
    ppermute x1, waiting for transfers between devices: 3.45 us -> 1.98 us  [shards(): zh = lax.ppermute(z_edges, 'tm', down)]
    ppermute x1, waiting for transfers between devices: 0.01 us -> 1.21 us  [shards(): by = lax.ppermute(by_send, axes, plane(pair_b, True))]
    ppermute x1, starting transfers between devices: 3.85 us -> 5.04 us  [shards(): z_f2 = lax.ppermute(f21, 'tm', up)]
    ppermute x1, starting transfers between devices: 4.11 us -> 3.13 us  [shards(): by = lax.ppermute(by_send, axes, plane(pair_b, True))]
    unnamed x36 -> x38, local copies, waits for them, and re-layouts: 2.05 us -> 2.05 us
  transfers between devices with their start and end apart: 11 -> 11, of which waited for: 3 -> 4; matrix products, arithmetic and copies ran while one was open for 0% -> 0% of each run, Pallas kernels for 18% -> 16%
where the time goes in v8:
time: 78.9 us; the launch traced here: 79 us
  starting transfers between devices  39.8 us (50%)
  Pallas kernels  18.4 us (23%)
  waiting for transfers between devices  17.7 us (22%)
  local copies, waits for them, and re-layouts  2.06 us (3%)
  between operations  1.02 us (1%)
    pallas_call x7, Pallas kernels, call(): pl.pallas_call(body, out_shape=shapes, in_specs=in_specs, out_specs=[FAR...  18.4 us
    all_to_all x1, starting transfers between devices, shards(): sums = lax.all_to_all(send, ('tm', 'gx', 'gy'), 0, 0, tiled=True)  17.1 us
    all_to_all x1, waiting for transfers between devices, shards(): sums = lax.all_to_all(send, ('tm', 'gx', 'gy'), 0, 0, tiled=True)  12.7 us
    ppermute x1, starting transfers between devices, shards(): bg = lax.ppermute(b_send, axes, plane(pair_b, False))  5.35 us
    ppermute x1, starting transfers between devices, shards(): z_f2 = lax.ppermute(f21, 'tm', up)  5.04 us
    ppermute x1, starting transfers between devices, shards(): even = lax.ppermute(even_send, 'tm', swap(0))  3.27 us
    ppermute x1, starting transfers between devices, shards(): by = lax.ppermute(by_send, axes, plane(pair_b, True))  3.13 us
    ppermute x1, starting transfers between devices, shards(): got = lax.ppermute(strips, axes, plane(lambda i: i, True))  2.21 us
  transfers between devices with their start and end apart: 11, of which 4 were waited for; matrix products, arithmetic and copies ran while one was open for 0% of the time, Pallas kernels for 16%

profile of v8, /device:TPU:1, one launch (start us, length us, event | category | flops | bytes accessed | tf_op | source)
XLA Modules:
  0.0 79.0 jit_solution(3001445517237910508)
XLA Ops:
  0.7 4.3 %shard_map.154 = (f32[86,8,128]{2,1,0:T(8,128)}, f32[86,8,128]{2,1,0:T(8,128)}, f32[6,8,128]{2,1,0:T(8,128)}, f32[6,64,128]{2,1,0:T(8,128)}, f32[136,8,128]{2,1,0:T(8,128)}) custom-call(s32[2,1,1,1024]{3,2,1,0:T(1,128)} %cells.3, f32[2,1,1,1024]{3,2,1,0:T(1,128)} %m.5, f32[2,8,64,128]{3,2,1,0:T(8,128)} %v.7, f32[2,8,64,128]{3,2,1,0:T(8,128)} %we.3, ...), custom_call_target="tpu_custom_call" | custom-call | flops 2750000128 | bytes 4644864 | tf_op jit(solution)/shard_map/pallas_call | solution.py:37
  5.0 2.2 %collective-permute-start = (f32[6,64,128]{2,1,0:T(8,128)}, f32[6,64,128]{2,1,0:T(8,128)S(1)}, u32[]{:S(2)}, u32[]{:S(2)}) collective-permute-start(f32[6,64,128]{2,1,0:T(8,128)} %get-tuple-element.33.strips), channel_id=1, source_target_pairs={{0,1},{1,0},{2,3},{3,2},{4,5},{5,4},{6,7},{7,6},{8,9},{9,8},{10,11... | collective-permute-start | bytes 589832 | tf_op jit(solution)/shard_map/ppermute | solution.py:659
  7.3 5.3 %collective-permute-start.1 = (f32[86,8,128]{2,1,0:T(8,128)}, f32[86,8,128]{2,1,0:T(8,128)S(1)}, u32[]{:S(2)}, u32[]{:S(2)}) collective-permute-start(f32[86,8,128]{2,1,0:T(8,128)} %get-tuple-element.37), channel_id=1, source_target_pairs={{2,4},{3,5},{4,2},{5,3},{6,8},{7,9},{8,6},{9,7},{10,12},{11,13},{1... | collective-permute-start | bytes 1056776 | tf_op jit(solution)/shard_map/ppermute | solution.py:660
  12.6 0.1 collective-permute-start.2
  12.7 1.4 %collective-permute-start.7 = (f32[136,8,128]{2,1,0:T(8,128)}, f32[136,8,128]{2,1,0:T(8,128)S(1)}, u32[]{:S(2)}, u32[]{:S(2)}) collective-permute-start(f32[136,8,128]{2,1,0:T(8,128)} %get-tuple-element.45.z_own), channel_id=1, source_target_pairs={{32,0},{64,32},{96,64},{128,96},{160,128},{192,160},{224,192},{33,... | collective-permute-start | bytes 1671176 | tf_op jit(solution)/shard_map/ppermute | solution.py:662
  14.2 0.9 %copy-done.9 = f32[6,64,128]{2,1,0:T(8,128)S(1)} copy-done((f32[6,64,128]{2,1,0:T(8,128)S(1)}, f32[6,64,128]{2,1,0:T(8,128)}, u32[]{:S(2)}) %copy-start.9) | copy-done | bytes 196632
  15.2 0.9 %shard_map.155 = (f32[2,8,64,128]{3,2,1,0:T(8,128)S(1)}, f32[8,64,128]{2,1,0:T(8,128)S(1)}, f32[6,64,128]{2,1,0:T(8,128)S(1)}) custom-call(s32[2,1,1,1024]{3,2,1,0:T(1,128)S(1)} %copy-done.10, f32[2,1,1,1024]{3,2,1,0:T(1,128)S(1)} %copy-done.1, f32[2,8,64,128]{3,2,1,0:T(8,128)S(1)} %copy-done.7, f32[2,8,64,128]{3,2,1,0:T(8,128)S(1)} %copy-done.2, ...), custom_call_target="tpu_custom_call" | custom-call | flops 1100000000 | bytes 3293184 | tf_op jit(solution)/shard_map/pallas_call | solution.py:37
  16.1 3.1 %collective-permute-start.3 = (f32[6,8,128]{2,1,0:T(8,128)S(1)}, f32[6,8,128]{2,1,0:T(8,128)S(1)}, u32[]{:S(2)}, u32[]{:S(2)}) collective-permute-start(f32[6,8,128]{2,1,0:T(8,128)S(1)} %copy-done.14), channel_id=1, source_target_pairs={{2,5},{3,4},{4,3},{5,2},{6,9},{7,8},{8,7},{9,6},{10,13},{11,12},{1... | collective-permute-start | bytes 73736 | tf_op jit(solution)/shard_map/ppermute | solution.py:665
  19.2 0.1 collective-permute-start.4
  19.3 1.9 %collective-permute-done.1.bg = f32[86,8,128]{2,1,0:T(8,128)S(1)} collective-permute-done((f32[86,8,128]{2,1,0:T(8,128)}, f32[86,8,128]{2,1,0:T(8,128)S(1)}, u32[]{:S(2)}, u32[]{:S(2)}) %collective-permute-start.1) | collective-permute-done | bytes 352288 | tf_op jit(solution)/shard_map/ppermute | solution.py:660
  21.2 1.2 %collective-permute-done.3.by = f32[6,8,128]{2,1,0:T(8,128)S(1)} collective-permute-done((f32[6,8,128]{2,1,0:T(8,128)S(1)}, f32[6,8,128]{2,1,0:T(8,128)S(1)}, u32[]{:S(2)}, u32[]{:S(2)}) %collective-permute-start.3) | collective-permute-done | bytes 24608 | tf_op jit(solution)/shard_map/ppermute | solution.py:665
  22.4 1.3 %collective-permute-start.8 = (f32[45,8,128]{2,1,0:T(8,128)S(1)}, f32[45,8,128]{2,1,0:T(8,128)S(1)}, u32[]{:S(2)}, u32[]{:S(2)}) collective-permute-start(f32[45,8,128]{2,1,0:T(8,128)S(1)} %fusion), channel_id=1, source_target_pairs={{32,0},{64,32},{96,64},{128,96},{160,128},{192,160},{224,192},{33,... | collective-permute-start | bytes 552968 | tf_op jit(solution)/shard_map/ppermute | solution.py:683
  23.8 3.1 %shard_map.156 = (f32[3,9,80,128]{3,2,1,0:T(8,128)S(1)}, f32[2,8,64,128]{3,2,1,0:T(8,128)S(1)}, f32[2,8,64,128]{3,2,1,0:T(8,128)S(1)}, f32[2,8,64,128]{3,2,1,0:T(8,128)S(1)}) custom-call(s32[2]{0:T(128)S(1)} %copy-done.13, f32[2,8,64,128]{3,2,1,0:T(8,128)S(1)} %copy-done.6, f32[2,8,64,128]{3,2,1,0:T(8,128)S(1)} %copy-done.7, ...), custom_call_target="tpu_custom_call" | custom-call | flops 5500000256 | bytes 7258120 | tf_op jit(solution)/shard_map/pallas_call | solution.py:37
  26.9 3.3 %collective-permute-start.5 = (f32[2,8,64,128]{3,2,1,0:T(8,128)S(1)}, f32[2,8,64,128]{3,2,1,0:T(8,128)S(1)}, u32[]{:S(2)}, u32[]{:S(2)}) collective-permute-start(f32[2,8,64,128]{3,2,1,0:T(8,128)S(1)} %get-tuple-element.42), channel_id=1, source_target_pairs={{0,32},{64,96},{128,160},{192,224},{32,0},{96,64},{160,128},{224,1... | collective-permute-start | bytes 1572872 | tf_op jit(solution)/shard_map/ppermute | solution.py:698
  30.2 0.9 %collective-permute-start.6 = (f32[2,8,64,128]{3,2,1,0:T(8,128)S(1)}, f32[2,8,64,128]{3,2,1,0:T(8,128)S(1)}, u32[]{:S(2)}, u32[]{:S(2)}) collective-permute-start(f32[2,8,64,128]{3,2,1,0:T(8,128)S(1)} %get-tuple-element.43), channel_id=1, source_target_pairs={{32,64},{96,128},{160,192},{64,32},{128,96},{192,160},{33,65},{97,... | collective-permute-start | bytes 1572872 | tf_op jit(solution)/shard_map/ppermute | solution.py:699
  31.1 2.0 %collective-permute-done.8.zh = f32[45,8,128]{2,1,0:T(8,128)S(1)} collective-permute-done((f32[45,8,128]{2,1,0:T(8,128)S(1)}, f32[45,8,128]{2,1,0:T(8,128)S(1)}, u32[]{:S(2)}, u32[]{:S(2)}) %collective-permute-start.8) | collective-permute-done | bytes 184352 | tf_op jit(solution)/shard_map/ppermute | solution.py:683
  33.1 5.1 %shard_map.157 = (f32[8,64,128]{2,1,0:T(8,128)S(1)}, f32[8,64,128]{2,1,0:T(8,128)S(1)}, f32[8,64,128]{2,1,0:T(8,128)S(1)}, f32[8,64,128]{2,1,0:T(8,128)S(1)}, f3...) custom-call(s32[2]{0:T(128)S(1)} %copy-done.13, ...), custom_call_target="tpu_custom_call" | custom-call | flops 9900000256 | bytes 6959112 | tf_op jit(solution)/shard_map/pallas_call | solution.py:37
  38.1 5.0 %collective-permute-start.9 = (f32[8,64,128]{2,1,0:T(8,128)S(1)}, f32[8,64,128]{2,1,0:T(8,128)S(1)}, u32[]{:S(2)}, u32[]{:S(2)}) collective-permute-start(f32[8,64,128]{2,1,0:T(8,128)S(1)} %get-tuple-element.47.f21), channel_id=1, source_target_pairs={{0,32},{32,64},{64,96},{96,128},{128,160},{160,192},{192,224},{1,3... | collective-permute-start | bytes 786440 | tf_op jit(solution)/shard_map/ppermute | solution.py:707
  43.2 2.4 %shard_map.158 = (f32[2,1,1,1024]{3,2,1,0:T(1,128)S(1)}, f32[2,1,1,1024]{3,2,1,0:T(1,128)S(1)}, f32[2,8,64,128]{3,2,1,0:T(8,128)S(1)}) custom-call(s32[2,1,1,1024]{3,2,1,0:T(1,128)S(1)} %copy-done.10, f32[2,1,1,1024]{3,2,1,0:T(1,128)S(1)} %copy-done.1, f32[2,8,64,128]{3,2,1,0:T(8,128)S(1)} %copy-done.6, f32[2,1,1,1024]{3,2,1,0:T(1,128)S(1)} %copy-done.11, ...), custom_call_target="tpu_custom_call" | custom-call | flops 3740000000 | bytes 1884160 | tf_op jit(solution)/shard_map/pallas_call | solution.py:37
  45.6 1.1 %shard_map.159 = (f32[7,8,64,128]{3,2,1,0:T(8,128)S(1)}, f32[256,128]{1,0:T(8,128)}) custom-call(f32[2,8,64,128]{3,2,1,0:T(8,128)S(1)} %collective-permute-done.5.even, f32[2,8,64,128]{3,2,1,0:T(8,128)S(1)} %collective-permute-done.6.odd, f32[8,64,128]{2,1,0:T(8,128)S(1)} %get-tuple-element.46.rl2, f32[8,64,128]{2,1,0:T(8,128)S(1)} %get-tuple-element.47.f21, ...), custom_call_target="tpu_custom_call" | custom-call | flops 440000000 | bytes 6488064 | tf_op jit(solution)/shard_map/pallas_call | solution.py:37
  46.7 17.1 %all-to-all-start = ((f32[256,1,128]{2,1,0:T(1,128)}), f32[256,1,128]{2,1,0:T(1,128)S(1)}, u32[]{:S(2)}, u32[]{:S(2)}) async-start(f32[256,1,128]{2,1,0:T(1,128)} %bitcast.3), calls=%async_computation | async-start | bytes 262144 | tf_op jit(solution)/shard_map/all_to_all | solution.py:718
  63.8 12.7 %all-to-all-done = f32[256,1,128]{2,1,0:T(1,128)S(1)} async-done(((f32[256,1,128]{2,1,0:T(1,128)}), f32[256,1,128]{2,1,0:T(1,128)S(1)}, u32[]{:S(2)}, u32[]{:S(2)}) %all-to-all-start) | async-done | bytes 131104 | tf_op jit(solution)/shard_map/all_to_all | solution.py:718
  76.5 1.0 %copy-done.8 = f32[2,8,64,128]{3,2,1,0:T(8,128)S(1)} copy-done((f32[2,8,64,128]{3,2,1,0:T(8,128)S(1)}, f32[2,8,64,128]{3,2,1,0:T(8,128)}, u32[]{:S(2)}) %copy-start.8) | copy-done | bytes 524312
  77.5 1.5 %shard_map.160 = (f32[2,8,64,128]{3,2,1,0:T(8,128)}, f32[2,1,1,1024]{3,2,1,0:T(1,128)}, f32[2,8,64,128]{3,2,1,0:T(8,128)}, f32[2,8,64,128]{3,2,1,0:T(8,128)}, f3...) custom-call(f32[256,128]{1,0:T(8,128)S(1)} %bitcast.12, f32[2,8,64,128]{3,2,1,0:T(8,128)S(1)} %copy-done.8, ...), custom_call_target="tpu_custom_call" | custom-call | flops 1650000000 | bytes 5914624 | tf_op jit(solution)/shard_map/pallas_call | solution.py:37
  (46 shorter events, 0.1 us)
Async XLA Ops:
  0.6 13.5 %copy-start.6 = (f32[2,8,64,128]{3,2,1,0:T(8,128)S(1)}, f32[2,8,64,128]{3,2,1,0:T(8,128)}, u32[]{:S(2)}) copy-start(f32[2,8,64,128]{3,2,1,0:T(8,128)} %v.7) | copy-start | bytes 1572868
  0.6 13.5 %copy-start.5 = (f32[2,8,64,128]{3,2,1,0:T(8,128)S(1)}, f32[2,8,64,128]{3,2,1,0:T(8,128)}, u32[]{:S(2)}) copy-start(f32[2,8,64,128]{3,2,1,0:T(8,128)} %mv.5) | copy-start | bytes 1572868
  0.7 13.5 %copy-start.1 = (f32[2,1,1,1024]{3,2,1,0:T(1,128)S(1)}, f32[2,1,1,1024]{3,2,1,0:T(1,128)}, u32[]{:S(2)}) copy-start(f32[2,1,1,1024]{3,2,1,0:T(1,128)} %m.5) | copy-start | bytes 24580
  0.7 13.5 %copy-start.7 = (f32[2,8,64,128]{3,2,1,0:T(8,128)S(1)}, f32[2,8,64,128]{3,2,1,0:T(8,128)}, u32[]{:S(2)}) copy-start(f32[2,8,64,128]{3,2,1,0:T(8,128)} %l.5) | copy-start | bytes 1572868
  0.7 13.5 %copy-start.10 = (s32[2,1,1,1024]{3,2,1,0:T(1,128)S(1)}, s32[2,1,1,1024]{3,2,1,0:T(1,128)}, u32[]{:S(2)}) copy-start(s32[2,1,1,1024]{3,2,1,0:T(1,128)} %cells.3) | copy-start | bytes 24580
  0.7 13.5 %copy-start.2 = (f32[2,8,64,128]{3,2,1,0:T(8,128)S(1)}, f32[2,8,64,128]{3,2,1,0:T(8,128)}, u32[]{:S(2)}) copy-start(f32[2,8,64,128]{3,2,1,0:T(8,128)} %f.1) | copy-start | bytes 1572868
  5.0 11.0 %collective-permute-start = (f32[6,64,128]{2,1,0:T(8,128)}, f32[6,64,128]{2,1,0:T(8,128)S(1)}, u32[]{:S(2)}, u32[]{:S(2)}) collective-permute-start(f32[6,64,128]{2,1,0:T(8,128)} %get-tuple-element.33.strips), channel_id=1, source_target_pairs={{0,1},{1,0},{2,3},{3,2},{4,5},{5,4},{6,7},{7,6},{8,9},{9,8},{10,11... | collective-permute-start | bytes 589832 | tf_op jit(solution)/shard_map/ppermute | solution.py:659
  7.3 13.9 %collective-permute-start.1 = (f32[86,8,128]{2,1,0:T(8,128)}, f32[86,8,128]{2,1,0:T(8,128)S(1)}, u32[]{:S(2)}, u32[]{:S(2)}) collective-permute-start(f32[86,8,128]{2,1,0:T(8,128)} %get-tuple-element.37), channel_id=1, source_target_pairs={{2,4},{3,5},{4,2},{5,3},{6,8},{7,9},{8,6},{9,7},{10,12},{11,13},{1... | collective-permute-start | bytes 1056776 | tf_op jit(solution)/shard_map/ppermute | solution.py:660
  12.6 8.6 %collective-permute-start.2 = (f32[86,8,128]{2,1,0:T(8,128)}, f32[86,8,128]{2,1,0:T(8,128)S(1)}, u32[]{:S(2)}, u32[]{:S(2)}) collective-permute-start(f32[86,8,128]{2,1,0:T(8,128)} %get-tuple-element.38), channel_id=1, source_target_pairs={{0,2},{1,3},{2,0},{3,1},{4,6},{5,7},{6,4},{7,5},{8,10},{9,11},{10,... | collective-permute-start | bytes 1056776 | tf_op jit(solution)/shard_map/ppermute | solution.py:661
  12.7 11.0 %copy-start.3 = (f32[2,8,64,128]{3,2,1,0:T(8,128)S(1)}, f32[2,8,64,128]{3,2,1,0:T(8,128)}, u32[]{:S(2)}) copy-start(f32[2,8,64,128]{3,2,1,0:T(8,128)} %we.3) | copy-start | bytes 1572868
  12.7 11.0 %copy-start.4 = (f32[2,8,64,128]{3,2,1,0:T(8,128)S(1)}, f32[2,8,64,128]{3,2,1,0:T(8,128)}, u32[]{:S(2)}) copy-start(f32[2,8,64,128]{3,2,1,0:T(8,128)} %wn.3) | copy-start | bytes 1572868
  12.7 20.3 %collective-permute-start.7 = (f32[136,8,128]{2,1,0:T(8,128)}, f32[136,8,128]{2,1,0:T(8,128)S(1)}, u32[]{:S(2)}, u32[]{:S(2)}) collective-permute-start(f32[136,8,128]{2,1,0:T(8,128)} %get-tuple-element.45.z_own), channel_id=1, source_target_pairs={{32,0},{64,32},{96,64},{128,96},{160,128},{192,160},{224,192},{33,... | collective-permute-start | bytes 1671176 | tf_op jit(solution)/shard_map/ppermute | solution.py:662
  15.2 8.6 %copy-start.13 = (s32[2]{0:T(128)S(1)}, s32[2]{0:T(128)}, u32[]{:S(2)}) copy-start(s32[2]{0:T(128)} %counts.3) | copy-start | bytes 28
  16.1 6.4 %collective-permute-start.3 = (f32[6,8,128]{2,1,0:T(8,128)S(1)}, f32[6,8,128]{2,1,0:T(8,128)S(1)}, u32[]{:S(2)}, u32[]{:S(2)}) collective-permute-start(f32[6,8,128]{2,1,0:T(8,128)S(1)} %copy-done.14), channel_id=1, source_target_pairs={{2,5},{3,4},{4,3},{5,2},{6,9},{7,8},{8,7},{9,6},{10,13},{11,12},{1... | collective-permute-start | bytes 73736 | tf_op jit(solution)/shard_map/ppermute | solution.py:665
  19.2 3.2 %collective-permute-start.4 = (f32[6,16,128]{2,1,0:T(8,128)S(1)}, f32[6,16,128]{2,1,0:T(8,128)S(1)}, u32[]{:S(2)}, u32[]{:S(2)}) collective-permute-start(f32[6,16,128]{2,1,0:T(8,128)S(1)} %pad_maximum_fusion), channel_id=1, source_target_pairs={{0,2},{1,3},{2,0},{3,1},{4,6},{5,7},{6,4},{7,5},{8,10},{9,11},{10,... | collective-permute-start | bytes 147464 | tf_op jit(solution)/shard_map/ppermute | solution.py:666
  22.4 10.6 %collective-permute-start.8 = (f32[45,8,128]{2,1,0:T(8,128)S(1)}, f32[45,8,128]{2,1,0:T(8,128)S(1)}, u32[]{:S(2)}, u32[]{:S(2)}) collective-permute-start(f32[45,8,128]{2,1,0:T(8,128)S(1)} %fusion), channel_id=1, source_target_pairs={{32,0},{64,32},{96,64},{128,96},{160,128},{192,160},{224,192},{33,... | collective-permute-start | bytes 552968 | tf_op jit(solution)/shard_map/ppermute | solution.py:683
  26.9 18.6 %collective-permute-start.5 = (f32[2,8,64,128]{3,2,1,0:T(8,128)S(1)}, f32[2,8,64,128]{3,2,1,0:T(8,128)S(1)}, u32[]{:S(2)}, u32[]{:S(2)}) collective-permute-start(f32[2,8,64,128]{3,2,1,0:T(8,128)S(1)} %get-tuple-element.42), channel_id=1, source_target_pairs={{0,32},{64,96},{128,160},{192,224},{32,0},{96,64},{160,128},{224,1... | collective-permute-start | bytes 1572872 | tf_op jit(solution)/shard_map/ppermute | solution.py:698
  30.2 15.4 %collective-permute-start.6 = (f32[2,8,64,128]{3,2,1,0:T(8,128)S(1)}, f32[2,8,64,128]{3,2,1,0:T(8,128)S(1)}, u32[]{:S(2)}, u32[]{:S(2)}) collective-permute-start(f32[2,8,64,128]{3,2,1,0:T(8,128)S(1)} %get-tuple-element.43), channel_id=1, source_target_pairs={{32,64},{96,128},{160,192},{64,32},{128,96},{192,160},{33,65},{97,... | collective-permute-start | bytes 1572872 | tf_op jit(solution)/shard_map/ppermute | solution.py:699
  33.0 10.1 %copy-start.11 = (f32[2,1,1,1024]{3,2,1,0:T(1,128)S(1)}, f32[2,1,1,1024]{3,2,1,0:T(1,128)}, u32[]{:S(2)}) copy-start(f32[2,1,1,1024]{3,2,1,0:T(1,128)} %dep.1) | copy-start | bytes 24580
  33.1 10.1 %copy-start.12 = (f32[2,1,1,1024]{3,2,1,0:T(1,128)S(1)}, f32[2,1,1,1024]{3,2,1,0:T(1,128)}, u32[]{:S(2)}) copy-start(f32[2,1,1,1024]{3,2,1,0:T(1,128)} %ov.1) | copy-start | bytes 24580
  38.1 25.6 %collective-permute-start.9 = (f32[8,64,128]{2,1,0:T(8,128)S(1)}, f32[8,64,128]{2,1,0:T(8,128)S(1)}, u32[]{:S(2)}, u32[]{:S(2)}) collective-permute-start(f32[8,64,128]{2,1,0:T(8,128)S(1)} %get-tuple-element.47.f21), channel_id=1, source_target_pairs={{0,32},{32,64},{64,96},{96,128},{128,160},{160,192},{192,224},{1,3... | collective-permute-start | bytes 786440 | tf_op jit(solution)/shard_map/ppermute | solution.py:707
  43.2 2.4 %copy-start = (f32[136,8,128]{2,1,0:T(8,128)S(1)}, f32[136,8,128]{2,1,0:T(8,128)}, u32[]{:S(2)}) copy-start(f32[136,8,128]{2,1,0:T(8,128)} %get-tuple-element.45.z_own) | copy-start | bytes 1671172
  46.7 29.8 %all-to-all-start = ((f32[256,1,128]{2,1,0:T(1,128)}), f32[256,1,128]{2,1,0:T(1,128)S(1)}, u32[]{:S(2)}, u32[]{:S(2)}) async-start(f32[256,1,128]{2,1,0:T(1,128)} %bitcast.3), calls=%async_computation | async-start | bytes 262144 | tf_op jit(solution)/shard_map/all_to_all | solution.py:718
  76.5 1.0 %copy-start.8 = (f32[2,8,64,128]{3,2,1,0:T(8,128)S(1)}, f32[2,8,64,128]{3,2,1,0:T(8,128)}, u32[]{:S(2)}) copy-start(f32[2,8,64,128]{3,2,1,0:T(8,128)} %l.5) | copy-start | bytes 1572868
  (2 other events, 1.8 us)
